TPU v7x, 32 devices: a whole 2x2x4 slice. The times are simulated.
32 devices in a mesh: ctx: 8 (over y, x, core), fsdp: 4 (over z).
Axes of the slice: x: 2, y: 2, z: 4, core: 2. Of those that a mesh axis runs over, the one named last changes fastest.
Arguments:
- acts: bfloat16 [4, 2048, 1024], P('fsdp', 'ctx'), may hold values from -6 to 6
- cotangent: bfloat16 [4, 2048, 1024], P('fsdp', 'ctx'), may hold values from -6 to 6
- pair_slots: int32 [8], replicated, may hold values from 0 to 7, as said below
- segments: int32 [4, 2048], P('fsdp'), may hold values from 0 to 2, as said below
- attn_gain: bfloat16 [2, 1024], P(None, 'fsdp'), may hold values from 0.099609375 to 1.8984375
- attn_shift: bfloat16 [2, 1024], P(None, 'fsdp'), may hold values from -3 to 3
- qkv_weight: bfloat16 [2, 1024, 3072], P(None, 'fsdp'), may hold values from -0.1875 to 0.1875
- qkv_bias: bfloat16 [2, 3072], P(None, 'fsdp'), may hold values from -2 to 2
- proj_weight: bfloat16 [2, 1024, 1024], P(None, 'fsdp'), may hold values from -3 to 3
- proj_bias: bfloat16 [2, 1024], P(None, 'fsdp'), may hold values from -2 to 2
- mlp_gain: bfloat16 [2, 1024], P(None, 'fsdp'), may hold values from 0.099609375 to 1.8984375
- mlp_shift: bfloat16 [2, 1024], P(None, 'fsdp'), may hold values from -3 to 3
- fc_weight: bfloat16 [2, 1024, 4096], P(None, 'fsdp'), may hold values from -0.1875 to 0.1875
- fc_bias: bfloat16 [2, 4096], P(None, 'fsdp'), may hold values from -2 to 2
- out_weight: bfloat16 [2, 4096, 1024], P(None, 'fsdp'), may hold values from -0.09375 to 0.09375
- out_bias: bfloat16 [2, 1024], P(None, 'fsdp'), may hold values from -2 to 2
- final_gain: bfloat16 [1024], P('fsdp'), may hold values from 0.099609375 to 1.8984375
- final_shift: bfloat16 [1024], P('fsdp'), may hold values from -3 to 3
Outputs:
- activations: bfloat16 [4, 2048, 1024], P('fsdp', 'ctx')
- input_grad: bfloat16 [4, 2048, 1024], P('fsdp', 'ctx')
- attn_gain_grad: float32 [2, 1024], P(None, 'fsdp')
- attn_shift_grad: float32 [2, 1024], P(None, 'fsdp')
- qkv_weight_grad: float32 [2, 1024, 3072], P(None, 'fsdp')
- qkv_bias_grad: float32 [2, 3072], P(None, 'fsdp')
- proj_weight_grad: float32 [2, 1024, 1024], P(None, 'fsdp')
- proj_bias_grad: float32 [2, 1024], P(None, 'fsdp')
- mlp_gain_grad: float32 [2, 1024], P(None, 'fsdp')
- mlp_shift_grad: float32 [2, 1024], P(None, 'fsdp')
- fc_weight_grad: float32 [2, 1024, 4096], P(None, 'fsdp')
- fc_bias_grad: float32 [2, 4096], P(None, 'fsdp')
- out_weight_grad: float32 [2, 4096, 1024], P(None, 'fsdp')
- out_bias_grad: float32 [2, 1024], P(None, 'fsdp')
- final_gain_grad: float32 [1024], P('fsdp')
- final_shift_grad: float32 [1024], P('fsdp')
Inputs may be any that keep to these rules, and one draw needn't show every extreme that they name: Each number once; index i of ctx holds the pieces pair_slots[i] and 15 - pair_slots[i] of its pack's sequence, each of 128 tokens, the lower piece in the first half of its rows. `segments`: three documents a pack; taken in the order of positions the numbers never fall; document 0 starts at position 0 and takes at least half of the pack.
All inputs are finite; a program needn't handle non-finite values.
Results may differ from a plain program's by a relative error of at most 0.018.
Values may be sent and summed in bfloat16 or wider, within the bound.
A program may use at most 320 MiB of HBM per device.

v0:
```python
import jax
import jax.numpy as jnp
from jax import lax
from jax.sharding import PartitionSpec as P

HEADS = 16
HEAD_DIM = 64
LAYERS = 2


EPS = 1e-05
NEG = -1e30


def layer_norm(values, gain, shift):
    center = values - jnp.mean(values, axis=-1, keepdims=True)
    spread = jnp.mean(center * center, axis=-1, keepdims=True)
    return center * lax.rsqrt(spread + EPS) * gain + shift


def gelu_tanh(values):
    return jax.nn.gelu(values, approximate=True)


def plain_dot(left, right):
    return jnp.dot(left, right, preferred_element_type=jnp.float32)


def contract_rows(left, right):
    return lax.dot_general(
        left, right, (((0,), (0,)), ((), ())), preferred_element_type=jnp.float32
    )


def contract_cols(left, right):
    return lax.dot_general(
        left, right, (((1,), (1,)), ((), ())), preferred_element_type=jnp.float32
    )


def row_sum(values):
    return jnp.sum(values.astype(jnp.float32), axis=0)


def key_positions(pair_slots, local_rows, ctx_size):
    indices = jnp.arange(local_rows * ctx_size, dtype=jnp.int32)
    owner = indices // local_rows
    within = indices % local_rows
    half_len = local_rows // 2
    owner_hit = owner[:, None] == jnp.arange(ctx_size, dtype=jnp.int32)[None, :]
    partner = jnp.sum(jnp.where(owner_hit, pair_slots[None, :], 0), axis=1)
    piece = jnp.where(within < half_len, partner, 2 * ctx_size - 1 - partner)
    return piece * half_len + within % half_len


def block_scores(queries, key_blk, query_pos, query_seg, key_pos, key_seg):
    raw = jnp.einsum(
        "thd,khd->htk", queries, key_blk, preferred_element_type=jnp.float32
    ) * HEAD_DIM ** (-0.5)
    visible = (query_seg[:, None] == key_seg[None, :]) & (key_pos[None, :] <= query_pos[:, None])
    return (jnp.where(visible[None], raw, NEG), visible)


def log_normalizer(queries, key_blocks, geometry):
    query_pos, query_seg, pos_blocks, seg_blocks = geometry
    local_rows = queries.shape[0]

    def advance(state, entry):
        top_score, total_mass = state
        key_blk, key_pos, key_seg = entry
        scores, visible = block_scores(queries, key_blk, query_pos, query_seg, key_pos, key_seg)
        new_top = jnp.maximum(top_score, jnp.max(scores, axis=-1))
        fresh = jnp.sum(
            jnp.where(visible[None], jnp.exp(scores - new_top[..., None]), 0.0), axis=-1
        )
        return ((new_top, total_mass * jnp.exp(top_score - new_top) + fresh), None)

    initial = (
        jnp.full((HEADS, local_rows), NEG, jnp.float32),
        jnp.zeros((HEADS, local_rows), jnp.float32),
    )
    (top_score, total_mass), skipped = lax.scan(
        advance, initial, (key_blocks, pos_blocks, seg_blocks)
    )
    return top_score + jnp.log(total_mass)


def attend(queries, key_blocks, value_blocks, log_norm, geometry):
    query_pos, query_seg, pos_blocks, seg_blocks = geometry

    def advance(accum, entry):
        key_blk, value_blk, key_pos, key_seg = entry
        scores, visible = block_scores(queries, key_blk, query_pos, query_seg, key_pos, key_seg)
        probs = jnp.where(visible[None], jnp.exp(scores - log_norm[..., None]), 0.0).astype(
            jnp.bfloat16
        )
        return (
            accum
            + jnp.einsum("htk,khd->thd", probs, value_blk, preferred_element_type=jnp.float32),
            None,
        )

    initial = jnp.zeros(queries.shape, jnp.float32)
    mixed, skipped = lax.scan(advance, initial, (key_blocks, value_blocks, pos_blocks, seg_blocks))
    return mixed.reshape(queries.shape[0], -1)


def attend_back(queries, key_blocks, value_blocks, log_norm, row_delta, grad_out, geometry):
    query_pos, query_seg, pos_blocks, seg_blocks = geometry
    score_scale = HEAD_DIM ** (-0.5)

    def advance(grad_query, entry):
        key_blk, value_blk, key_pos, key_seg = entry
        scores, visible = block_scores(queries, key_blk, query_pos, query_seg, key_pos, key_seg)
        probs = jnp.where(visible[None], jnp.exp(scores - log_norm[..., None]), 0.0)
        grad_value = jnp.einsum(
            "htk,thd->khd", probs.astype(jnp.bfloat16), grad_out, preferred_element_type=jnp.float32
        )
        grad_prob = jnp.einsum(
            "thd,khd->htk", grad_out, value_blk, preferred_element_type=jnp.float32
        )
        grad_score = (probs * (grad_prob - row_delta[..., None])).astype(jnp.bfloat16)
        grad_query = (
            grad_query
            + jnp.einsum("htk,khd->thd", grad_score, key_blk, preferred_element_type=jnp.float32)
            * score_scale
        )
        grad_key = (
            jnp.einsum("htk,thd->khd", grad_score, queries, preferred_element_type=jnp.float32)
            * score_scale
        )
        return (grad_query, (grad_key, grad_value))

    initial = jnp.zeros(queries.shape, jnp.float32)
    grad_query, (grad_key, grad_value) = lax.scan(
        advance, initial, (key_blocks, value_blocks, pos_blocks, seg_blocks)
    )
    all_rows = grad_key.shape[0] * grad_key.shape[1]
    return (
        grad_query.reshape(queries.shape[0], -1),
        grad_key.reshape(all_rows, -1),
        grad_value.reshape(all_rows, -1),
    )


def forward_layer(hidden, weights, geometry, num_blocks):
    (
        gain_one,
        shift_one,
        w_qkv,
        b_qkv,
        w_proj,
        b_proj,
        gain_two,
        shift_two,
        w_fc,
        b_fc,
        w_out,
        b_out,
    ) = weights[:12]
    width = w_proj.shape[1]
    normed = layer_norm(hidden, gain_one.astype(jnp.float32), shift_one.astype(jnp.float32)).astype(
        jnp.bfloat16
    )
    packed = (plain_dot(normed, w_qkv) + b_qkv.astype(jnp.float32)).astype(jnp.bfloat16)
    local_keys = packed[:, width : 2 * width]
    local_values = packed[:, 2 * width :]
    key_all, value_all = (
        lax.all_gather(local_keys, "ctx", axis=0, tiled=True),
        lax.all_gather(local_values, "ctx", axis=0, tiled=True),
    )
    queries = packed[:, :width].reshape(-1, HEADS, HEAD_DIM)
    key_blocks = key_all.reshape(num_blocks, -1, HEADS, HEAD_DIM)
    value_blocks = value_all.reshape(num_blocks, -1, HEADS, HEAD_DIM)
    log_norm = log_normalizer(queries, key_blocks, geometry)
    mixed = attend(queries, key_blocks, value_blocks, log_norm, geometry)
    middle = hidden + plain_dot(mixed.astype(jnp.bfloat16), w_proj) + b_proj.astype(jnp.float32)
    normed_two = layer_norm(
        middle, gain_two.astype(jnp.float32), shift_two.astype(jnp.float32)
    ).astype(jnp.bfloat16)
    pre_act = plain_dot(normed_two, w_fc) + b_fc.astype(jnp.float32)
    activated = gelu_tanh(pre_act).astype(jnp.bfloat16)
    output = middle + plain_dot(activated, w_out) + b_out.astype(jnp.float32)
    saved = (
        normed,
        queries,
        key_blocks,
        value_blocks,
        log_norm,
        mixed,
        middle,
        normed_two,
        pre_act,
        activated,
    )
    return (output, saved)


def backward_layer(grad_next, hidden, saved, weights, geometry):
    (
        gain_one,
        shift_one,
        w_qkv,
        b_qkv,
        w_proj,
        b_proj,
        gain_two,
        shift_two,
        w_fc,
        b_fc,
        w_out,
        b_out,
    ) = weights[:12]
    (
        normed,
        queries,
        key_blocks,
        value_blocks,
        log_norm,
        mixed,
        middle,
        normed_two,
        pre_act,
        activated,
    ) = saved
    grad_branch = grad_next.astype(jnp.bfloat16)
    g_out_bias = row_sum(grad_branch)
    g_out_weight = contract_rows(activated, grad_branch)
    grad_act = contract_cols(grad_branch, w_out)
    gelu_pull = jax.vjp(gelu_tanh, pre_act)[1]
    grad_pre = gelu_pull(grad_act)[0].astype(jnp.bfloat16)
    g_fc_bias = row_sum(grad_pre)
    g_fc_weight = contract_rows(normed_two, grad_pre)
    grad_norm_two = contract_cols(grad_pre, w_fc)
    norm_pull = jax.vjp(
        layer_norm, middle, gain_two.astype(jnp.float32), shift_two.astype(jnp.float32)
    )[1]
    grad_mid_part, g_gain_two, g_shift_two = norm_pull(grad_norm_two)
    grad_mid = grad_next + grad_mid_part
    grad_attn = grad_mid.astype(jnp.bfloat16)
    g_proj_bias = row_sum(grad_attn)
    g_proj_weight = contract_rows(mixed.astype(jnp.bfloat16), grad_attn)
    grad_mixed = contract_cols(grad_attn, w_proj).astype(jnp.bfloat16)
    grad_out = grad_mixed.reshape(-1, HEADS, HEAD_DIM)
    row_delta = jnp.sum(
        grad_out.astype(jnp.float32) * mixed.reshape(-1, HEADS, HEAD_DIM), axis=-1
    ).T
    grad_query, grad_key_all, grad_value_all = attend_back(
        queries, key_blocks, value_blocks, log_norm, row_delta, grad_out, geometry
    )
    own_keys, own_values = (
        lax.psum_scatter(
            grad_key_all.astype(jnp.bfloat16), "ctx", scatter_dimension=0, tiled=True
        ).astype(jnp.float32),
        lax.psum_scatter(
            grad_value_all.astype(jnp.bfloat16), "ctx", scatter_dimension=0, tiled=True
        ).astype(jnp.float32),
    )
    grad_packed = jnp.concatenate([grad_query, own_keys, own_values], axis=1).astype(jnp.bfloat16)
    g_qkv_bias = row_sum(grad_packed)
    g_qkv_weight = contract_rows(normed, grad_packed)
    grad_norm_one = contract_cols(grad_packed, w_qkv)
    first_pull = jax.vjp(
        layer_norm, hidden, gain_one.astype(jnp.float32), shift_one.astype(jnp.float32)
    )[1]
    grad_in_part, g_gain_one, g_shift_one = first_pull(grad_norm_one)
    grads = (
        g_gain_one,
        g_shift_one,
        g_qkv_weight,
        g_qkv_bias,
        g_proj_weight,
        g_proj_bias,
        g_gain_two,
        g_shift_two,
        g_fc_weight,
        g_fc_bias,
        g_out_weight,
        g_out_bias,
    )
    return (grad_mid + grad_in_part, grads)


def fetch_layer(shards):
    return (
        lax.all_gather(shards[0], "fsdp", axis=0, tiled=True),
        lax.all_gather(shards[1], "fsdp", axis=0, tiled=True),
        lax.all_gather(shards[2], "fsdp", axis=0, tiled=True),
        lax.all_gather(shards[3], "fsdp", axis=0, tiled=True),
        lax.all_gather(shards[4], "fsdp", axis=0, tiled=True),
        lax.all_gather(shards[5], "fsdp", axis=0, tiled=True),
        lax.all_gather(shards[6], "fsdp", axis=0, tiled=True),
        lax.all_gather(shards[7], "fsdp", axis=0, tiled=True),
        lax.all_gather(shards[8], "fsdp", axis=0, tiled=True),
        lax.all_gather(shards[9], "fsdp", axis=0, tiled=True),
        lax.all_gather(shards[10], "fsdp", axis=0, tiled=True),
        lax.all_gather(shards[11], "fsdp", axis=0, tiled=True),
        lax.all_gather(shards[12], "fsdp", axis=0, tiled=True),
        lax.all_gather(shards[13], "fsdp", axis=0, tiled=True),
    )


def fetch_again(shards):
    return (
        lax.all_gather(shards[0], "fsdp", axis=0, tiled=True),
        lax.all_gather(shards[1], "fsdp", axis=0, tiled=True),
        lax.all_gather(shards[2], "fsdp", axis=0, tiled=True),
        lax.all_gather(shards[3], "fsdp", axis=0, tiled=True),
        lax.all_gather(shards[4], "fsdp", axis=0, tiled=True),
        lax.all_gather(shards[5], "fsdp", axis=0, tiled=True),
        lax.all_gather(shards[6], "fsdp", axis=0, tiled=True),
        lax.all_gather(shards[7], "fsdp", axis=0, tiled=True),
        lax.all_gather(shards[8], "fsdp", axis=0, tiled=True),
        lax.all_gather(shards[9], "fsdp", axis=0, tiled=True),
        lax.all_gather(shards[10], "fsdp", axis=0, tiled=True),
        lax.all_gather(shards[11], "fsdp", axis=0, tiled=True),
        lax.all_gather(shards[12], "fsdp", axis=0, tiled=True),
        lax.all_gather(shards[13], "fsdp", axis=0, tiled=True),
    )


def regroup(grad, ctx_size, fsdp_size):
    shaped = grad.reshape(
        (fsdp_size, ctx_size, grad.shape[0] // (fsdp_size * ctx_size)) + grad.shape[1:]
    )
    return jnp.swapaxes(shaped, 0, 1).reshape(grad.shape)


def reduce_layer(grads, ctx_size, fsdp_size):
    mixed = tuple((regroup(grad, ctx_size, fsdp_size) for grad in grads))
    parts = (
        lax.psum_scatter(mixed[0], ("ctx", "fsdp"), scatter_dimension=0, tiled=True),
        lax.psum_scatter(mixed[1], ("ctx", "fsdp"), scatter_dimension=0, tiled=True),
        lax.psum_scatter(mixed[2], ("ctx", "fsdp"), scatter_dimension=0, tiled=True),
        lax.psum_scatter(mixed[3], ("ctx", "fsdp"), scatter_dimension=0, tiled=True),
        lax.psum_scatter(mixed[4], ("ctx", "fsdp"), scatter_dimension=0, tiled=True),
        lax.psum_scatter(mixed[5], ("ctx", "fsdp"), scatter_dimension=0, tiled=True),
        lax.psum_scatter(mixed[6], ("ctx", "fsdp"), scatter_dimension=0, tiled=True),
        lax.psum_scatter(mixed[7], ("ctx", "fsdp"), scatter_dimension=0, tiled=True),
        lax.psum_scatter(mixed[8], ("ctx", "fsdp"), scatter_dimension=0, tiled=True),
        lax.psum_scatter(mixed[9], ("ctx", "fsdp"), scatter_dimension=0, tiled=True),
        lax.psum_scatter(mixed[10], ("ctx", "fsdp"), scatter_dimension=0, tiled=True),
        lax.psum_scatter(mixed[11], ("ctx", "fsdp"), scatter_dimension=0, tiled=True),
        lax.psum_scatter(mixed[12], ("ctx", "fsdp"), scatter_dimension=0, tiled=True),
        lax.psum_scatter(mixed[13], ("ctx", "fsdp"), scatter_dimension=0, tiled=True),
    )
    return (
        lax.all_gather(parts[0].astype(jnp.bfloat16), "ctx", axis=0, tiled=True).astype(
            jnp.float32
        ),
        lax.all_gather(parts[1].astype(jnp.bfloat16), "ctx", axis=0, tiled=True).astype(
            jnp.float32
        ),
        lax.all_gather(parts[2].astype(jnp.bfloat16), "ctx", axis=0, tiled=True).astype(
            jnp.float32
        ),
        lax.all_gather(parts[3].astype(jnp.bfloat16), "ctx", axis=0, tiled=True).astype(
            jnp.float32
        ),
        lax.all_gather(parts[4].astype(jnp.bfloat16), "ctx", axis=0, tiled=True).astype(
            jnp.float32
        ),
        lax.all_gather(parts[5].astype(jnp.bfloat16), "ctx", axis=0, tiled=True).astype(
            jnp.float32
        ),
        lax.all_gather(parts[6].astype(jnp.bfloat16), "ctx", axis=0, tiled=True).astype(
            jnp.float32
        ),
        lax.all_gather(parts[7].astype(jnp.bfloat16), "ctx", axis=0, tiled=True).astype(
            jnp.float32
        ),
        lax.all_gather(parts[8].astype(jnp.bfloat16), "ctx", axis=0, tiled=True).astype(
            jnp.float32
        ),
        lax.all_gather(parts[9].astype(jnp.bfloat16), "ctx", axis=0, tiled=True).astype(
            jnp.float32
        ),
        lax.all_gather(parts[10].astype(jnp.bfloat16), "ctx", axis=0, tiled=True).astype(
            jnp.float32
        ),
        lax.all_gather(parts[11].astype(jnp.bfloat16), "ctx", axis=0, tiled=True).astype(
            jnp.float32
        ),
        lax.all_gather(parts[12].astype(jnp.bfloat16), "ctx", axis=0, tiled=True).astype(
            jnp.float32
        ),
        lax.all_gather(parts[13].astype(jnp.bfloat16), "ctx", axis=0, tiled=True).astype(
            jnp.float32
        ),
    )


def local(
    acts,
    cotangent,
    pair_slots,
    segments,
    attn_gain,
    attn_shift,
    qkv_weight,
    qkv_bias,
    proj_weight,
    proj_bias,
    mlp_gain,
    mlp_shift,
    fc_weight,
    fc_bias,
    out_weight,
    out_bias,
    final_gain,
    final_shift,
):
    local_rows = acts.shape[1]
    ctx_size = lax.axis_size("ctx")
    fsdp_size = lax.axis_size("fsdp")
    ctx_rank = lax.axis_index("ctx")
    key_pos = key_positions(pair_slots, local_rows, ctx_size)
    all_rows = key_pos.shape[0]
    block_rows = min(512, all_rows)
    num_blocks = all_rows // block_rows
    key_seg = segments[0]
    query_pos = lax.dynamic_slice_in_dim(key_pos, ctx_rank * local_rows, local_rows)
    query_seg = lax.dynamic_slice_in_dim(key_seg, ctx_rank * local_rows, local_rows)
    geometry = (
        query_pos,
        query_seg,
        key_pos.reshape(num_blocks, block_rows),
        key_seg.reshape(num_blocks, block_rows),
    )
    stacked = (
        attn_gain,
        attn_shift,
        qkv_weight,
        qkv_bias,
        proj_weight,
        proj_bias,
        mlp_gain,
        mlp_shift,
        fc_weight,
        fc_bias,
        out_weight,
        out_bias,
    )
    hidden = acts[0].astype(jnp.float32)
    records = []
    for layer_index in range(LAYERS):
        shards = tuple((tensor[layer_index] for tensor in stacked)) + (final_gain, final_shift)
        weights = fetch_layer(shards)
        output, saved = forward_layer(hidden, weights, geometry, num_blocks)
        held = shards
        records.append((hidden, saved, held))
        hidden = output
    top_gain = weights[12].astype(jnp.float32)
    top_shift = weights[13].astype(jnp.float32)
    result = layer_norm(hidden, top_gain, top_shift)
    final_pull = jax.vjp(layer_norm, hidden, top_gain, top_shift)[1]
    grad_hidden, g_final_gain, g_final_shift = final_pull(cotangent[0].astype(jnp.float32))
    reduced = [None] * LAYERS
    for layer_index in reversed(range(LAYERS)):
        layer_in, saved, held = records[layer_index]
        weights = fetch_again(held)
        grad_hidden, grads = backward_layer(grad_hidden, layer_in, saved, weights, geometry)
        if layer_index == LAYERS - 1:
            extras = (g_final_gain, g_final_shift)
        else:
            extras = (jnp.zeros_like(g_final_gain), jnp.zeros_like(g_final_shift))
        reduced[layer_index] = reduce_layer(grads + extras, ctx_size, fsdp_size)
    stacked_grads = tuple(
        (
            jnp.stack([reduced[layer_index][slot] for layer_index in range(LAYERS)])
            for slot in range(12)
        )
    )
    top_grads = (reduced[LAYERS - 1][12], reduced[LAYERS - 1][13])
    return (
        (result.astype(jnp.bfloat16)[None], grad_hidden.astype(jnp.bfloat16)[None])
        + stacked_grads
        + top_grads
    )


def solution(mesh):
    return jax.shard_map(
        local,
        mesh=mesh,
        in_specs=(
            P("fsdp", "ctx", None),
            P("fsdp", "ctx", None),
            P(),
            P("fsdp", None),
            P(None, "fsdp"),
            P(None, "fsdp"),
            P(None, "fsdp", None),
            P(None, "fsdp"),
            P(None, "fsdp", None),
            P(None, "fsdp"),
            P(None, "fsdp"),
            P(None, "fsdp"),
            P(None, "fsdp", None),
            P(None, "fsdp"),
            P(None, "fsdp", None),
            P(None, "fsdp"),
            P("fsdp"),
            P("fsdp"),
        ),
        out_specs=(
            P("fsdp", "ctx", None),
            P("fsdp", "ctx", None),
            P(None, "fsdp"),
            P(None, "fsdp"),
            P(None, "fsdp", None),
            P(None, "fsdp"),
            P(None, "fsdp", None),
            P(None, "fsdp"),
            P(None, "fsdp"),
            P(None, "fsdp"),
            P(None, "fsdp", None),
            P(None, "fsdp"),
            P(None, "fsdp", None),
            P(None, "fsdp"),
            P("fsdp"),
            P("fsdp"),
        ),
        check_vma=False,
    )
```

profile of v0, /device:TPU:0, one launch (start us, length us, event | category | flops | bytes accessed | tf_op | source)
XLA Modules:
  0.0 3858.2 jit_solution(15503010777332376323)
XLA Ops:
  46.9 82.5 %all-gather.67.cloned.1.call-done = bf16[1,1024,3072]{2,1,0:T(8,128)(2,1)} async-done(((bf16[1,256,3072]{2,1,0:T(8,128)(2,1)}), bf16[1,1024,3072]{2,1,0:T(8,128)(2,1)}) %all-gather.67.cloned.1.call-update) | async-done | bytes 6291472 | tf_op jit(solution)/shard_map/all_gather | solution.py:288
  249.4 44.6 %while.78 = (s32[]{:T(128)}, f32[16,256]{1,0:T(8,128)S(1)}, f32[16,256]{1,0:T(8,128)S(1)}, s32[256]{0:T(256)S(1)}, s32[4,512]{1,0:T(4,128)S(1)}, /*index=5*/s32[...) while((s32[]{:T(128)}, f32[16,256]{1,0:T(8,128)S(1)}, ...), condition=%wide.region_6.7_spmd.clone, body=%wide.region_3.6_spmd.clone.sunk | while | flops 285626368 | bytes 18971260 | solution.py:82
  340.2 66.8 %all-gather.71.cloned.1.call-done = bf16[1,1024,4096]{2,1,0:T(8,128)(2,1)} async-done(((bf16[1,256,4096]{2,1,0:T(8,128)(2,1)}), bf16[1,1024,4096]{2,1,0:T(8,128)(2,1)}) %all-gather.71.cloned.1.call-update) | async-done | bytes 8388624 | tf_op jit(solution)/shard_map/all_gather | solution.py:294
  414.9 141.4 %all-gather.73.cloned.1.call-done = bf16[1,4096,1024]{2,1,0:T(8,128)(2,1)} async-done(((bf16[1,1024,1024]{2,1,0:T(8,128)(2,1)}), bf16[1,4096,1024]{2,1,0:T(8,128)(2,1)}) %all-gather.73.cloned.1.call-update) | async-done | bytes 8388624 | tf_op jit(solution)/shard_map/all_gather | solution.py:296
  564.1 107.4 %all-gather.75.cloned.1.call-done = bf16[1,1024,3072]{2,1,0:T(8,128)(2,1)} async-done(((bf16[1,256,3072]{2,1,0:T(8,128)(2,1)}), bf16[1,1024,3072]{2,1,0:T(8,128)(2,1)}) %all-gather.75.cloned.1.call-update) | async-done | bytes 6291472 | tf_op jit(solution)/shard_map/all_gather | solution.py:288
  787.9 44.7 %while.80 = (s32[]{:T(128)}, f32[16,256]{1,0:T(8,128)S(1)}, f32[16,256]{1,0:T(8,128)S(1)}, s32[256]{0:T(256)S(1)}, s32[4,512]{1,0:T(4,128)S(1)}, /*index=5*/s32[...) while((s32[]{:T(128)}, f32[16,256]{1,0:T(8,128)S(1)}, ...), condition=%wide.region_16.17_spmd.clone, body=%wide.region_13.16_spmd.clone.sunk | while | flops 285626368 | bytes 18971260 | solution.py:82
  861.6 87.4 %all-gather.79.cloned.1.call-done = bf16[1,1024,4096]{2,1,0:T(8,128)(2,1)} async-done(((bf16[1,256,4096]{2,1,0:T(8,128)(2,1)}), bf16[1,1024,4096]{2,1,0:T(8,128)(2,1)}) %all-gather.79.cloned.1.call-update) | async-done | bytes 8388624 | tf_op jit(solution)/shard_map/all_gather | solution.py:294
  957.2 141.7 %all-gather.81.cloned.1.call-done = bf16[1,4096,1024]{2,1,0:T(8,128)(2,1)} async-done(((bf16[1,1024,1024]{2,1,0:T(8,128)(2,1)}), bf16[1,4096,1024]{2,1,0:T(8,128)(2,1)}) %all-gather.81.cloned.1.call-update) | async-done | bytes 8388624 | tf_op jit(solution)/shard_map/all_gather | solution.py:296
  1130.4 91.9 %while.82 = (s32[]{:T(128)}, f32[256,16,64]{0,2,1:T(8,128)S(1)}, bf16[4,512,16,64]{1,3,2,0:T(8,128)(2,1)}, bf16[4,512,16,64]{1,3,2,0:T(8,128)(2,1)}, bf16[4,512,...) while((s32[]{:T(128)}, f32[256,16,64]{0,2,1:T(8,128)S(1)}, ...), condition=%wide.region_29.30_spmd.clone, body=%wide.region_28.29_spmd.clone.sunk | while | flops 1369047040 | bytes 100074200 | solution.py:135
  1241.2 40.0 %reduce-scatter.13.cloned.1.call-done = bf16[256,1024]{0,1:T(8,128)(2,1)} async-done(((bf16[2048,1024]{0,1:T(8,128)(2,1)}), bf16[256,1024]{0,1:T(8,128)(2,1)}) %reduce-scatter.13.cloned.1.call-update) | async-done | bytes 524304 | tf_op jit(solution)/shard_map/reduce_scatter | solution.py:252
  1281.1 55.5 %reduce-scatter.15.cloned.1.call-done = bf16[256,1024]{0,1:T(8,128)(2,1)} async-done(((bf16[2048,1024]{0,1:T(8,128)(2,1)}), bf16[256,1024]{0,1:T(8,128)(2,1)}) %reduce-scatter.15.cloned.1.call-update) | async-done | bytes 524304 | tf_op jit(solution)/shard_map/reduce_scatter | solution.py:255
  1369.6 92.1 %while.83 = (s32[]{:T(128)}, f32[256,16,64]{0,2,1:T(8,128)S(1)}, bf16[4,512,16,64]{1,3,2,0:T(8,128)(2,1)}, bf16[4,512,16,64]{1,3,2,0:T(8,128)(2,1)}, bf16[4,512,...) while((s32[]{:T(128)}, f32[256,16,64]{0,2,1:T(8,128)S(1)}, ...), condition=%wide.region_38.39_spmd.clone, body=%wide.region_37.38_spmd.clone.sunk | while | flops 1369047040 | bytes 104268560 | solution.py:135
  1535.9 55.5 %reduce-scatter.19.cloned.1.call-done = bf16[256,1024]{1,0:T(8,128)(2,1)} async-done(((bf16[2048,1024]{1,0:T(8,128)(2,1)}), bf16[256,1024]{1,0:T(8,128)(2,1)}) %reduce-scatter.19.cloned.1.call-update) | async-done | bytes 524304 | tf_op jit(solution)/shard_map/reduce_scatter | solution.py:255
  1678.0 74.6 %reduce-scatter.23.cloned.1.call-done = f32[32,3072]{1,0:T(8,128)} async-done(((f32[1024,3072]{1,0:T(8,128)}), f32[32,3072]{1,0:T(8,128)}) %reduce-scatter.23.cloned.1.call-update) | async-done | bytes 393232 | tf_op jit(solution)/shard_map/reduce_scatter | solution.py:334
  1754.4 159.6 %reduce-scatter.21.cloned.1.call-done = f32[32,3072]{1,0:T(8,128)} async-done(((f32[1024,3072]{1,0:T(8,128)}), f32[32,3072]{1,0:T(8,128)}) %reduce-scatter.21.cloned.1.call-update) | async-done | bytes 393232 | tf_op jit(solution)/shard_map/reduce_scatter | solution.py:334
  1915.9 363.8 %reduce-scatter.35.cloned.1.call-done = f32[128,1024]{1,0:T(8,128)} async-done(((f32[4096,1024]{1,0:T(8,128)}), f32[128,1024]{1,0:T(8,128)}) %reduce-scatter.35.cloned.1.call-update) | async-done | bytes 524304 | tf_op jit(solution)/shard_map/reduce_scatter | solution.py:342
  2281.5 362.5 %reduce-scatter.33.cloned.1.call-done = f32[128,1024]{1,0:T(8,128)} async-done(((f32[4096,1024]{1,0:T(8,128)}), f32[128,1024]{1,0:T(8,128)}) %reduce-scatter.33.cloned.1.call-update) | async-done | bytes 524304 | tf_op jit(solution)/shard_map/reduce_scatter | solution.py:342
  2645.9 362.6 %reduce-scatter.31.cloned.1.call-done = f32[32,4096]{1,0:T(8,128)} async-done(((f32[1024,4096]{1,0:T(8,128)}), f32[32,4096]{1,0:T(8,128)}) %reduce-scatter.31.cloned.1.call-update) | async-done | bytes 524304 | tf_op jit(solution)/shard_map/reduce_scatter | solution.py:340
  3010.4 362.6 %reduce-scatter.29.cloned.1.call-done = f32[32,4096]{1,0:T(8,128)} async-done(((f32[1024,4096]{1,0:T(8,128)}), f32[32,4096]{1,0:T(8,128)}) %reduce-scatter.29.cloned.1.call-update) | async-done | bytes 524304 | tf_op jit(solution)/shard_map/reduce_scatter | solution.py:340
  3379.5 142.1 %reduce-scatter.27.cloned.1.call-done = f32[32,1024]{1,0:T(8,128)} async-done(((f32[1024,1024]{1,0:T(8,128)}), f32[32,1024]{1,0:T(8,128)}) %reduce-scatter.27.cloned.1.call-update) | async-done | bytes 131088 | tf_op jit(solution)/shard_map/reduce_scatter | solution.py:336
  3535.7 40.1 %all-reduce.34 = (bf16[1024]{0:T(1024)(128)(2,1)S(1)}, bf16[1024]{0:T(1024)(128)(2,1)S(1)}, bf16[1024]{0:T(1024)(128)(2,1)S(1)}, bf16[1024]{0:T(1024)(128)(2,1)S...) all-reduce(f32[1024]{0:T(1024)S(1)} %reshape.790, ...), channel_id=31, replica_groups=mesh['ctx'=8,'fsdp'=4] {'ctx','fsdp'}, use_global_device_ids=true, to_apply=%region_46.47.clone | all-reduce | flops 28672 | bytes 172032
  3628.2 43.2 %reduce-scatter.25.cloned.1.call-done = f32[32,1024]{1,0:T(8,128)} async-done(((f32[1024,1024]{1,0:T(8,128)}), f32[32,1024]{1,0:T(8,128)}) %reduce-scatter.25.cloned.1.call-update) | async-done | bytes 131088 | tf_op jit(solution)/shard_map/reduce_scatter | solution.py:336
  3755.1 29.8 all-gather.63.cloned.1.call-done
  3815.4 29.7 all-gather.59.cloned.1.call-done
  (811 shorter events, 1132.8 us)
Async XLA Ops:
  11.1 217.0 %all-gather.49.cloned.1.call-start = ((), (), s32[]{:S(2)}) async-start(), calls=%async_computation.13 | async-start | bytes 4718592 | tf_op jit(solution)/shard_map/all_gather | solution.py:169
  136.1 201.2 %all-gather.69.cloned.1.call-start = ((), (), s32[]{:S(2)}) async-start(), calls=%async_computation.35 | async-start | bytes 2621440 | tf_op jit(solution)/shard_map/all_gather | solution.py:290
  137.2 269.8 %all-gather.71.cloned.1.call-start = ((), (), s32[]{:S(2)}) async-start(), calls=%async_computation.36 | async-start | bytes 10485760 | tf_op jit(solution)/shard_map/all_gather | solution.py:294
  142.1 414.2 %all-gather.73.cloned.1.call-start = ((), (), s32[]{:S(2)}) async-start(), calls=%async_computation.37 | async-start | bytes 10485760 | tf_op jit(solution)/shard_map/all_gather | solution.py:296
  147.0 524.5 %all-gather.75.cloned.1.call-start = ((), (), s32[]{:S(2)}) async-start(), calls=%async_computation.38 | async-start | bytes 7864320 | tf_op jit(solution)/shard_map/all_gather | solution.py:288
  147.7 597.3 %all-gather.53.cloned.1.call-start = ((), (), s32[]{:S(2)}) async-start(), calls=%async_computation.15 | async-start | bytes 4718592 | tf_op jit(solution)/shard_map/all_gather | solution.py:169
  678.7 270.3 %all-gather.79.cloned.1.call-start = ((), (), s32[]{:S(2)}) async-start(), calls=%async_computation.40 | async-start | bytes 10485760 | tf_op jit(solution)/shard_map/all_gather | solution.py:294
  679.4 419.4 %all-gather.81.cloned.1.call-start = ((), (), s32[]{:S(2)}) async-start(), calls=%async_computation.41 | async-start | bytes 10485760 | tf_op jit(solution)/shard_map/all_gather | solution.py:296
  680.0 601.1 %reduce-scatter.13.cloned.1.call-start = ((), (), s32[]{:S(2)}) async-start(), calls=%async_computation.16 | async-start | bytes 4718592 | tf_op jit(solution)/shard_map/reduce_scatter | solution.py:252
  1240.6 295.2 %reduce-scatter.17.cloned.1.call-start = ((), (), s32[]{:S(2)}) async-start(), calls=%async_computation.18 | async-start | bytes 4718592 | tf_op jit(solution)/shard_map/reduce_scatter | solution.py:252
  1507.4 245.3 %reduce-scatter.23.cloned.1.call-start = ((), (), s32[]{:S(2)}) async-start(), calls=%async_computation.22 | async-start | bytes 12976128 | tf_op jit(solution)/shard_map/reduce_scatter | solution.py:334
  1527.1 387.0 %reduce-scatter.21.cloned.1.call-start = ((), (), s32[]{:S(2)}) async-start(), calls=%async_computation.20 | async-start | bytes 12976128 | tf_op jit(solution)/shard_map/reduce_scatter | solution.py:334
  1619.5 660.2 %reduce-scatter.35.cloned.1.call-start = ((), (), s32[]{:S(2)}) async-start(), calls=%async_computation.32 | async-start | bytes 17301504 | tf_op jit(solution)/shard_map/reduce_scatter | solution.py:342
  1632.3 1011.8 %reduce-scatter.33.cloned.1.call-start = ((), (), s32[]{:S(2)}) async-start(), calls=%async_computation.30 | async-start | bytes 17301504 | tf_op jit(solution)/shard_map/reduce_scatter | solution.py:342
  1644.7 1363.8 %reduce-scatter.31.cloned.1.call-start = ((), (), s32[]{:S(2)}) async-start(), calls=%async_computation.28 | async-start | bytes 17301504 | tf_op jit(solution)/shard_map/reduce_scatter | solution.py:340
  1656.9 1716.1 %reduce-scatter.29.cloned.1.call-start = ((), (), s32[]{:S(2)}) async-start(), calls=%async_computation.26 | async-start | bytes 17301504 | tf_op jit(solution)/shard_map/reduce_scatter | solution.py:340
  1668.5 1853.1 %reduce-scatter.27.cloned.1.call-start = ((), (), s32[]{:S(2)}) async-start(), calls=%async_computation.25 | async-start | bytes 4325376 | tf_op jit(solution)/shard_map/reduce_scatter | solution.py:336
  1673.8 1997.6 %reduce-scatter.25.cloned.1.call-start = ((), (), s32[]{:S(2)}) async-start(), calls=%async_computation.24 | async-start | bytes 4325376 | tf_op jit(solution)/shard_map/reduce_scatter | solution.py:336
  1678.0 2020.0 %all-gather.57.cloned.1.call-start = ((), (), s32[]{:S(2)}) async-start(), calls=%async_computation.23 | async-start | bytes 1769472 | tf_op jit(solution)/shard_map/all_gather | solution.py:354
  1754.4 1971.1 %all-gather.55.cloned.1.call-start = ((), (), s32[]{:S(2)}) async-start(), calls=%async_computation.21 | async-start | bytes 1769472 | tf_op jit(solution)/shard_map/all_gather | solution.py:354
  1915.8 1839.3 %all-gather.65.cloned.1.call-start = ((), (), s32[]{:S(2)}) async-start(), calls=%async_computation.33 | async-start | bytes 2359296 | tf_op jit(solution)/shard_map/all_gather | solution.py:378
  2281.5 1503.5 %all-gather.63.cloned.1.call-start = ((), (), s32[]{:S(2)}) async-start(), calls=%async_computation.31 | async-start | bytes 2359296 | tf_op jit(solution)/shard_map/all_gather | solution.py:378
  2645.8 1169.5 %all-gather.61.cloned.1.call-start = ((), (), s32[]{:S(2)}) async-start(), calls=%async_computation.29 | async-start | bytes 2359296 | tf_op jit(solution)/shard_map/all_gather | solution.py:372
  3010.3 834.7 %all-gather.59.cloned.1.call-start = ((), (), s32[]{:S(2)}) async-start(), calls=%async_computation.27 | async-start | bytes 2359296 | tf_op jit(solution)/shard_map/all_gather | solution.py:372
  (146 other events, 36861.1 us)
Sparse Core Ops, SparseCore 0:
  11.2 118.2 all-gather.66
  135.4 35.0 all-gather.48
  173.0 36.7 all-gather.46
  211.1 45.9 all-gather.68
  258.5 148.4 all-gather.70
  408.4 147.8 all-gather.72
  557.9 113.5 all-gather.74
  677.5 34.9 all-gather.52
  714.9 36.7 all-gather.50
  753.1 45.9 all-gather.76
  800.7 148.2 all-gather.78
  951.0 147.8 all-gather.80
  1231.6 49.5 reduce-scatter.12
  1285.3 51.3 reduce-scatter.14
  1484.5 51.2 reduce-scatter.16
  1540.0 51.3 reduce-scatter.18
  1597.3 155.3 reduce-scatter.22
  1759.6 154.4 reduce-scatter.20
  1916.4 363.2 reduce-scatter.34
  2281.8 362.1 reduce-scatter.32
  2646.3 362.1 reduce-scatter.30
  3010.8 362.1 reduce-scatter.28
  3375.9 145.6 reduce-scatter.26
  3524.3 147.0 reduce-scatter.24
  (6 shorter events, 161.7 us)
where the time goes:
time: 3870 us; the launch traced here: 3860 us
  waiting for transfers between devices  2810 us (73%)
  matrix products  372 us (10%)
  blocking collectives  281 us (7%)
  local copies, waits for them, and re-layouts  274 us (7%)
  other arithmetic  97.3 us (3%)
    reduce_scatter x2, waiting for transfers between devices, reduce_layer(): lax.psum_scatter(mixed[10], ('ctx', 'fsdp'), scatter_dimension=0, tiled=T...  726 us
    reduce_scatter x2, waiting for transfers between devices, reduce_layer(): lax.psum_scatter(mixed[8], ('ctx', 'fsdp'), scatter_dimension=0, tiled=True)  725 us
    all_gather x2, waiting for transfers between devices, fetch_layer(): lax.all_gather(shards[10], 'fsdp', axis=0, tiled=True)  283 us
    reduce_scatter x2, waiting for transfers between devices, reduce_layer(): lax.psum_scatter(mixed[2], ('ctx', 'fsdp'), scatter_dimension=0, tiled=True)  234 us
    all_gather x2, waiting for transfers between devices, fetch_layer(): lax.all_gather(shards[2], 'fsdp', axis=0, tiled=True)  190 us
    reduce_scatter x2, waiting for transfers between devices, reduce_layer(): lax.psum_scatter(mixed[4], ('ctx', 'fsdp'), scatter_dimension=0, tiled=True)  185 us
    all_gather x2, waiting for transfers between devices, fetch_layer(): lax.all_gather(shards[8], 'fsdp', axis=0, tiled=True)  154 us
    reduce_scatter x2, waiting for transfers between devices, backward_layer(): lax.psum_scatter(grad_value_all.astype(jnp.bfloat16), 'ctx', scatter_dime...  111 us
  transfers between devices with their start and end apart: 30, of which 24 were waited for; matrix products, arithmetic and copies ran while one was open for 11% of the time, Pallas kernels for 0%

commit v1 on v0

v1 whole, which is shorter than its diff:
```python
import collections
import functools
import itertools

import jax
import jax.numpy as jnp
from jax import lax
from jax.experimental import pallas as pl
from jax.experimental.pallas import tpu as pltpu
from jax.sharding import PartitionSpec as P

HEADS = 16
HEAD_DIM = 64
LAYERS = 2
EPS = 1e-05
NEG = -1e30
LOW = -1e29
F32 = jnp.float32
BF16 = jnp.bfloat16
VMEM_BYTES = 56 * 1024 * 1024

FIELDS = ("t", "d", "ff", "nf", "nc", "pr", "pc", "nq", "ncs", "ffn", "w", "hl", "rows", "half")
Dims = collections.namedtuple("Dims", FIELDS)


def dims_of(acts, fc_weight, nf, nc):
    t, d = acts.shape[1], acts.shape[2]
    ff = fc_weight.shape[2]
    pr, pc = d // nf, ff // nc
    return Dims(
        t=t, d=d, ff=ff, nf=nf, nc=nc, pr=pr, pc=pc, nq=3 * d // pc, ncs=d // pc, ffn=ff // nf,
        w=d // nc, hl=HEADS // nc, rows=t * nc, half=t // 2,
    )


SMALL = (("g1", 1), ("s1", 1), ("bq", 3), ("bp", 1), ("g2", 1), ("s2", 1), ("bf", 4), ("bo", 1))


def small_offsets(dm):
    table, at = {}, 0
    for layer in range(LAYERS):
        for name, _ in SMALL:
            size = {"bq": 3 * dm.pr, "bf": dm.ffn}.get(name, dm.pr)
            table[name + str(layer)] = (at, size)
            at += size
    for name in ("gf", "sf"):
        table[name] = (at, dm.pr)
        at += dm.pr
    return table, at


def send_blocks(dm, at, shape):
    return Move(
        shape, BF16,
        [([(None, Local(at), (j,))], ("ctx", j) if j else None, (j,)) for j in range(dm.nc)],
    )


def mult(value, by):
    return pl.multiple_of(value, by)


def nn(a, b):
    return lax.dot_general(a, b, (((1,), (0,)), ((), ())), preferred_element_type=F32)


def nt(a, b):
    return lax.dot_general(a, b, (((1,), (1,)), ((), ())), preferred_element_type=F32)


def tn(a, b):
    return lax.dot_general(a, b, (((0,), (0,)), ((), ())), preferred_element_type=F32)


def col_sum(v):
    return jnp.sum(v.astype(F32), axis=0, keepdims=True)


def small_vec(dm, small_ref, name):
    at, size = small_offsets(dm)[0][name]
    return jnp.concatenate([small_ref[g : g + 1, at : at + size] for g in range(dm.nf)], axis=1)


def norm_parts(v):
    center = v - jnp.mean(v, axis=-1, keepdims=True)
    scale = lax.rsqrt(jnp.mean(center * center, axis=-1, keepdims=True) + EPS)
    return center * scale, scale


def norm(v, gain, shift):
    return norm_parts(v)[0] * gain + shift


def norm_back(v, gain, dy):
    xh, scale = norm_parts(v)
    e = dy * gain
    dv = scale * (
        e - jnp.mean(e, axis=-1, keepdims=True) - xh * jnp.mean(e * xh, axis=-1, keepdims=True)
    )
    return dv, col_sum(dy * xh), col_sum(dy)


K0 = 0.7978845608028654
K1 = 0.044715


def gelu(u):
    return 0.5 * u * (1.0 + jnp.tanh(K0 * (u + K1 * u * u * u)))


def gelu_slope(u):
    th = jnp.tanh(K0 * (u + K1 * u * u * u))
    return 0.5 * (1.0 + th) + 0.5 * u * (1.0 - th * th) * (K0 * (1.0 + 3.0 * K1 * u * u))


class Local:
    def __init__(self, at):
        self.at = at


class Move:
    def __init__(self, shape, dtype, parts):
        self.shape, self.dtype, self.parts = shape, dtype, parts
        self.result = None

    def inside(self):
        return any(
            isinstance(src, Local) or (isinstance(src, Move) and src.result is None)
            for sources, _, _ in self.parts
            for _, src, _ in sources
        )


def whole(array, route):
    return Move(array.shape, array.dtype, [([(None, array, None)], route, None)])


def at_of(ref, index):
    return ref if index is None else ref.at[index() if callable(index) else index]


def run(dm, body, operands, outs, scratch, flops, grid=None, in_specs=None, out_specs=None, alias=None,
        moves=(), ids=None):
    places = {"v": pltpu.VMEM, "s": pltpu.SMEM, "a": pl.ANY}
    specs = list(in_specs or [pl.BlockSpec(memory_space=places[p]) for _, p in operands])
    arrays = [a for a, _ in operands]
    outs = list(outs)
    out_specs = list(out_specs or [pl.BlockSpec(memory_space=pltpu.VMEM)] * len(outs))
    scratch = list(scratch)
    n_in, n_out, n_scratch = len(arrays), len(outs), len(scratch)
    bytes_moved = sum(a.size * a.dtype.itemsize for a in arrays)
    bytes_moved += sum(o.size * o.dtype.itemsize for o in outs)
    kwargs = {"grid": grid} if grid else {}
    params = {}
    kernel = body
    moves = list(moves)
    if moves:
        sent = {}
        for move in moves:
            for sources, _, _ in move.parts:
                for _, src, _ in sources:
                    array = src.result if isinstance(src, Move) else src
                    if array is not None and not isinstance(array, Local) and id(array) not in sent:
                        sent[id(array)] = n_in + len(sent)
                        arrays.append(array)
                        specs.append(pl.BlockSpec(memory_space=pl.ANY))
        total_in = len(arrays)
        outs += [sds(m.shape, m.dtype) for m in moves]
        out_specs += [pl.BlockSpec(memory_space=pl.ANY)] * len(moves)
        count = sum(len(m.parts) for m in moves)
        scratch += [pltpu.SemaphoreType.DMA((count,)), pltpu.SemaphoreType.DMA((count,))]
        pending = {id(m): n for n, m in enumerate(moves)}
        fixed = [m.result is None for m in moves]
        assert all(fixed)
        routes = sorted({route for m in moves for _, route, _ in m.parts if route is not None})

        def kernel(*refs):
            ins, out_refs = refs[:total_in], refs[total_in : total_in + len(outs)]
            rest = refs[total_in + len(outs) :]
            own_refs = ins[:n_in] + out_refs[:n_out] + rest[:n_scratch]
            send_sems, recv_sems = rest[n_scratch], rest[n_scratch + 1]
            c, f = lax.axis_index("ctx"), lax.axis_index("fsdp")

            def device(route, back=False):
                axis, by = route
                if axis == "ctx":
                    return (c ^ by, f)
                by = dm.nf - by if back else by
                return (c, lax.rem(f + by, dm.nf))

            barrier = pltpu.get_barrier_semaphore()
            for route in routes:
                pl.semaphore_signal(
                    barrier, inc=1, device_id=device(route, True), device_id_type=pl.DeviceIdType.MESH
                )
            pl.semaphore_wait(barrier, len(routes))

            def ref_of(src):
                if isinstance(src, Local):
                    return own_refs[src.at]
                if isinstance(src, Move):
                    if id(src) in pending:
                        return out_refs[n_out + pending[id(src)]]
                    src = src.result
                return ins[sent[id(src)]]

            first, copies = 0, []
            for n, move in enumerate(moves):
                row = []
                for sources, route, place in move.parts:
                    choices = []
                    for cond, src, index in sources:
                        if route is None:
                            choices.append((cond, pltpu.make_async_copy(
                                at_of(ref_of(src), index), at_of(out_refs[n_out + n], place),
                                recv_sems.at[first],
                            )))
                            continue
                        copy = pltpu.make_async_remote_copy(
                            src_ref=at_of(ref_of(src), index),
                            dst_ref=at_of(out_refs[n_out + n], place),
                            send_sem=send_sems.at[first],
                            recv_sem=recv_sems.at[first],
                            device_id=device(route),
                            device_id_type=pl.DeviceIdType.MESH,
                        )
                        choices.append((cond, copy))
                    row.append(choices)
                    first += 1
                copies.append(row)
            arrived = set()

            def wait(n):
                if n not in arrived:
                    arrived.add(n)
                    for choices, part in zip(copies[n], moves[n].parts):
                        copy = choices[0][1]
                        copy.wait() if part[1] is None else copy.wait_recv()

            def start(n):
                for sources, _, _ in moves[n].parts:
                    for _, src, _ in sources:
                        if isinstance(src, Move) and id(src) in pending:
                            wait(pending[id(src)])
                for choices in copies[n]:
                    for cond, copy in choices:
                        if cond is None:
                            copy.start()
                        else:
                            pl.when(cond())(copy.start)

            early = 0
            while early < len(moves) and not moves[early].inside():
                start(early)
                early += 1
            if body is not None:
                body(*own_refs)
            for n in range(early, len(moves)):
                start(n)
            for n in range(len(moves)):
                wait(n)
            for row, move in zip(copies, moves):
                for choices, part in zip(row, move.parts):
                    if part[1] is not None:
                        choices[0][1].wait_send()

        params = {"collective_id": next(ids), "has_side_effects": True}
    results = pl.pallas_call(
        kernel,
        out_shape=outs,
        in_specs=specs,
        out_specs=out_specs,
        scratch_shapes=scratch,
        input_output_aliases=alias or {},
        compiler_params=pltpu.CompilerParams(vmem_limit_bytes=VMEM_BYTES, **params),
        cost_estimate=pl.CostEstimate(flops=flops, bytes_accessed=bytes_moved, transcendentals=0),
        **kwargs,
    )(*arrays)
    for move, result in zip(moves, results[n_out:]):
        move.result = result
    return results[:n_out]


def sds(shape, dtype):
    return jax.ShapeDtypeStruct(shape, dtype)


class Pieces:
    def __init__(self, dm, layer, own, pieces, own_buf, piece_buf, sems, wanted):
        self.dm, self.wanted = dm, wanted
        self.own_copy = pltpu.make_async_copy(own.at[layer], own_buf, sems.at[dm.nc])
        self.copies = [
            pltpu.make_async_copy(pieces[j], piece_buf.at[j], sems.at[j]) for j in range(dm.nc)
        ]
        self.own, self.buf = own_buf, piece_buf

    def start(self):
        self.own_copy.start()
        for j in range(self.dm.nc):
            self.each(j, self.copies[j].start)

    def each(self, j, act):
        if self.wanted is None:
            act()
        else:
            pl.when(self.wanted(j))(act)

    def wait_own(self):
        self.own_copy.wait()

    def flat(self, j):
        return self.buf[j].reshape((self.dm.nf - 1) * self.dm.pr, self.dm.pc)


def piece_scratch(dm, own_shape):
    return [
        pltpu.VMEM(own_shape, BF16),
        pltpu.VMEM((dm.nc, dm.nf - 1, dm.pr, dm.pc), BF16),
        pltpu.SemaphoreType.DMA((dm.nc + 1,)),
    ]


def ring(dm, f, s):
    return lax.rem(f + (dm.nf - s), dm.nf)


def relative(dm, f, src, dst):
    for s in range(dm.nf):
        at = mult(ring(dm, f, s) * dm.pr, dm.pr)
        dst[:, s * dm.pr : (s + 1) * dm.pr] = src[:, pl.ds(at, dm.pr)]


def take_heads(dm, ref, base, i):
    if dm.w % 128 == 0:
        return ref[:, pl.ds(mult(base + i * dm.w, 128), dm.w)]
    per = 128 // dm.w
    wide = ref[:, pl.ds(mult(base + (i // per) * 128, 128), 128)]
    part = wide[:, : dm.w]
    for at in range(1, per):
        part = jnp.where(lax.rem(i, per) == at, wide[:, at * dm.w : (at + 1) * dm.w], part)
    return part


def put_heads(dm, ref, base, blocks, at, c):
    if dm.w % 128 == 0:
        for j in range(dm.nc):
            ref[:, pl.ds(mult(base + (c ^ j) * dm.w, 128), dm.w)] = blocks[j][:, at : at + dm.w]
        return
    for j in range(0, dm.nc, 2):
        one, two = blocks[j][:, at : at + dm.w], blocks[j + 1][:, at : at + dm.w]
        even = lax.rem(c, 2) == 0
        pair = jnp.concatenate([jnp.where(even, one, two), jnp.where(even, two, one)], axis=1)
        ref[:, pl.ds(mult(base + ((c ^ j) // 2) * 128, 128), 128)] = pair


def qkv_body(dm, layer, *refs):
    nc = dm.nc
    meta, h, small, own = refs[:4]
    pieces = refs[4 : 4 + nc]
    n1, xr, y, bias, blocks, own_buf, piece_buf, sems = refs[4 + nc :]
    c, f = lax.axis_index("ctx"), lax.axis_index("fsdp")
    weight = Pieces(dm, layer, own, pieces, own_buf, piece_buf, sems, lambda j: (c ^ j) < dm.nq)
    weight.start()
    tag = str(layer)
    n1[...] = norm(
        h[...].astype(F32), small_vec(dm, small, "g1" + tag), small_vec(dm, small, "s1" + tag)
    ).astype(BF16)
    bias[...] = small_vec(dm, small, "bq" + tag)
    relative(dm, f, n1, xr)
    weight.wait_own()
    for j in range(nc):
        i = c ^ j

        @pl.when(i < dm.nq)
        def _():
            weight.copies[j].wait()
            at = pl.ds(mult(i * dm.pc, dm.pc), dm.pc)
            acc = nn(xr[:, dm.pr :], weight.flat(j)) + nn(xr[:, : dm.pr], own_buf[:, at])
            y[:, at] = (acc + bias[:, at]).astype(BF16)

    for j in range(nc):
        for third in range(3):
            blocks[j, :, third * dm.w : (third + 1) * dm.w] = take_heads(
                dm, y, third * dm.d, c ^ j
            )


def qkv_call(dm, layer, meta, h, small, own, pieces, moves, ids):
    shape = (dm.nc, dm.t, 3 * dm.w)
    blocks = send_blocks(dm, 8 + dm.nc, shape)
    n1 = run(
        dm,
        functools.partial(qkv_body, dm, layer),
        [(meta, "s"), (h, "v"), (small, "v"), (own, "a")] + [(p, "a") for p in pieces],
        [sds((dm.t, dm.d), BF16)],
        [
            pltpu.VMEM((dm.t, dm.d), BF16),
            pltpu.VMEM((dm.t, 3 * dm.d), BF16),
            pltpu.VMEM((1, 3 * dm.d), F32),
            pltpu.VMEM(shape, BF16),
        ]
        + piece_scratch(dm, (dm.pr, 3 * dm.d)),
        flops=2 * dm.t * dm.d * 3 * dm.d,
        moves=moves + [blocks],
        ids=ids,
    )
    return n1[0], blocks.result


def proj_body(dm, layer, *refs):
    nc = dm.nc
    meta, h, small, own, heads = refs[:5]
    pieces = refs[5 : 5 + nc]
    ob, mid, n2 = refs[5 + nc : 8 + nc]
    xr, bias, own_buf, piece_buf, sems = refs[8 + nc :]
    c, f = lax.axis_index("ctx"), lax.axis_index("fsdp")
    weight = Pieces(dm, layer, own, pieces, own_buf, piece_buf, sems, lambda j: (c ^ j) >= dm.nq)
    weight.start()
    tag = str(layer)
    bias[...] = small_vec(dm, small, "bp" + tag)
    put_heads(dm, ob, 0, [heads.at[j] for j in range(nc)], 0, c)
    relative(dm, f, ob, xr)
    weight.wait_own()
    for j in range(nc):
        i = c ^ j

        @pl.when(i >= dm.nq)
        def _():
            weight.copies[j].wait()
            at = pl.ds(mult((i - dm.nq) * dm.pc, dm.pc), dm.pc)
            acc = nn(xr[:, dm.pr :], weight.flat(j)) + nn(xr[:, : dm.pr], own_buf[:, at])
            mid[:, at] = h[:, at].astype(F32) + acc + bias[:, at]

    n2[...] = norm(
        mid[...], small_vec(dm, small, "g2" + tag), small_vec(dm, small, "s2" + tag)
    ).astype(BF16)


def proj_call(dm, layer, meta, h, small, own, heads, pieces, moves, ids):
    td = (dm.t, dm.d)
    return run(
        dm,
        functools.partial(proj_body, dm, layer),
        [(meta, "s"), (h, "v"), (small, "v"), (own, "a"), (heads, "v")] + [(p, "a") for p in pieces],
        [sds(td, BF16), sds(td, F32), sds(td, BF16)],
        [pltpu.VMEM(td, BF16), pltpu.VMEM((1, dm.d), F32)] + piece_scratch(dm, (dm.pr, dm.d)),
        flops=2 * dm.t * dm.d * dm.d,
        moves=moves,
        ids=ids,
    )


def fc_body(dm, layer, *refs):
    nc = dm.nc
    meta, n2, small, own = refs[:4]
    pieces = refs[4 : 4 + nc]
    u, act = refs[4 + nc : 6 + nc]
    xr, bias, own_buf, piece_buf, sems = refs[6 + nc :]
    c, f = lax.axis_index("ctx"), lax.axis_index("fsdp")
    weight = Pieces(dm, layer, own, pieces, own_buf, piece_buf, sems, None)
    weight.start()
    bias[...] = small_vec(dm, small, "bf" + str(layer))
    relative(dm, f, n2, xr)
    weight.wait_own()
    for j in range(nc):
        i = c ^ j
        weight.copies[j].wait()
        at = pl.ds(mult(i * dm.pc, dm.pc), dm.pc)
        acc = nn(xr[:, dm.pr :], weight.flat(j)) + nn(xr[:, : dm.pr], own_buf[:, at])
        acc = acc + bias[:, at]
        u[:, at] = acc
        act[:, at] = gelu(acc).astype(BF16)


def fc_call(dm, layer, meta, n2, small, own, pieces, moves, ids):
    return run(
        dm,
        functools.partial(fc_body, dm, layer),
        [(meta, "s"), (n2, "v"), (small, "v"), (own, "a")] + [(p, "a") for p in pieces],
        [sds((dm.t, dm.ff), F32), sds((dm.t, dm.ff), BF16)],
        [pltpu.VMEM((dm.t, dm.d), BF16), pltpu.VMEM((1, dm.ff), F32)] + piece_scratch(dm, (dm.pr, dm.ff)),
        flops=2 * dm.t * dm.d * dm.ff,
        moves=moves,
        ids=ids,
    )


def out_body(dm, layer, *refs):
    nc = dm.nc
    meta, mid, act, small, own = refs[:5]
    pieces = refs[5 : 5 + nc]
    h = refs[5 + nc]
    own_buf, piece_buf, sems = refs[6 + nc :]
    c, f = lax.axis_index("ctx"), lax.axis_index("fsdp")
    weight = Pieces(dm, layer, own, pieces, own_buf, piece_buf, sems, None)
    weight.start()
    weight.wait_own()
    mine = act[:, pl.ds(mult(f * dm.ffn, dm.ffn), dm.ffn)]
    h[...] = mid[...] + nn(mine, own_buf[...]) + small_vec(dm, small, "bo" + str(layer))
    for col in range(dm.ncs):
        acc = None
        for j in range(col, nc, dm.ncs):
            i = c ^ j
            weight.copies[j].wait()
            for s in range(1, dm.nf):
                at = mult(ring(dm, f, s) * dm.ffn + (i // dm.ncs) * dm.pr, dm.pr)
                part = nn(act[:, pl.ds(at, dm.pr)], piece_buf[j, s - 1])
                acc = part if acc is None else acc + part
        at = pl.ds(mult((lax.rem(c, dm.ncs) ^ col) * dm.pc, dm.pc), dm.pc)
        h[:, at] = h[:, at] + acc


def out_call(dm, layer, meta, mid, act, small, own, pieces, moves, ids):
    return run(
        dm,
        functools.partial(out_body, dm, layer),
        [(meta, "s"), (mid, "v"), (act, "v"), (small, "v"), (own, "a")] + [(p, "a") for p in pieces],
        [sds((dm.t, dm.d), F32)],
        piece_scratch(dm, (dm.ffn, dm.d)),
        flops=2 * dm.t * dm.d * dm.ff,
        moves=moves,
        ids=ids,
    )[0]


def chosen(dm, which, take):
    out = take(0).astype(F32)
    pick = jnp.full(out.shape, which, jnp.int32)
    for k in range(1, dm.nc):
        out = jnp.where(pick == k, take(k).astype(F32), out)
    return out.astype(BF16)


def sort_rows(dm, meta, blocks, dst):
    for piece in range(2 * dm.nc):
        slot = meta[4 + dm.nc + min(piece, 2 * dm.nc - 1 - piece)]
        half = 0 if piece < dm.nc else dm.half
        dst[piece * dm.half : (piece + 1) * dm.half, :] = chosen(
            dm, slot, lambda j: blocks[j, half : half + dm.half, :]
        )


def unsort_rows(dm, meta, src, blocks, at):
    cols = slice(at, at + src.shape[1])

    def rows(piece):
        return src[piece * dm.half : (piece + 1) * dm.half, :]

    for j in range(dm.nc):
        low = meta[4 + j]
        blocks[j, : dm.half, cols] = chosen(dm, low, rows)
        blocks[j, dm.half :, cols] = chosen(dm, low, lambda k: rows(2 * dm.nc - 1 - k))


def stack_heads(dm, v, scale=None):
    if scale is not None:
        v = v * scale
    if dm.hl == 1:
        return v
    lane = lax.broadcasted_iota(jnp.int32, v.shape, 1) // HEAD_DIM
    return jnp.concatenate([jnp.where(lane == k, v, 0.0).astype(v.dtype) for k in range(dm.hl)], axis=0)


def pick_heads(dm, v):
    if dm.hl == 1:
        return v
    rows = v.shape[0] // dm.hl
    lane = lax.broadcasted_iota(jnp.int32, (rows, v.shape[1]), 1) // HEAD_DIM
    out = v[:rows]
    for k in range(1, dm.hl):
        out = jnp.where(lane == k, v[k * rows : (k + 1) * rows], out)
    return out


def doc_start(first_cut, second_cut, row):
    return jnp.where(row < first_cut, 0, jnp.where(row < second_cut, first_cut, second_cut))


def tile_rows(dm, t, tq, cuts):
    row = t * tq + lax.rem(lax.broadcasted_iota(jnp.int32, (dm.hl * tq, 1), 0), tq)
    return row, doc_start(cuts[0], cuts[1], row)


TQ = 256
TK = 256


def attend_body(dm, *refs):
    nc, w = dm.nc, dm.w
    meta, blocks, packed, lse, mixed, heads = refs
    cuts = (meta[2], meta[3])
    tq, tk = min(TQ, dm.rows), min(TK, dm.rows)
    sort_rows(dm, meta, blocks, packed)

    def tile(t, carry):
        here = pl.ds(mult(t * tq, tq), tq)
        q = stack_heads(dm, packed[here, :w], HEAD_DIM**-0.5)
        row, start = tile_rows(dm, t, tq, cuts)

        def chunk(kb, state):
            top, mass, acc = state
            there = pl.ds(mult(kb * tk, tk), tk)
            col = kb * tk + lax.broadcasted_iota(jnp.int32, (1, tk), 1)
            s = jnp.where((col <= row) & (col >= start), nt(q, packed[there, w : 2 * w]), NEG)
            new_top = jnp.maximum(top, jnp.max(s, axis=1, keepdims=True))
            p = jnp.exp(s - new_top)
            fade = jnp.exp(top - new_top)
            mass = mass * fade + jnp.sum(p, axis=1, keepdims=True)
            acc = acc * fade + nn(p.astype(BF16), packed[there, 2 * w :])
            return new_top, mass, acc

        initial = (
            jnp.full((dm.hl * tq, 1), LOW, F32),
            jnp.zeros((dm.hl * tq, 1), F32),
            jnp.zeros((dm.hl * tq, w), F32),
        )
        top, mass, acc = lax.fori_loop(0, ((t + 1) * tq + tk - 1) // tk, chunk, initial)
        mixed[here, :] = pick_heads(dm, acc * (1.0 / mass))
        norms = top + jnp.log(mass)
        for k in range(dm.hl):
            lse[k, here, :] = norms[k * tq : (k + 1) * tq]
        return carry

    lax.fori_loop(0, dm.rows // tq, tile, 0)
    unsort_rows(dm, meta, mixed, heads, 0)


def attend_call(dm, meta, blocks, moves, ids):
    shape = (dm.nc, dm.t, dm.w)
    heads = send_blocks(dm, 5, shape)
    saved = run(
        dm,
        functools.partial(attend_body, dm),
        [(meta, "s"), (blocks, "v")],
        [sds((dm.rows, 3 * dm.w), BF16), sds((dm.hl, dm.rows, 1), F32), sds((dm.rows, dm.w), F32)],
        [pltpu.VMEM(shape, BF16)],
        flops=8 * dm.rows * dm.rows * dm.w,
        moves=moves + [heads],
        ids=ids,
    )
    return saved, heads.result


def attend_back_body(dm, *refs):
    nc, w = dm.nc, dm.w
    meta, packed, lse, mixed, grads, blocks, dmix, dq, dk, dv = refs
    cuts = (meta[2], meta[3])
    tq, tk = min(TQ, dm.rows), min(TK, dm.rows)
    scale = HEAD_DIM**-0.5
    sort_rows(dm, meta, grads, dmix)
    dk[...] = jnp.zeros_like(dk)
    dv[...] = jnp.zeros_like(dv)

    def tile(t, carry):
        here = pl.ds(mult(t * tq, tq), tq)
        q = stack_heads(dm, packed[here, :w], scale)
        do = stack_heads(dm, dmix[here, :])
        o = jnp.concatenate([mixed[here, :]] * dm.hl, axis=0)
        delta = jnp.sum(do.astype(F32) * o, axis=1, keepdims=True)
        norms = jnp.concatenate([lse[k, here, :] for k in range(dm.hl)], axis=0)
        row, start = tile_rows(dm, t, tq, cuts)

        def chunk(kb, acc):
            there = pl.ds(mult(kb * tk, tk), tk)
            col = kb * tk + lax.broadcasted_iota(jnp.int32, (1, tk), 1)
            keys = packed[there, w : 2 * w]
            s = jnp.where((col <= row) & (col >= start), nt(q, keys), NEG)
            p = jnp.exp(s - norms)
            dp = nt(do, packed[there, 2 * w :])
            ds = (p * (dp - delta)).astype(BF16)
            dv[there, :] += tn(p.astype(BF16), do)
            dk[there, :] += tn(ds, q)
            return acc + nn(ds, keys)

        acc = lax.fori_loop(
            0, ((t + 1) * tq + tk - 1) // tk, chunk, jnp.zeros((dm.hl * tq, w), F32)
        )
        dq[here, :] = pick_heads(dm, acc) * scale
        return carry

    lax.fori_loop(0, dm.rows // tq, tile, 0)
    for at, src in enumerate((dq, dk, dv)):
        unsort_rows(dm, meta, src, blocks, at * w)


def attend_back_call(dm, meta, saved, grads, moves, ids):
    shape = (dm.nc, dm.t, 3 * dm.w)
    blocks = send_blocks(dm, 5, shape)
    run(
        dm,
        functools.partial(attend_back_body, dm),
        [(meta, "s")] + [(a, "v") for a in saved] + [(grads, "v")],
        [],
        [pltpu.VMEM(shape, BF16), pltpu.VMEM((dm.rows, dm.w), BF16)]
        + [pltpu.VMEM((dm.rows, dm.w), F32)] * 3,
        flops=16 * dm.rows * dm.rows * dm.w,
        moves=moves + [blocks],
        ids=ids,
    )
    return blocks.result


def top_body(dm, h, cot, small, result, dh, low, g_gain, g_shift):
    gain = small_vec(dm, small, "gf")
    v = h[...]
    result[...] = norm(v, gain, small_vec(dm, small, "sf")).astype(BF16)
    dv, g_gain[...], g_shift[...] = norm_back(v, gain, cot[...].astype(F32))
    dh[...] = dv
    low[...] = dv.astype(BF16)


def top_call(dm, h, cot, small):
    td, vec = (dm.t, dm.d), sds((1, dm.d), F32)
    return run(
        dm,
        functools.partial(top_body, dm),
        [(h, "v"), (cot, "v"), (small, "v")],
        [sds(td, BF16), sds(td, F32), sds(td, BF16), vec, vec],
        [],
        flops=20 * dm.t * dm.d,
    )


def out_back_body(dm, layer, *refs):
    nc = dm.nc
    meta, gm, u, own = refs[:4]
    pieces = refs[4 : 4 + nc]
    du, sum_gm, sum_du = refs[4 + nc : 7 + nc]
    gr, own_buf, piece_buf, sems = refs[7 + nc :]
    c, f = lax.axis_index("ctx"), lax.axis_index("fsdp")
    weight = Pieces(dm, layer, own, pieces, own_buf, piece_buf, sems, None)
    weight.start()
    sum_gm[...] = col_sum(gm[...])
    for col in range(dm.ncs):
        at = mult((lax.rem(c, dm.ncs) ^ col) * dm.pc, dm.pc)
        gr[:, col * dm.pc : (col + 1) * dm.pc] = gm[:, pl.ds(at, dm.pc)]

    def finish(dact, at):
        at = pl.ds(mult(at, dm.pr), dm.pr)
        low = (dact * gelu_slope(u[:, at])).astype(BF16)
        du[:, at] = low
        sum_du[:, at] = col_sum(low)

    weight.wait_own()
    for g in range(nc // dm.ncs):
        finish(nt(gm[...], own_buf[g * dm.pr : (g + 1) * dm.pr, :]), f * dm.ffn + g * dm.pr)
    for g in range(nc // dm.ncs):
        for col in range(dm.ncs):
            weight.copies[g * dm.ncs + col].wait()
        for s in range(1, dm.nf):
            dact = None
            for col in range(dm.ncs):
                part = nt(gr[:, col * dm.pc : (col + 1) * dm.pc], piece_buf[g * dm.ncs + col, s - 1])
                dact = part if dact is None else dact + part
            finish(dact, ring(dm, f, s) * dm.ffn + ((c // dm.ncs) ^ g) * dm.pr)


def out_back_call(dm, layer, meta, gm, u, own, pieces, moves, ids):
    return run(
        dm,
        functools.partial(out_back_body, dm, layer),
        [(meta, "s"), (gm, "v"), (u, "v"), (own, "a")] + [(p, "a") for p in pieces],
        [sds((dm.t, dm.ff), BF16), sds((1, dm.d), F32), sds((1, dm.ff), F32)],
        [pltpu.VMEM((dm.t, dm.d), BF16)] + piece_scratch(dm, (dm.ffn, dm.d)),
        flops=2 * dm.t * dm.d * dm.ff,
        moves=moves,
        ids=ids,
    )


def cols_back(dm, f, c, weight, dy, first, last, acc, out):
    weight.wait_own()
    acc[:, : dm.pr] = nt(dy[...], weight.own[...])
    acc[:, dm.pr :] = jnp.zeros((dm.t, dm.d - dm.pr), F32)
    for j in range(dm.nc):
        i = c ^ j

        def step():
            weight.copies[j].wait()
            at = pl.ds(mult((i - first) * dm.pc, dm.pc), dm.pc)
            acc[:, dm.pr :] += nt(dy[:, at], weight.flat(j))

        weight.each(j, step)
    for s in range(dm.nf):
        at = mult(ring(dm, f, s) * dm.pr, dm.pr)
        out[:, pl.ds(at, dm.pr)] = acc[:, s * dm.pr : (s + 1) * dm.pr].astype(out.dtype)


def fc_back_body(dm, layer, *refs):
    nc = dm.nc
    meta, du, dh, mid, small, own = refs[:6]
    pieces = refs[6 : 6 + nc]
    dmid, ga, sum_ga, g_gain, g_shift = refs[6 + nc : 11 + nc]
    acc, dn, own_buf, piece_buf, sems = refs[11 + nc :]
    c, f = lax.axis_index("ctx"), lax.axis_index("fsdp")
    weight = Pieces(dm, layer, own, pieces, own_buf, piece_buf, sems, None)
    weight.start()
    cols_back(dm, f, c, weight, du, 0, nc, acc, dn)
    dv, g_gain[...], g_shift[...] = norm_back(
        mid[...], small_vec(dm, small, "g2" + str(layer)), dn[...]
    )
    total = dh[...] + dv
    dmid[...] = total
    low = total.astype(BF16)
    ga[...] = low
    sum_ga[...] = col_sum(low)


def fc_back_call(dm, layer, meta, du, dh, mid, small, own, pieces, moves, ids):
    td, vec = (dm.t, dm.d), sds((1, dm.d), F32)
    return run(
        dm,
        functools.partial(fc_back_body, dm, layer),
        [(meta, "s"), (du, "v"), (dh, "v"), (mid, "v"), (small, "v"), (own, "a")]
        + [(p, "a") for p in pieces],
        [sds(td, F32), sds(td, BF16), vec, vec, vec],
        [pltpu.VMEM(td, F32), pltpu.VMEM(td, F32)] + piece_scratch(dm, (dm.pr, dm.ff)),
        flops=2 * dm.t * dm.d * dm.ff,
        moves=moves,
        ids=ids,
    )


def proj_back_body(dm, layer, *refs):
    nc = dm.nc
    meta, ga, own = refs[:3]
    pieces = refs[3 : 3 + nc]
    acc, dob, blocks, own_buf, piece_buf, sems = refs[3 + nc :]
    c, f = lax.axis_index("ctx"), lax.axis_index("fsdp")
    weight = Pieces(dm, layer, own, pieces, own_buf, piece_buf, sems, lambda j: (c ^ j) >= dm.nq)
    weight.start()
    cols_back(dm, f, c, weight, ga, dm.nq, nc, acc, dob)
    for j in range(nc):
        blocks[j] = take_heads(dm, dob, 0, c ^ j)


def proj_back_call(dm, layer, meta, ga, own, pieces, moves, ids):
    td, shape = (dm.t, dm.d), (dm.nc, dm.t, dm.w)
    blocks = send_blocks(dm, 5 + dm.nc, shape)
    run(
        dm,
        functools.partial(proj_back_body, dm, layer),
        [(meta, "s"), (ga, "v"), (own, "a")] + [(p, "a") for p in pieces],
        [],
        [pltpu.VMEM(td, F32), pltpu.VMEM(td, BF16), pltpu.VMEM(shape, BF16)]
        + piece_scratch(dm, (dm.pr, dm.d)),
        flops=2 * dm.t * dm.d * dm.d,
        moves=moves + [blocks],
        ids=ids,
    )
    return blocks.result


def qkv_back_body(dm, layer, *refs):
    nc = dm.nc
    meta, dmid, h, small, own, blocks = refs[:6]
    pieces = refs[6 : 6 + nc]
    dh, low, dqkv, sum_dqkv, g_gain, g_shift = refs[6 + nc : 12 + nc]
    acc, dn, own_buf, piece_buf, sems = refs[12 + nc :]
    blocks = [blocks.at[j] for j in range(nc)]
    c, f = lax.axis_index("ctx"), lax.axis_index("fsdp")
    weight = Pieces(dm, layer, own, pieces, own_buf, piece_buf, sems, lambda j: (c ^ j) < dm.nq)
    weight.start()
    for third in range(3):
        put_heads(dm, dqkv, third * dm.d, blocks, third * dm.w, c)
    sum_dqkv[...] = col_sum(dqkv[...])
    cols_back(dm, f, c, weight, dqkv, 0, dm.nq, acc, dn)
    dv, g_gain[...], g_shift[...] = norm_back(
        h[...].astype(F32), small_vec(dm, small, "g1" + str(layer)), dn[...]
    )
    total = dmid[...] + dv
    dh[...] = total
    low[...] = total.astype(BF16)


def qkv_back_call(dm, layer, meta, dmid, h, small, own, blocks, pieces, moves, ids):
    td, vec = (dm.t, dm.d), sds((1, dm.d), F32)
    return run(
        dm,
        functools.partial(qkv_back_body, dm, layer),
        [(meta, "s"), (dmid, "v"), (h, "v"), (small, "v"), (own, "a"), (blocks, "v")]
        + [(p, "a") for p in pieces],
        [sds(td, F32), sds(td, BF16), sds((dm.t, 3 * dm.d), BF16), sds((1, 3 * dm.d), F32), vec, vec],
        [pltpu.VMEM(td, F32), pltpu.VMEM(td, F32)] + piece_scratch(dm, (dm.pr, 3 * dm.d)),
        flops=2 * dm.t * dm.d * 3 * dm.d,
        moves=moves,
        ids=ids,
    )


def grad_body(dm, kind, meta, *refs):
    c, f = lax.axis_index("ctx"), lax.axis_index("fsdp")
    step = pl.program_id(0)
    if kind == "attn":
        n1, ob, dqkv, ga, keep, send, xt = refs
    else:
        x, y, keep, send, xt = refs

    @pl.when(step == 0)
    def _():
        if kind == "attn":
            xt[: dm.d, :] = n1[...].T
            xt[dm.d :, :] = ob[...].T
        else:
            xt[...] = x[...].T

    for odd, dst in enumerate((keep, send)):
        i = c ^ (2 * step + odd)

        def fill(row_base, row_step, dy):
            for s in range(dm.nf):
                at = mult(row_base + ring(dm, f, s) * row_step, dm.pr)
                dst[0, s] = nn(xt[pl.ds(at, dm.pr), :], dy).astype(BF16)

        if kind == "attn":

            @pl.when(i < dm.nq)
            def _():
                fill(0, dm.pr, dqkv[:, pl.ds(mult(i * dm.pc, dm.pc), dm.pc)])

            @pl.when(i >= dm.nq)
            def _():
                fill(dm.d, dm.pr, ga[:, pl.ds(mult((i - dm.nq) * dm.pc, dm.pc), dm.pc)])

        elif kind == "fc":
            fill(0, dm.pr, y[:, pl.ds(mult(i * dm.pc, dm.pc), dm.pc)])
        else:
            dy = y[:, pl.ds(mult(lax.rem(i, dm.ncs) * dm.pc, dm.pc), dm.pc)]
            fill((i // dm.ncs) * dm.pr, dm.ffn, dy)


def grad_call(dm, kind, meta, *arrays):
    depth = {"attn": 2 * dm.d, "fc": dm.d, "out": dm.ff}[kind]
    steps = dm.nc // 2
    block = (1, dm.nf, dm.pr, dm.pc)
    out = sds((steps,) + block[1:], BF16)
    return run(
        dm,
        functools.partial(grad_body, dm, kind),
        [(meta, "s")] + [(a, "v") for a in arrays],
        [out, out],
        [pltpu.VMEM((depth, dm.t), BF16)],
        flops=2 * dm.t * dm.d * dm.ff,
        grid=(steps,),
        in_specs=[pl.BlockSpec(memory_space=pltpu.SMEM)]
        + [pl.BlockSpec(a.shape, lambda k: (0, 0)) for a in arrays],
        out_specs=[pl.BlockSpec(block, lambda k: (k, 0, 0, 0))] * 2,
    )


def place_body(dm, kind, layer, old, *refs):
    nc = dm.nc
    meta = refs[0]
    pieces = refs[1 : 1 + nc]
    rest = refs[1 + nc + old :]
    count = 2 if kind == "attn" else 1
    outs, buf, sems = rest[:count], rest[count], rest[count + 1]
    c = lax.axis_index("ctx")
    for j in range(nc):
        i = c ^ j
        if kind == "out":
            rows = pl.ds(mult((i // dm.ncs) * dm.pr, dm.pr), dm.pr)
            cols = pl.ds(mult(lax.rem(i, dm.ncs) * dm.pc, dm.pc), dm.pc)
            buf[rows, cols] = pieces[j][...].astype(F32)
        else:
            buf[:, pl.ds(mult(i * dm.pc, dm.pc), dm.pc)] = pieces[j][...].astype(F32)
    if kind == "attn":
        copies = [
            pltpu.make_async_copy(buf.at[:, pl.ds(0, 3 * dm.d)], outs[0].at[layer], sems.at[0]),
            pltpu.make_async_copy(buf.at[:, pl.ds(3 * dm.d, dm.d)], outs[1].at[layer], sems.at[1]),
        ]
    else:
        copies = [pltpu.make_async_copy(buf, outs[0].at[layer], sems.at[0])]
    for copy in copies:
        copy.start()
    for copy in copies:
        copy.wait()


def place_call(dm, kind, layer, meta, pieces, old):
    shapes = {
        "attn": [(LAYERS, dm.pr, 3 * dm.d), (LAYERS, dm.pr, dm.d)],
        "fc": [(LAYERS, dm.pr, dm.ff)],
        "out": [(LAYERS, dm.ffn, dm.d)],
    }[kind]
    buf = {"attn": (dm.pr, dm.ff), "fc": (dm.pr, dm.ff), "out": (dm.ffn, dm.d)}[kind]
    return run(
        dm,
        functools.partial(place_body, dm, kind, layer, len(old)),
        [(meta, "s")] + [(p, "v") for p in pieces] + [(o, "a") for o in old],
        [sds(s, F32) for s in shapes],
        [pltpu.VMEM(buf, F32), pltpu.SemaphoreType.DMA((2,))],
        flops=0,
        out_specs=[pl.BlockSpec(memory_space=pl.ANY)] * len(shapes),
        alias={1 + dm.nc + k: k for k in range(len(old))},
    )


def plane_bits(nc):
    bits = []
    bit = 2
    while bit < nc:
        bits.append(bit)
        bit *= 2
    return bits


def value(v):
    return v.result if isinstance(v, Move) else v


def spread(dm, first):
    bits = plane_bits(dm.nc)
    held = {0: first}
    if len(bits) == 2:
        one, two = bits
        held.update({bit: whole(first, ("ctx", bit)) for bit in (one, two, 1)})
        yield [held[one], held[two], held[1]]
        lead = (slice(None),) * (len(first.shape) - 2)
        cut = first.shape[-2] // 2
        low, high = lead + (pl.ds(0, cut),), lead + (pl.ds(cut, cut),)
        far = Move(
            first.shape, first.dtype,
            [([(None, held[two], low)], ("ctx", one), low), ([(None, held[one], high)], ("ctx", two), high)],
        )
        held[one ^ two] = far
        held.update({bit ^ 1: whole(held[bit], ("ctx", 1)) for bit in bits})
        yield [far, held[one ^ 1], held[two ^ 1]]
        held[one ^ two ^ 1] = whole(far, ("ctx", 1))
        yield [held[one ^ two ^ 1]]
    else:
        for bit in bits + [1]:
            new = {j ^ bit: whole(v, ("ctx", bit)) for j, v in held.items()}
            yield list(new.values())
            held.update(new)
    return [held[j] for j in range(dm.nc)]


def gather(dm, source):
    others = Move(
        (dm.nf - 1, dm.pr, dm.pc), BF16,
        [(source, ("fsdp", s), (s - 1,)) for s in range(1, dm.nf)],
    )
    yield [others]
    return (yield from spread(dm, others))


def plane_sum(dm, keep, send):
    bits = plane_bits(dm.nc)
    other = whole(send, ("ctx", 1))
    yield [other]
    other = value(other)
    if len(bits) == 2:
        one, two = bits
        cut = dm.pr // 2
        low, high = slice(0, cut), slice(cut, dm.pr)

        def part(t, rows, *more):
            v = keep[t, :, rows].astype(F32) + other[t, :, rows].astype(F32)
            for m in more:
                v = v + value(m).astype(F32)
            return v

        def moved(v, bit):
            return whole(v.astype(BF16), ("ctx", bit))

        far_x, own_x = moved(part(3, low), one), moved(part(1, low), one)
        far_y, own_y = moved(part(3, high), two), moved(part(2, high), two)
        yield [far_x, own_x, far_y, own_y]
        x, y = moved(part(1, high, far_y), one), moved(part(2, low, far_x), two)
        yield [x, y]
        return jnp.concatenate([part(0, low, own_x, y), part(0, high, x, own_y)], axis=1)
    total = (keep.astype(F32) + other.astype(F32)).reshape((2,) * len(bits) + keep.shape[1:])
    for bit in reversed(bits):
        away = whole(total[1].astype(BF16), ("ctx", bit))
        yield [away]
        total = total[0] + value(away).astype(F32)
    return total


def reduce(dm, keep, send):
    total = (yield from plane_sum(dm, keep, send)).astype(BF16)
    others = Move(
        (dm.nf - 1,) + total.shape[1:], BF16,
        [([(None, total, (s,))], ("fsdp", dm.nf - s), (s - 1,)) for s in range(1, dm.nf)],
    )
    yield [others]
    mine = total[0].astype(F32)
    for s in range(1, dm.nf):
        mine = mine + value(others)[s - 1].astype(F32)
    return (yield from spread(dm, mine.astype(BF16)))


def reduce_small(dm, rows, f):
    n = rows.shape[1]
    total = rows.reshape(dm.nf, n // 128, 128)
    bit = 1
    while bit < dm.nc:
        other = whole(total, ("ctx", bit))
        yield [other]
        total = total + value(other)
        bit *= 2
    double = jnp.concatenate([total, total])
    turned = lax.dynamic_slice_in_dim(double, f, dm.nf)
    others = Move(
        (dm.nf - 1,) + total.shape[1:], F32,
        [([(None, turned, (dm.nf - s,))], ("fsdp", dm.nf - s), (s - 1,)) for s in range(1, dm.nf)],
    )
    yield [others]
    return (turned[0] + jnp.sum(value(others), axis=0)).reshape(n)


class Flow:
    def __init__(self, dm):
        self.dm, self.live, self.done = dm, {}, {}
        self.ids = itertools.count()

    def add(self, name, transfer):
        self.live[name] = transfer

    def take(self, *names):
        moves = []
        for name in names:
            if name in self.live:
                try:
                    moves += next(self.live[name])
                except StopIteration as stop:
                    self.done[name] = [value(v) for v in stop.value]
                    del self.live[name]
        return moves

    def move(self, *names):
        moves = self.take(*names)
        if moves:
            run(self.dm, None, [], [], [], 0, moves=moves, ids=self.ids)

    def finish(self, name):
        while name in self.live:
            self.move(name)
        return self.done[name]


def local(acts, cotangent, pair_slots, segments, *tensors):
    (
        attn_gain, attn_shift, qkv_weight, qkv_bias, proj_weight, proj_bias, mlp_gain, mlp_shift,
        fc_weight, fc_bias, out_weight, out_bias, final_gain, final_shift,
    ) = tensors
    nf, nc = lax.axis_size("fsdp"), lax.axis_size("ctx")
    dm = dims_of(acts, fc_weight, nf, nc)
    c, f = lax.axis_index("ctx"), lax.axis_index("fsdp")
    offsets, small_size = small_offsets(dm)

    seg = segments[0]
    cut_one = jnp.sum((seg == 0).astype(jnp.int32))
    cut_two = cut_one + jnp.sum((seg == 1).astype(jnp.int32))
    index = jnp.arange(nc, dtype=jnp.int32)
    others = jnp.bitwise_xor(c, index)
    lows = jnp.sum(jnp.where(others[:, None] == index[None, :], pair_slots[None, :], 0), axis=1)
    slots = jnp.sum(jnp.where(lows[None, :] == index[:, None], index[None, :], 0), axis=1)
    meta = jnp.concatenate([jnp.stack([c, f, cut_one, cut_two]).astype(jnp.int32), lows, slots])

    def source(kind, layer):
        def cols(first, last):
            at = jnp.clip(lax.axis_index("ctx"), first, last - 1) - first
            return (layer, pl.ds(0, dm.pr), pl.ds(mult(at * dm.pc, dm.pc), dm.pc))

        def place():
            at = lax.axis_index("ctx")
            row, col = (at // dm.ncs) * dm.pr, lax.rem(at, dm.ncs) * dm.pc
            return (layer, pl.ds(mult(row, dm.pr), dm.pr), pl.ds(mult(col, dm.pc), dm.pc))

        if kind == "attn":
            return [
                (lambda: lax.axis_index("ctx") < dm.nq, qkv_weight, lambda: cols(0, dm.nq)),
                (lambda: lax.axis_index("ctx") >= dm.nq, proj_weight, lambda: cols(dm.nq, nc)),
            ]
        if kind == "fc":
            return [(None, fc_weight, lambda: cols(0, nc))]
        return [(None, out_weight, place)]

    per_layer = (attn_gain, attn_shift, qkv_bias, proj_bias, mlp_gain, mlp_shift, fc_bias, out_bias)
    parts = [p[layer] for layer in range(LAYERS) for p in per_layer] + [final_gain, final_shift]
    packed = jnp.concatenate(parts).reshape(small_size // 128, 128)
    small_move = Move(
        (nf - 1,) + packed.shape, BF16,
        [([(None, packed, None)], ("fsdp", s), (s - 1,)) for s in range(1, nf)],
    )

    flow = Flow(dm)
    ids = flow.ids
    for layer in range(LAYERS):
        for kind, name in (("attn", "A"), ("fc", "C"), ("out", "O")):
            flow.add(name + str(layer), gather(dm, source(kind, layer)))
    moves = [small_move] + flow.take("A0") + flow.take("A0", "C0") + flow.take("A0", "C0", "O0")
    while "A0" in flow.live:
        extra = []
        try:
            extra = next(flow.live["A0"])
        except StopIteration as stop:
            flow.done["A0"] = stop.value
            del flow.live["A0"]
        moves += extra
    run(dm, None, [], [], [], 0, moves=moves, ids=ids)
    flow.done["A0"] = [value(v) for v in flow.done["A0"]]
    backwards = jnp.concatenate([packed[None], value(small_move)])[::-1]
    small = lax.dynamic_slice_in_dim(jnp.concatenate([backwards, backwards]), nf - 1 - f, nf)
    small = small.reshape(nf, small_size).astype(F32)

    h = acts[0]
    kept = []
    plan = (
        (("O0",), ("C0", "O0", "A1"), ("C0", "O0", "A1", "C1"), ("A1",), ("A1", "C1", "O1")),
        (("C1",), ("O1",), ("C1", "O1"), ("O1",), ()),
    )
    for layer in range(LAYERS):
        tag = str(layer)
        beside = plan[layer]
        attn = flow.finish("A" + tag)
        n1, blocks = qkv_call(dm, layer, meta, h, small, qkv_weight, attn, flow.take(*beside[0]), ids)
        saved, heads = attend_call(dm, meta, blocks, flow.take(*beside[1]), ids)
        ob, mid, n2 = proj_call(
            dm, layer, meta, h, small, proj_weight, heads, attn, flow.take(*beside[2]), ids
        )
        fc = flow.finish("C" + tag)
        u, act = fc_call(dm, layer, meta, n2, small, fc_weight, fc, flow.take(*beside[3]), ids)
        kept.append((h, n1, saved, ob, mid, n2, u, act))
        out = flow.finish("O" + tag)
        h = out_call(dm, layer, meta, mid, act, small, out_weight, out, flow.take(*beside[4]), ids)

    weights = flow.done
    vectors = {}
    result, dh, gm, vectors["gf"], vectors["sf"] = top_call(dm, h, cotangent[0], small)
    placed = {"attn": [], "fc": [], "out": []}

    def start(name, kind, *arrays):
        keep, send = grad_call(dm, kind, meta, *arrays)
        flow.add(name, reduce(dm, keep, send))

    def place(name, kind, layer):
        placed[kind] = place_call(dm, kind, layer, meta, flow.finish(name), placed[kind])

    for layer in reversed(range(LAYERS)):
        tag, nxt = str(layer), str(layer + 1)
        o_, a_, k_ = "o" + nxt, "a" + nxt, "c" + nxt
        o, a, k = "o" + tag, "a" + tag, "c" + tag
        h, n1, saved, ob, mid, n2, u, act = kept[layer]
        du, vectors["bo" + tag], vectors["bf" + tag] = out_back_call(
            dm, layer, meta, gm, u, out_weight, weights["O" + tag], flow.take(a_, k_, o_), ids
        )
        start(o, "out", act, gm)
        dmid, ga, vectors["bp" + tag], vectors["g2" + tag], vectors["s2" + tag] = fc_back_call(
            dm, layer, meta, du, dh, mid, small, fc_weight, weights["C" + tag], flow.take(o, a_, k_, o_), ids
        )
        start(k, "fc", n2, du)
        grads = proj_back_call(
            dm, layer, meta, ga, proj_weight, weights["A" + tag], flow.take(k, o, a_, k_, o_), ids
        )
        blocks = attend_back_call(dm, meta, saved, grads, flow.take(k, o, a_, k_), ids)
        dh, gm, dqkv, vectors["bq" + tag], vectors["g1" + tag], vectors["s1" + tag] = qkv_back_call(
            dm, layer, meta, dmid, h, small, qkv_weight, blocks, weights["A" + tag],
            flow.take(o, k, a_), ids,
        )
        start(a, "attn", n1, ob, dqkv, ga)

    names = [name + str(layer) for layer in range(LAYERS) for name, _ in SMALL] + ["gf", "sf"]
    rows = jnp.concatenate([vectors[name].reshape(nf, -1) for name in names], axis=1)
    small_sum = reduce_small(dm, rows, f)

    def listed(transfer):
        return [(yield from transfer)]

    flow.add("small", listed(small_sum))
    while flow.live:
        flow.move(*list(flow.live))
    for layer in reversed(range(LAYERS)):
        tag = str(layer)
        place("o" + tag, "out", layer)
        place("c" + tag, "fc", layer)
        place("a" + tag, "attn", layer)
    mine = flow.finish("small")[0]

    def vec(name):
        at, size = offsets[name]
        return mine[at : at + size]

    def both(name):
        return jnp.stack([vec(name + str(layer)) for layer in range(LAYERS)])

    return (
        result[None], gm[None], both("g1"), both("s1"), placed["attn"][0], both("bq"),
        placed["attn"][1], both("bp"), both("g2"), both("s2"), placed["fc"][0], both("bf"),
        placed["out"][0], both("bo"), vec("gf"), vec("sf"),
    )


def solution(mesh):
    row = P("fsdp", "ctx", None)
    vec, mat = P(None, "fsdp"), P(None, "fsdp", None)
    tensors = (vec, vec, mat, vec, mat, vec, vec, vec, mat, vec, mat, vec, P("fsdp"), P("fsdp"))
    return jax.shard_map(
        local,
        mesh=mesh,
        in_specs=(row, row, P(), P("fsdp", None)) + tensors,
        out_specs=(row, row) + tensors,
        check_vma=False,
    )
```

time: 3870 us -> 990 us (0.26)
  waiting for transfers between devices: 2810 us -> 0 us
  Pallas kernels: 0 us -> 870 us
  matrix products: 372 us -> 0 us
  blocking collectives: 281 us -> 0 us
  local copies, waits for them, and re-layouts: 274 us -> 17 us
    reduce_scatter x12 -> x0, waiting for transfers between devices: 2030 us -> none  [the longest x2 726 us: reduce_layer(): lax.psum_scatter(mixed[10], ('ctx', 'fsdp'), scatter_dimension=0, tiled=T...]
    pallas_call x0 -> x41, Pallas kernels: none -> 870 us  [run(): pl.pallas_call(kernel, out_shape=outs, in_specs=specs, out_specs=out_spec...]
    all_gather x18 -> x0, waiting for transfers between devices: 778 us -> none  [the longest x2 283 us: fetch_layer(): lax.all_gather(shards[10], 'fsdp', axis=0, tiled=True)]
    dot_general x80 -> x0, matrix products: 372 us -> none  [the longest x16 69.8 us: block_scores(): jnp.einsum('thd,khd->htk', queries, key_blk, preferred_element_type=jnp.f...]
    all_gather x22 -> x0, blocking collectives: 216 us -> none  [the longest x2 28.6 us: fetch_layer(): lax.all_gather(shards[3], 'fsdp', axis=0, tiled=True)]
    unnamed x2 -> x0, blocking collectives: 64.5 us -> none
    convert_element_type x8 -> x0, local copies, waits for them, and re-layouts: 59.6 us -> none  [the longest x3 28.6 us: backward_layer(): grad_value_all.astype(jnp.bfloat16)]
    unnamed x292 -> x150, local copies, waits for them, and re-layouts: 66.5 us -> 7.3 us
  transfers between devices with their start and end apart: 30 -> 0, of which waited for: 24 -> 0; matrix products, arithmetic and copies ran while one was open for 11% -> 0% of each run, Pallas kernels for 0% -> 0%
where the time goes in v1:
time: 990 us; the launch traced here: 979 us
  Pallas kernels  870 us (88%)
  other arithmetic  89.4 us (9%)
  local copies, waits for them, and re-layouts  17 us (2%)
    pallas_call x41, Pallas kernels, run(): pl.pallas_call(kernel, out_shape=outs, in_specs=specs, out_specs=out_spec...  870 us
    convert_element_type x12, other arithmetic, moved(): return whole(v.astype(BF16), ('ctx', bit))  40.4 us

profile of v1, /device:TPU:0, one launch (start us, length us, event | category | flops | bytes accessed | tf_op | source)
XLA Modules:
  0.0 979.4 jit_solution(15300976729878589193)
XLA Ops:
  17.5 71.0 %shard_map.297 = (bf16[3,56,128]{2,1,0:T(8,128)(2,1)}, bf16[3,256,512]{2,1,0:T(8,128)(2,1)}, bf16[3,256,512]{2,1,0:T(8,128)(2,1)}, bf16[3,256,512]{2,1,0:T(8,128...) custom-call(bf16[56,128]{1,0:T(8,128)(2,1)} %bitcast.256, ...), custom_call_target="tpu_custom_call" | custom-call | tf_op jit(solution)/shard_map/pallas_call | solution.py:268
  90.0 39.8 %shard_map.298 = (bf16[256,1024]{1,0:T(8,128)(2,1)}, bf16[3,256,512]{2,1,0:T(8,128)(2,1)}, bf16[3,256,512]{2,1,0:T(8,128)(2,1)}, bf16[3,256,512]{2,1,0:T(8,128)(2,1)}, bf16[8,256,384]{2,1,0:T(8,128)(2,1)}) custom-call(s32[20]{0:T(128)} %concatenate.42.refs_0_.meta, bf16[256,1024]{1,0:T(8,128)(2,1)} %bitcast.248, f32[4,7168]{1,0:T(4,128)} %bitcast.235, ...), custom_call_target="tpu_custom_call" | custom-call | flops 1610612736 | bytes 10600528 | tf_op jit(solution)/shard_map/pallas_call | solution.py:268
  129.8 44.8 %shard_map.299 = (bf16[2048,384]{1,0:T(8,128)(2,1)}, f32[2,2048,1]{2,1,0:T(8,128)}, f32[2048,128]{1,0:T(8,128)}, bf16[3,256,512]{2,1,0:T(8,128)(2,1)}, bf16[3,25...) custom-call(s32[20]{0:T(128)} %concatenate.42.refs_0_.meta, ...), custom_call_target="tpu_custom_call" | custom-call | flops 4294967296 | bytes 4210768 | tf_op jit(solution)/shard_map/pallas_call | solution.py:268
  174.7 24.7 %shard_map.300 = (bf16[256,1024]{1,0:T(8,128)(2,1)}, f32[256,1024]{1,0:T(8,128)}, bf16[256,1024]{1,0:T(8,128)(2,1)}, bf16[3,256,512]{2,1,0:T(8,128)(2,1)}, bf16[...) custom-call(s32[20]{0:T(128)} %concatenate.42.refs_0_.meta, ...), custom_call_target="tpu_custom_call" | custom-call | flops 536870912 | bytes 10600528 | tf_op jit(solution)/shard_map/pallas_call | solution.py:268
  199.3 14.6 %shard_map.301 = (f32[256,4096]{1,0:T(8,128)}, bf16[256,4096]{1,0:T(8,128)(2,1)}, bf16[3,256,512]{2,1,0:T(8,128)(2,1)}, bf16[3,256,512]{2,1,0:T(8,128)(2,1)}, bf16[3,256,512]{2,1,0:T(8,128)(2,1)}) custom-call(s32[20]{0:T(128)} %concatenate.42.refs_0_.meta, bf16[256,1024]{1,0:T(8,128)(2,1)} %get-tuple-element.253.refs_1_.refs_0_, f32[4,7168]{1,0:T(4,128)} %bitcast.237, ...), custom_call_target="tpu_custom_call" | custom-call | flops 2147483648 | bytes 17416272 | tf_op jit(solution)/shard_map/pallas_call | solution.py:268
  213.9 28.8 %shard_map.302 = (f32[256,1024]{1,0:T(8,128)}, bf16[3,256,512]{2,1,0:T(8,128)(2,1)}, bf16[3,256,512]{2,1,0:T(8,128)(2,1)}, bf16[3,256,512]{2,1,0:T(8,128)(2,1)},...) custom-call(s32[20]{0:T(128)} %concatenate.42.refs_0_.meta, f32[256,1024]{1,0:T(8,128)} %get-tuple-element.252.refs_1_.refs_3_, ...), custom_call_target="tpu_custom_call" | custom-call | flops 2147483648 | bytes 14794832 | tf_op jit(solution)/shard_map/pallas_call | solution.py:268
  242.7 31.5 %shard_map.303 = (bf16[256,1024]{1,0:T(8,128)(2,1)}, bf16[3,256,512]{2,1,0:T(8,128)(2,1)}, bf16[3,256,512]{2,1,0:T(8,128)(2,1)}, bf16[3,256,512]{2,1,0:T(8,128)(2,1)}, bf16[8,256,384]{2,1,0:T(8,128)(2,1)}) custom-call(s32[20]{0:T(128)} %concatenate.42.refs_0_.meta, f32[256,1024]{1,0:T(8,128)} %get-tuple-element.268.refs_1_.refs_2_, f32[4,7168]{1,0:T(4,128)} %bitcast.239, ...), custom_call_target="tpu_custom_call" | custom-call | flops 1610612736 | bytes 11124816 | tf_op jit(solution)/shard_map/pallas_call | solution.py:268
  274.2 37.8 %shard_map.304 = (bf16[2048,384]{1,0:T(8,128)(2,1)}, f32[2,2048,1]{2,1,0:T(8,128)}, f32[2048,128]{1,0:T(8,128)}, bf16[3,256,512]{2,1,0:T(8,128)(2,1)}, bf16[3,25...) custom-call(s32[20]{0:T(128)} %concatenate.42.refs_0_.meta, ...), custom_call_target="tpu_custom_call" | custom-call | flops 4294967296 | bytes 4210768 | tf_op jit(solution)/shard_map/pallas_call | solution.py:268
  312.0 14.6 %shard_map.305 = (bf16[256,1024]{1,0:T(8,128)(2,1)}, f32[256,1024]{1,0:T(8,128)}, bf16[256,1024]{1,0:T(8,128)(2,1)}, bf16[3,256,512]{2,1,0:T(8,128)(2,1)}, bf16[...) custom-call(s32[20]{0:T(128)} %concatenate.42.refs_0_.meta, ...), custom_call_target="tpu_custom_call" | custom-call | flops 536870912 | bytes 11124816 | tf_op jit(solution)/shard_map/pallas_call | solution.py:268
  326.6 10.1 %shard_map.306 = (f32[256,4096]{1,0:T(8,128)}, bf16[256,4096]{1,0:T(8,128)(2,1)}, bf16[3,256,512]{2,1,0:T(8,128)(2,1)}) custom-call(s32[20]{0:T(128)} %concatenate.42.refs_0_.meta, bf16[256,1024]{1,0:T(8,128)(2,1)} %get-tuple-element.282.refs_1_.refs_0_, f32[4,7168]{1,0:T(4,128)} %bitcast.241, bf16[2,256,4096]{2,1,0:T(8,128)(2,1)} %refs_5_.3, ...), custom_call_target="tpu_custom_call" | custom-call | flops 2147483648 | bytes 17416272 | tf_op jit(solution)/shard_map/pallas_call | solution.py:268
  347.7 10.4 %shard_map.309 = (bf16[256,4096]{1,0:T(8,128)(2,1)}, f32[1,1024]{1,0:T(1,128)}, f32[1,4096]{1,0:T(1,128)}) custom-call(s32[20]{0:T(128)} %concatenate.42.refs_0_.meta, bf16[256,1024]{1,0:T(8,128)(2,1)} %get-tuple-element.294.refs_1_, f32[256,4096]{1,0:T(8,128)} %get-tuple-element.295.refs_2_, bf16[2,1024,1024]{2,1,0:T(8,128)(2,1)} %refs_3_.17, ...), custom_call_target="tpu_custom_call" | custom-call | flops 2147483648 | bytes 17322064 | tf_op jit(solution)/shard_map/pallas_call | solution.py:268
  365.1 11.5 %shard_map.311 = (f32[256,1024]{1,0:T(8,128)}, bf16[256,1024]{1,0:T(8,128)(2,1)}, f32[1,1024]{1,0:T(1,128)}, f32[1,1024]{1,0:T(1,128)}, f32[1,1024]{1,0:T(1,128)}, /*index=5*/bf16[4,4,256,512]{3,2,1,0:T(8,128)(2,1)}) custom-call(s32[20]{0:T(128)} %concatenate.42.refs_0_.meta, bf16[256,4096]{1,0:T(8,128)(2,1)} %get-tuple-element.296.refs_1_, ...), custom_call_target="tpu_custom_call" | custom-call | flops 2147483648 | bytes 16379984 | tf_op jit(solution)/shard_map/pallas_call | solution.py:268
  386.3 33.4 %shard_map.313 = (bf16[4,4,256,512]{3,2,1,0:T(8,128)(2,1)}, bf16[4,128,512]{2,1,0:T(8,128)(2,1)}, bf16[4,128,512]{2,1,0:T(8,128)(2,1)}, bf16[4,128,512]{2,1,0:T(...) custom-call(s32[20]{0:T(128)} %concatenate.42.refs_0_.meta, ...), custom_call_target="tpu_custom_call" | custom-call | flops 536870912 | bytes 7864400 | tf_op jit(solution)/shard_map/pallas_call | solution.py:268
  426.0 57.2 %shard_map.314 = (bf16[4,128,512]{2,1,0:T(8,128)(2,1)}, bf16[4,128,512]{2,1,0:T(8,128)(2,1)}, bf16[4,128,512]{2,1,0:T(8,128)(2,1)}, bf16[4,128,512]{2,1,0:T(8,12...) custom-call(s32[20]{0:T(128)} %concatenate.42.refs_0_.meta, ...), custom_call_target="tpu_custom_call" | custom-call | flops 8589934592 | bytes 3162192 | tf_op jit(solution)/shard_map/pallas_call | solution.py:268
  489.0 35.2 %shard_map.315 = (f32[256,1024]{1,0:T(8,128)}, bf16[256,1024]{1,0:T(8,128)(2,1)}, bf16[256,3072]{1,0:T(8,128)(2,1)}, f32[1,3072]{1,0:T(1,128)}, f32[1,1024]{1,0:...) custom-call(s32[20]{0:T(128)} %concatenate.42.refs_0_.meta, ...), custom_call_target="tpu_custom_call" | custom-call | flops 1610612736 | bytes 16388176 | tf_op jit(solution)/shard_map/pallas_call | solution.py:268
  535.9 29.8 %shard_map.317 = (bf16[256,4096]{1,0:T(8,128)(2,1)}, f32[1,1024]{1,0:T(1,128)}, f32[1,4096]{1,0:T(1,128)}, bf16[4,4,256,512]{3,2,1,0:T(8,128)(2,1)}, bf16[3,256,...) custom-call(s32[20]{0:T(128)} %concatenate.42.refs_0_.meta, ...), custom_call_target="tpu_custom_call" | custom-call | flops 2147483648 | bytes 17322064 | tf_op jit(solution)/shard_map/pallas_call | solution.py:268
  577.0 37.4 %shard_map.319 = (f32[256,1024]{1,0:T(8,128)}, bf16[256,1024]{1,0:T(8,128)(2,1)}, f32[1,1024]{1,0:T(1,128)}, f32[1,1024]{1,0:T(1,128)}, f32[1,1024]{1,0:T(1,128)...) custom-call(s32[20]{0:T(128)} %concatenate.42.refs_0_.meta, ...), custom_call_target="tpu_custom_call" | custom-call | flops 2147483648 | bytes 16379984 | tf_op jit(solution)/shard_map/pallas_call | solution.py:268
  627.4 47.5 %shard_map.321 = (bf16[4,4,256,512]{3,2,1,0:T(8,128)(2,1)}, bf16[4,128,512]{2,1,0:T(8,128)(2,1)}, bf16[4,128,512]{2,1,0:T(8,128)(2,1)}, bf16[4,128,512]{2,1,0:T(...) custom-call(s32[20]{0:T(128)} %concatenate.42.refs_0_.meta, ...), custom_call_target="tpu_custom_call" | custom-call | flops 536870912 | bytes 7864400 | tf_op jit(solution)/shard_map/pallas_call | solution.py:268
  684.8 57.3 %shard_map.322 = (bf16[4,128,512]{2,1,0:T(8,128)(2,1)}, bf16[4,128,512]{2,1,0:T(8,128)(2,1)}, bf16[4,128,512]{2,1,0:T(8,128)(2,1)}, bf16[4,128,512]{2,1,0:T(8,12...) custom-call(s32[20]{0:T(128)} %concatenate.42.refs_0_.meta, ...), custom_call_target="tpu_custom_call" | custom-call | flops 8589934592 | bytes 3162192 | tf_op jit(solution)/shard_map/pallas_call | solution.py:268
  749.4 30.5 %shard_map.323 = (f32[256,1024]{1,0:T(8,128)}, bf16[256,1024]{1,0:T(8,128)(2,1)}, bf16[256,3072]{1,0:T(8,128)(2,1)}, f32[1,3072]{1,0:T(1,128)}, f32[1,1024]{1,0:...) custom-call(s32[20]{0:T(128)} %concatenate.42.refs_0_.meta, ...), custom_call_target="tpu_custom_call" | custom-call | flops 1610612736 | bytes 15863888 | tf_op jit(solution)/shard_map/pallas_call | solution.py:268
  807.2 26.0 %shard_map.325 = (bf16[256,512]{1,0:T(8,128)(2,1)}, bf16[256,512]{1,0:T(8,128)(2,1)}, bf16[256,512]{1,0:T(8,128)(2,1)}, bf16[256,512]{1,0:T(8,128)(2,1)}, bf16[2...) custom-call(bf16[256,512]{1,0:T(8,128)(2,1)} %get-tuple-element.388., ...), custom_call_target="tpu_custom_call" | custom-call | tf_op jit(solution)/shard_map/pallas_call | solution.py:268
  839.2 36.1 %shard_map.326 = (bf16[256,512]{1,0:T(8,128)(2,1)}, bf16[256,512]{1,0:T(8,128)(2,1)}, bf16[256,512]{1,0:T(8,128)(2,1)}, bf16[256,512]{1,0:T(8,128)(2,1)}, bf16[2...) custom-call(bf16[256,512]{1,0:T(8,128)(2,1)} %get-tuple-element.400., ...), custom_call_target="tpu_custom_call" | custom-call | tf_op jit(solution)/shard_map/pallas_call | solution.py:268
  879.0 19.5 %shard_map.327 = (bf16[256,512]{1,0:T(8,128)(2,1)}, bf16[256,512]{1,0:T(8,128)(2,1)}, bf16[256,512]{1,0:T(8,128)(2,1)}, bf16[256,512]{1,0:T(8,128)(2,1)}, bf16[4...) custom-call(bf16[256,512]{1,0:T(8,128)(2,1)} %get-tuple-element.407.refs_0_.refs_7_, ...), custom_call_target="tpu_custom_call" | custom-call | tf_op jit(solution)/shard_map/pallas_call | solution.py:268
  902.4 28.0 %shard_map.328 = (bf16[256,512]{1,0:T(8,128)(2,1)}, bf16[3,256,512]{2,1,0:T(8,128)(2,1)}, f32[3,56,128]{2,1,0:T(8,128)}) custom-call(bf16[256,512]{1,0:T(8,128)(2,1)} %get-tuple-element.413.refs_0_.refs_7_, bf16[4,256,512]{2,1,0:T(8,128)(2,1)} %pad_maximum_fusion.5.refs_1_, f32[4,56,128]{2,1,0:T(8,128)} %fusion.72.refs_2_), custom_call_target="tpu_custom_call" | custom-call | tf_op jit(solution)/shard_map/pallas_call | solution.py:268
  (268 shorter events, 198.5 us)
Async XLA Ops:
  386.3 33.5 %copy-start = (bf16[4,4,256,512]{3,2,1,0:T(8,128)(2,1)S(1)}, bf16[4,4,256,512]{3,2,1,0:T(8,128)(2,1)}, u32[]{:S(2)}) copy-start(bf16[4,4,256,512]{3,2,1,0:T(8,128)(2,1)} %get-tuple-element.308) | copy-start | bytes 12582916
  426.0 57.2 %copy-start.17 = (bf16[4,128,512]{2,1,0:T(8,128)(2,1)S(1)}, bf16[4,128,512]{2,1,0:T(8,128)(2,1)}, u32[]{:S(2)}) copy-start(bf16[4,128,512]{2,1,0:T(8,128)(2,1)} %get-tuple-element.313) | copy-start | bytes 1572868
  426.0 57.2 %copy-start.18 = (bf16[4,128,512]{2,1,0:T(8,128)(2,1)S(1)}, bf16[4,128,512]{2,1,0:T(8,128)(2,1)}, u32[]{:S(2)}) copy-start(bf16[4,128,512]{2,1,0:T(8,128)(2,1)} %get-tuple-element.316) | copy-start | bytes 1572868
  684.8 57.3 %copy-start.15 = (bf16[4,128,512]{2,1,0:T(8,128)(2,1)S(1)}, bf16[4,128,512]{2,1,0:T(8,128)(2,1)}, u32[]{:S(2)}) copy-start(bf16[4,128,512]{2,1,0:T(8,128)(2,1)} %get-tuple-element.362) | copy-start | bytes 1572868
  684.8 57.3 %copy-start.16 = (bf16[4,128,512]{2,1,0:T(8,128)(2,1)S(1)}, bf16[4,128,512]{2,1,0:T(8,128)(2,1)}, u32[]{:S(2)}) copy-start(bf16[4,128,512]{2,1,0:T(8,128)(2,1)} %get-tuple-element.365) | copy-start | bytes 1572868
  749.4 32.5 %copy-start.11 = (bf16[4,128,512]{2,1,0:T(8,128)(2,1)S(1)}, bf16[4,128,512]{2,1,0:T(8,128)(2,1)}, u32[]{:S(2)}) copy-start(bf16[4,128,512]{2,1,0:T(8,128)(2,1)} %get-tuple-element.391) | copy-start | bytes 1572868
  749.4 32.5 %copy-start.12 = (bf16[4,128,512]{2,1,0:T(8,128)(2,1)S(1)}, bf16[4,128,512]{2,1,0:T(8,128)(2,1)}, u32[]{:S(2)}) copy-start(bf16[4,128,512]{2,1,0:T(8,128)(2,1)} %get-tuple-element.394) | copy-start | bytes 1572868
  785.5 12.6 %copy-start.38 = (f32[1,4096]{1,0:T(1,128)S(1)}, f32[1,4096]{1,0:T(1,128)}, u32[]{:S(2)}) copy-start(f32[1,4096]{1,0:T(1,128)} %get-tuple-element.376) | copy-start | bytes 49156
  785.5 13.3 %copy-start.49 = (f32[1,1024]{1,0:T(1,128)S(1)}, f32[1,1024]{1,0:T(1,128)}, u32[]{:S(2)}) copy-start(f32[1,1024]{1,0:T(1,128)} %get-tuple-element.377) | copy-start | bytes 12292
  785.5 14.0 %copy-start.48 = (f32[1,1024]{1,0:T(1,128)S(1)}, f32[1,1024]{1,0:T(1,128)}, u32[]{:S(2)}) copy-start(f32[1,1024]{1,0:T(1,128)} %get-tuple-element.378) | copy-start | bytes 12292
  785.5 14.7 %copy-start.47 = (f32[1,1024]{1,0:T(1,128)S(1)}, f32[1,1024]{1,0:T(1,128)}, u32[]{:S(2)}) copy-start(f32[1,1024]{1,0:T(1,128)} %get-tuple-element.379) | copy-start | bytes 12292
  785.5 15.4 %copy-start.39 = (f32[1,3072]{1,0:T(1,128)S(1)}, f32[1,3072]{1,0:T(1,128)}, u32[]{:S(2)}) copy-start(f32[1,3072]{1,0:T(1,128)} %get-tuple-element.380) | copy-start | bytes 36868
  785.5 16.1 %copy-start.46 = (f32[1,1024]{1,0:T(1,128)S(1)}, f32[1,1024]{1,0:T(1,128)}, u32[]{:S(2)}) copy-start(f32[1,1024]{1,0:T(1,128)} %get-tuple-element.381) | copy-start | bytes 12292
  785.5 16.8 %copy-start.45 = (f32[1,1024]{1,0:T(1,128)S(1)}, f32[1,1024]{1,0:T(1,128)}, u32[]{:S(2)}) copy-start(f32[1,1024]{1,0:T(1,128)} %get-tuple-element.382) | copy-start | bytes 12292
  785.5 17.5 %copy-start.44 = (f32[1,1024]{1,0:T(1,128)S(1)}, f32[1,1024]{1,0:T(1,128)}, u32[]{:S(2)}) copy-start(f32[1,1024]{1,0:T(1,128)} %get-tuple-element.383) | copy-start | bytes 12292
  785.5 18.2 %copy-start.37 = (f32[1,4096]{1,0:T(1,128)S(1)}, f32[1,4096]{1,0:T(1,128)}, u32[]{:S(2)}) copy-start(f32[1,4096]{1,0:T(1,128)} %get-tuple-element.384) | copy-start | bytes 49156
  785.5 18.9 %copy-start.43 = (f32[1,1024]{1,0:T(1,128)S(1)}, f32[1,1024]{1,0:T(1,128)}, u32[]{:S(2)}) copy-start(f32[1,1024]{1,0:T(1,128)} %get-tuple-element.385) | copy-start | bytes 12292
  785.6 19.6 %copy-start.42 = (f32[1,1024]{1,0:T(1,128)S(1)}, f32[1,1024]{1,0:T(1,128)}, u32[]{:S(2)}) copy-start(f32[1,1024]{1,0:T(1,128)} %get-tuple-element.386) | copy-start | bytes 12292
  785.6 20.3 %copy-start.41 = (f32[1,1024]{1,0:T(1,128)S(1)}, f32[1,1024]{1,0:T(1,128)}, u32[]{:S(2)}) copy-start(f32[1,1024]{1,0:T(1,128)} %get-tuple-element.387) | copy-start | bytes 12292
  806.5 28.7 %copy-start.1 = (bf16[4,4,256,512]{3,2,1,0:T(8,128)(2,1)S(1)}, bf16[4,4,256,512]{3,2,1,0:T(8,128)(2,1)}, u32[]{:S(2)}) copy-start(bf16[4,4,256,512]{3,2,1,0:T(8,128)(2,1)} %get-tuple-element.404) | copy-start | bytes 12582916
  839.2 39.2 %copy-start.4 = (f32[4,56,128]{2,1,0:T(8,128)S(1)}, f32[4,56,128]{2,1,0:T(8,128)}, u32[]{:S(2)}) copy-start(f32[4,56,128]{2,1,0:T(8,128)} %fusion.77.refs_8_) | copy-start | bytes 344068
  875.3 23.2 %copy-start.22 = (bf16[4,128,512]{2,1,0:T(8,128)(2,1)S(1)}, bf16[4,128,512]{2,1,0:T(8,128)(2,1)}, u32[]{:S(2)}) copy-start(bf16[4,128,512]{2,1,0:T(8,128)(2,1)} %get-tuple-element.414) | copy-start | bytes 1572868
  875.3 23.2 %copy-start.23 = (bf16[4,128,512]{2,1,0:T(8,128)(2,1)S(1)}, bf16[4,128,512]{2,1,0:T(8,128)(2,1)}, u32[]{:S(2)}) copy-start(bf16[4,128,512]{2,1,0:T(8,128)(2,1)} %get-tuple-element.417) | copy-start | bytes 1572868
  879.0 22.8 %copy-start.5 = (f32[4,56,128]{2,1,0:T(8,128)S(1)}, f32[4,56,128]{2,1,0:T(8,128)}, u32[]{:S(2)}) copy-start(f32[4,56,128]{2,1,0:T(8,128)} %add.571.refs_5_) | copy-start | bytes 344068
  (31 other events, 183.3 us)

commit v2 on v1

v2 whole, which is shorter than its diff:
```python
import collections
import functools
import itertools

import jax
import jax.numpy as jnp
from jax import lax
from jax.experimental import pallas as pl
from jax.experimental.pallas import tpu as pltpu
from jax.sharding import PartitionSpec as P

HEADS = 16
HEAD_DIM = 64
LAYERS = 2
EPS = 1e-05
NEG = -1e30
LOW = -1e29
F32 = jnp.float32
BF16 = jnp.bfloat16
VMEM_BYTES = 56 * 1024 * 1024

FIELDS = ("t", "d", "ff", "nf", "nc", "pr", "pc", "nq", "ncs", "ffn", "w", "hl", "rows", "half")
Dims = collections.namedtuple("Dims", FIELDS)


def dims_of(acts, fc_weight, nf, nc):
    t, d = acts.shape[1], acts.shape[2]
    ff = fc_weight.shape[2]
    pr, pc = d // nf, ff // nc
    return Dims(
        t=t, d=d, ff=ff, nf=nf, nc=nc, pr=pr, pc=pc, nq=3 * d // pc, ncs=d // pc, ffn=ff // nf,
        w=d // nc, hl=HEADS // nc, rows=t * nc, half=t // 2,
    )


SMALL = (("g1", 1), ("s1", 1), ("bq", 3), ("bp", 1), ("g2", 1), ("s2", 1), ("bf", 4), ("bo", 1))


def small_offsets(dm):
    table, at = {}, 0
    for layer in range(LAYERS):
        for name, _ in SMALL:
            size = {"bq": 3 * dm.pr, "bf": dm.ffn}.get(name, dm.pr)
            table[name + str(layer)] = (at, size)
            at += size
    for name in ("gf", "sf"):
        table[name] = (at, dm.pr)
        at += dm.pr
    return table, at


def send_blocks(dm, slot, shape):
    return Move(
        shape, BF16,
        [([(None, slot, (j,))], ("ctx", j) if j else None, (j,)) for j in range(dm.nc)],
    )


def vector_names():
    return [name + str(layer) for layer in range(LAYERS) for name, _ in SMALL] + ["gf", "sf"]


def mult(v, by):
    return pl.multiple_of(v, by)


def nn(a, b):
    return lax.dot_general(a, b, (((1,), (0,)), ((), ())), preferred_element_type=F32)


def nt(a, b):
    return lax.dot_general(a, b, (((1,), (1,)), ((), ())), preferred_element_type=F32)


def tn(a, b):
    return lax.dot_general(a, b, (((0,), (0,)), ((), ())), preferred_element_type=F32)


def col_sum(v):
    return jnp.sum(v.astype(F32), axis=0, keepdims=True)


def small_vec(dm, small_ref, name):
    at, size = small_offsets(dm)[0][name]
    return jnp.concatenate([small_ref[g : g + 1, at : at + size] for g in range(dm.nf)], axis=1)


def norm_parts(v):
    center = v - jnp.mean(v, axis=-1, keepdims=True)
    scale = lax.rsqrt(jnp.mean(center * center, axis=-1, keepdims=True) + EPS)
    return center * scale, scale


def norm(v, gain, shift):
    return norm_parts(v)[0] * gain + shift


def norm_back(v, gain, dy):
    xh, scale = norm_parts(v)
    e = dy * gain
    dv = scale * (
        e - jnp.mean(e, axis=-1, keepdims=True) - xh * jnp.mean(e * xh, axis=-1, keepdims=True)
    )
    return dv, col_sum(dy * xh), col_sum(dy)


K0 = 0.7978845608028654
K1 = 0.044715


def gelu(u):
    return 0.5 * u * (1.0 + jnp.tanh(K0 * (u + K1 * u * u * u)))


def gelu_slope(u):
    th = jnp.tanh(K0 * (u + K1 * u * u * u))
    return 0.5 * (1.0 + th) + 0.5 * u * (1.0 - th * th) * (K0 * (1.0 + 3.0 * K1 * u * u))


class Slot:
    def __init__(self, kind, at, like=None):
        self.kind, self.at, self.result = kind, at, None
        if like is not None:
            self.shape, self.dtype = like.shape, like.dtype


class Move:
    def __init__(self, shape, dtype, parts):
        self.shape, self.dtype, self.parts = shape, dtype, parts
        self.result = None


def whole(array, route):
    return Move(array.shape, array.dtype, [([(None, array, None)], route, None)])


def value(v):
    return v.result if isinstance(v, (Move, Slot)) else v


def at_of(ref, index):
    return ref if index is None else ref.at[index() if callable(index) else index]


class Kernel:
    def __init__(self, dm, ids=None):
        self.dm, self.ids = dm, ids
        self.arrays, self.in_specs, self.slots = [], [], {}
        self.outs, self.out_specs, self.out_slots = [], [], []
        self.scratch, self.keys, self.steps = [], {}, []
        self.moves, self.flops = [], 0

    def operand(self, a, place):
        if isinstance(a, (Slot, Move)) and a.result is None:
            return a
        a = value(a)
        key = (id(a), place)
        if key not in self.slots:
            spaces = {"v": pltpu.VMEM, "s": pltpu.SMEM, "a": pl.ANY}
            self.slots[key] = Slot("in", len(self.arrays))
            self.arrays.append(a)
            self.in_specs.append(pl.BlockSpec(memory_space=spaces[place]))
        return self.slots[key]

    def output(self, out, space):
        slot = Slot("out", len(self.outs), out)
        self.outs.append(out)
        self.out_specs.append(pl.BlockSpec(memory_space=space))
        self.out_slots.append(slot)
        return slot

    def buffer(self, spec):
        key, spec = spec if isinstance(spec, tuple) else (None, spec)
        if key is None or key not in self.keys:
            slot = Slot("scratch", len(self.scratch))
            self.scratch.append(spec)
            if key is None:
                return slot
            self.keys[key] = slot
        return self.keys[key]

    def section(self, body, operands, outs, scratch, flops):
        refs = [self.operand(a, place) for a, place in operands]
        made = [self.output(o, pltpu.VMEM) for o in outs]
        bufs = [self.buffer(spec) for spec in scratch]
        self.steps.append(("body", body, refs + made + bufs))
        self.flops += flops
        return made, bufs

    def start(self, moves):
        for move in moves:
            parts = [
                ([(cond, self.operand(src, "a"), index) for cond, src, index in sources], route, place)
                for sources, route, place in move.parts
            ]
            slot = self.output(sds(move.shape, move.dtype), pl.ANY)
            self.moves.append((move, parts, slot))
            self.steps.append(("start", len(self.moves) - 1, None))

    def run(self, local=None):
        dm, moves, steps = self.dm, self.moves, self.steps
        order = {id(m): n for n, (m, _, _) in enumerate(moves)}
        count = sum(len(parts) for _, parts, _ in moves)
        routes = sorted({route for _, parts, _ in moves for _, route, _ in parts if route is not None})
        n_in, n_out, n_scratch = len(self.arrays), len(self.outs), len(self.scratch)
        sems = [pltpu.SemaphoreType.DMA((count,))] * 2 if count else []

        def kernel(*refs):
            groups = {"in": refs[:n_in], "out": refs[n_in : n_in + n_out], "scratch": refs[n_in + n_out :]}
            if count:
                send_sems, recv_sems = refs[-2:]
            c, f = lax.axis_index("ctx"), lax.axis_index("fsdp")

            def device(route, back=False):
                axis, by = route
                if axis == "ctx":
                    return (c ^ by, f)
                return (c, lax.rem(f + (dm.nf - by if back else by), dm.nf))

            if routes:
                barrier = pltpu.get_barrier_semaphore()
                for route in routes:
                    pl.semaphore_signal(
                        barrier, inc=1, device_id=device(route, True), device_id_type=pl.DeviceIdType.MESH
                    )
                pl.semaphore_wait(barrier, len(routes))

            def ref_of(src):
                if isinstance(src, Move):
                    src = moves[order[id(src)]][2]
                return groups[src.kind][src.at]

            at, copies = 0, []
            for _, parts, slot in moves:
                rows = []
                for sources, route, place in parts:
                    choices = []
                    for cond, src, index in sources:
                        ends = at_of(ref_of(src), index), at_of(ref_of(slot), place)
                        if route is None:
                            copy = pltpu.make_async_copy(*ends, recv_sems.at[at])
                        else:
                            copy = pltpu.make_async_remote_copy(
                                *ends, send_sems.at[at], recv_sems.at[at],
                                device_id=device(route), device_id_type=pl.DeviceIdType.MESH,
                            )
                        choices.append((cond, copy))
                    rows.append((route, choices))
                    at += 1
                copies.append(rows)
            arrived = set()

            def wait(n):
                if n in arrived:
                    return
                arrived.add(n)
                for route, choices in copies[n]:
                    copy = choices[0][1]
                    copy.wait() if route is None else copy.wait_recv()

            def ready(src):
                if isinstance(src, Move):
                    wait(order[id(src)])

            for kind, what, used in steps:
                if kind == "body":
                    for slot in used:
                        ready(slot)
                    what(*[ref_of(slot) for slot in used])
                    continue
                for sources, _, _ in moves[what][1]:
                    for _, src, _ in sources:
                        ready(src)
                for _, choices in copies[what]:
                    for cond, copy in choices:
                        if cond is None:
                            copy.start()
                        else:
                            pl.when(cond())(copy.start)
            for n in range(len(moves)):
                wait(n)
            for rows in copies:
                for route, choices in rows:
                    if route is not None:
                        choices[0][1].wait_send()

        params = {"collective_id": next(self.ids), "has_side_effects": True} if routes else {}
        moved = sum(a.size * a.dtype.itemsize for a in self.arrays + self.outs)
        results = pl.pallas_call(
            kernel,
            out_shape=self.outs,
            in_specs=self.in_specs,
            out_specs=self.out_specs,
            scratch_shapes=self.scratch + sems,
            compiler_params=pltpu.CompilerParams(vmem_limit_bytes=VMEM_BYTES, **params),
            cost_estimate=pl.CostEstimate(flops=self.flops, bytes_accessed=moved, transcendentals=0),
        )(*self.arrays)
        for slot, result in zip(self.out_slots, results):
            slot.result = result
        for move, _, slot in moves:
            move.result = slot.result


def sds(shape, dtype):
    return jax.ShapeDtypeStruct(shape, dtype)


class Pieces:
    def __init__(self, dm, layer, own, pieces, own_buf, piece_buf, sems, wanted):
        self.dm, self.wanted = dm, wanted
        self.own_copy = pltpu.make_async_copy(own.at[layer], own_buf, sems.at[dm.nc])
        self.copies = [
            pltpu.make_async_copy(pieces[j], piece_buf.at[j], sems.at[j]) for j in range(dm.nc)
        ]
        self.own, self.buf = own_buf, piece_buf

    def start(self):
        self.own_copy.start()
        for j in range(self.dm.nc):
            self.each(j, self.copies[j].start)

    def each(self, j, act):
        if self.wanted is None:
            act()
        else:
            pl.when(self.wanted(j))(act)

    def wait_own(self):
        self.own_copy.wait()

    def flat(self, j):
        return self.buf[j].reshape((self.dm.nf - 1) * self.dm.pr, self.dm.pc)


def piece_scratch(dm, own_shape):
    return [
        ("own" + str(own_shape), pltpu.VMEM(own_shape, BF16)),
        ("pieces", pltpu.VMEM((dm.nc, dm.nf - 1, dm.pr, dm.pc), BF16)),
        ("loads", pltpu.SemaphoreType.DMA((dm.nc + 1,))),
    ]


def ring(dm, f, s):
    return lax.rem(f + (dm.nf - s), dm.nf)


def relative(dm, f, src, dst):
    for s in range(dm.nf):
        at = mult(ring(dm, f, s) * dm.pr, dm.pr)
        dst[:, s * dm.pr : (s + 1) * dm.pr] = src[:, pl.ds(at, dm.pr)]


def take_heads(dm, ref, base, i):
    if dm.w % 128 == 0:
        return ref[:, pl.ds(mult(base + i * dm.w, 128), dm.w)]
    per = 128 // dm.w
    wide = ref[:, pl.ds(mult(base + (i // per) * 128, 128), 128)]
    part = wide[:, : dm.w]
    for at in range(1, per):
        part = jnp.where(lax.rem(i, per) == at, wide[:, at * dm.w : (at + 1) * dm.w], part)
    return part


def put_heads(dm, ref, base, blocks, at, c):
    if dm.w % 128 == 0:
        for j in range(dm.nc):
            ref[:, pl.ds(mult(base + (c ^ j) * dm.w, 128), dm.w)] = blocks[j][:, at : at + dm.w]
        return
    for j in range(0, dm.nc, 2):
        one, two = blocks[j][:, at : at + dm.w], blocks[j + 1][:, at : at + dm.w]
        even = lax.rem(c, 2) == 0
        pair = jnp.concatenate([jnp.where(even, one, two), jnp.where(even, two, one)], axis=1)
        ref[:, pl.ds(mult(base + ((c ^ j) // 2) * 128, 128), 128)] = pair


def qkv_body(dm, layer, *refs):
    nc = dm.nc
    meta, h, small, own = refs[:4]
    pieces = refs[4 : 4 + nc]
    n1, xr, y, bias, blocks, own_buf, piece_buf, sems = refs[4 + nc :]
    c, f = lax.axis_index("ctx"), lax.axis_index("fsdp")
    weight = Pieces(dm, layer, own, pieces, own_buf, piece_buf, sems, lambda j: (c ^ j) < dm.nq)
    weight.start()
    tag = str(layer)
    n1[...] = norm(
        h[...].astype(F32), small_vec(dm, small, "g1" + tag), small_vec(dm, small, "s1" + tag)
    ).astype(BF16)
    bias[...] = small_vec(dm, small, "bq" + tag)
    relative(dm, f, n1, xr)
    weight.wait_own()
    for j in range(nc):
        i = c ^ j

        @pl.when(i < dm.nq)
        def _():
            weight.copies[j].wait()
            at = pl.ds(mult(i * dm.pc, dm.pc), dm.pc)
            acc = nn(xr[:, dm.pr :], weight.flat(j)) + nn(xr[:, : dm.pr], own_buf[:, at])
            y[:, at] = (acc + bias[:, at]).astype(BF16)

    for j in range(nc):
        for third in range(3):
            blocks[j, :, third * dm.w : (third + 1) * dm.w] = take_heads(
                dm, y, third * dm.d, c ^ j
            )


def qkv_section(k, layer, h, small, own, pieces, meta):
    dm = k.dm
    shape = (dm.nc, dm.t, 3 * dm.w)
    (n1,), bufs = k.section(
        functools.partial(qkv_body, dm, layer),
        [(meta, "s"), (h, "v"), (small, "v"), (own, "a")] + [(p, "a") for p in pieces],
        [sds((dm.t, dm.d), BF16)],
        [
            ("xr", pltpu.VMEM((dm.t, dm.d), BF16)),
            pltpu.VMEM((dm.t, 3 * dm.d), BF16),
            pltpu.VMEM((1, 3 * dm.d), F32),
            pltpu.VMEM(shape, BF16),
        ]
        + piece_scratch(dm, (dm.pr, 3 * dm.d)),
        2 * dm.t * dm.d * 3 * dm.d,
    )
    blocks = send_blocks(dm, bufs[3], shape)
    k.start([blocks])
    return n1, blocks


def proj_body(dm, layer, *refs):
    nc = dm.nc
    meta, h, small, own, heads = refs[:5]
    pieces = refs[5 : 5 + nc]
    ob, mid, n2 = refs[5 + nc : 8 + nc]
    xr, bias, own_buf, piece_buf, sems = refs[8 + nc :]
    c, f = lax.axis_index("ctx"), lax.axis_index("fsdp")
    weight = Pieces(dm, layer, own, pieces, own_buf, piece_buf, sems, lambda j: (c ^ j) >= dm.nq)
    weight.start()
    tag = str(layer)
    bias[...] = small_vec(dm, small, "bp" + tag)
    put_heads(dm, ob, 0, [heads.at[j] for j in range(nc)], 0, c)
    relative(dm, f, ob, xr)
    weight.wait_own()
    for j in range(nc):
        i = c ^ j

        @pl.when(i >= dm.nq)
        def _():
            weight.copies[j].wait()
            at = pl.ds(mult((i - dm.nq) * dm.pc, dm.pc), dm.pc)
            acc = nn(xr[:, dm.pr :], weight.flat(j)) + nn(xr[:, : dm.pr], own_buf[:, at])
            mid[:, at] = h[:, at].astype(F32) + acc + bias[:, at]

    n2[...] = norm(
        mid[...], small_vec(dm, small, "g2" + tag), small_vec(dm, small, "s2" + tag)
    ).astype(BF16)


def proj_section(k, layer, h, small, own, heads, pieces, meta):
    dm = k.dm
    td = (dm.t, dm.d)
    return k.section(
        functools.partial(proj_body, dm, layer),
        [(meta, "s"), (h, "v"), (small, "v"), (own, "a"), (heads, "v")] + [(p, "a") for p in pieces],
        [sds(td, BF16), sds(td, F32), sds(td, BF16)],
        [("xr", pltpu.VMEM(td, BF16)), pltpu.VMEM((1, dm.d), F32)] + piece_scratch(dm, (dm.pr, dm.d)),
        2 * dm.t * dm.d * dm.d,
    )[0]


def fc_body(dm, layer, *refs):
    nc = dm.nc
    meta, n2, small, own = refs[:4]
    pieces = refs[4 : 4 + nc]
    u, act = refs[4 + nc : 6 + nc]
    xr, bias, own_buf, piece_buf, sems = refs[6 + nc :]
    c, f = lax.axis_index("ctx"), lax.axis_index("fsdp")
    weight = Pieces(dm, layer, own, pieces, own_buf, piece_buf, sems, None)
    weight.start()
    bias[...] = small_vec(dm, small, "bf" + str(layer))
    relative(dm, f, n2, xr)
    weight.wait_own()
    for j in range(nc):
        i = c ^ j
        weight.copies[j].wait()
        at = pl.ds(mult(i * dm.pc, dm.pc), dm.pc)
        acc = nn(xr[:, dm.pr :], weight.flat(j)) + nn(xr[:, : dm.pr], own_buf[:, at])
        acc = acc + bias[:, at]
        u[:, at] = acc
        act[:, at] = gelu(acc).astype(BF16)


def fc_section(k, layer, n2, small, own, pieces, meta):
    dm = k.dm
    return k.section(
        functools.partial(fc_body, dm, layer),
        [(meta, "s"), (n2, "v"), (small, "v"), (own, "a")] + [(p, "a") for p in pieces],
        [sds((dm.t, dm.ff), F32), sds((dm.t, dm.ff), BF16)],
        [("xr", pltpu.VMEM((dm.t, dm.d), BF16)), pltpu.VMEM((1, dm.ff), F32)]
        + piece_scratch(dm, (dm.pr, dm.ff)),
        2 * dm.t * dm.d * dm.ff,
    )[0]


def out_body(dm, layer, *refs):
    nc = dm.nc
    meta, mid, act, small, own = refs[:5]
    pieces = refs[5 : 5 + nc]
    h = refs[5 + nc]
    own_buf, piece_buf, sems = refs[6 + nc :]
    c, f = lax.axis_index("ctx"), lax.axis_index("fsdp")
    weight = Pieces(dm, layer, own, pieces, own_buf, piece_buf, sems, None)
    weight.start()
    weight.wait_own()
    mine = act[:, pl.ds(mult(f * dm.ffn, dm.ffn), dm.ffn)]
    h[...] = mid[...] + nn(mine, own_buf[...]) + small_vec(dm, small, "bo" + str(layer))
    for col in range(dm.ncs):
        acc = None
        for j in range(col, nc, dm.ncs):
            i = c ^ j
            weight.copies[j].wait()
            for s in range(1, dm.nf):
                at = mult(ring(dm, f, s) * dm.ffn + (i // dm.ncs) * dm.pr, dm.pr)
                part = nn(act[:, pl.ds(at, dm.pr)], piece_buf[j, s - 1])
                acc = part if acc is None else acc + part
        at = pl.ds(mult((lax.rem(c, dm.ncs) ^ col) * dm.pc, dm.pc), dm.pc)
        h[:, at] = h[:, at] + acc


def out_section(k, layer, mid, act, small, own, pieces, meta):
    dm = k.dm
    return k.section(
        functools.partial(out_body, dm, layer),
        [(meta, "s"), (mid, "v"), (act, "v"), (small, "v"), (own, "a")] + [(p, "a") for p in pieces],
        [sds((dm.t, dm.d), F32)],
        piece_scratch(dm, (dm.ffn, dm.d)),
        2 * dm.t * dm.d * dm.ff,
    )[0][0]


def chosen(dm, which, take):
    out = take(0).astype(F32)
    pick = jnp.full(out.shape, which, jnp.int32)
    for k in range(1, dm.nc):
        out = jnp.where(pick == k, take(k).astype(F32), out)
    return out.astype(BF16)


def sort_rows(dm, meta, blocks, dst):
    for piece in range(2 * dm.nc):
        slot = meta[4 + dm.nc + min(piece, 2 * dm.nc - 1 - piece)]
        half = 0 if piece < dm.nc else dm.half
        dst[piece * dm.half : (piece + 1) * dm.half, :] = chosen(
            dm, slot, lambda j: blocks[j, half : half + dm.half, :]
        )


def unsort_rows(dm, meta, src, blocks, at):
    cols = slice(at, at + src.shape[1])

    def rows(piece):
        return src[piece * dm.half : (piece + 1) * dm.half, :]

    for j in range(dm.nc):
        low = meta[4 + j]
        blocks[j, : dm.half, cols] = chosen(dm, low, rows)
        blocks[j, dm.half :, cols] = chosen(dm, low, lambda k: rows(2 * dm.nc - 1 - k))


def stack_heads(dm, v, scale=None):
    if scale is not None:
        v = v * scale
    if dm.hl == 1:
        return v
    lane = lax.broadcasted_iota(jnp.int32, v.shape, 1) // HEAD_DIM
    return jnp.concatenate([jnp.where(lane == k, v, 0.0).astype(v.dtype) for k in range(dm.hl)], axis=0)


def pick_heads(dm, v):
    if dm.hl == 1:
        return v
    rows = v.shape[0] // dm.hl
    lane = lax.broadcasted_iota(jnp.int32, (rows, v.shape[1]), 1) // HEAD_DIM
    out = v[:rows]
    for k in range(1, dm.hl):
        out = jnp.where(lane == k, v[k * rows : (k + 1) * rows], out)
    return out


def doc_start(first_cut, second_cut, row):
    return jnp.where(row < first_cut, 0, jnp.where(row < second_cut, first_cut, second_cut))


def tile_rows(dm, t, tq, cuts):
    row = t * tq + lax.rem(lax.broadcasted_iota(jnp.int32, (dm.hl * tq, 1), 0), tq)
    return row, doc_start(cuts[0], cuts[1], row)


TQ = 256
TK = 256


def attend_body(dm, *refs):
    nc, w = dm.nc, dm.w
    meta, blocks, packed, lse, mixed, heads = refs
    cuts = (meta[2], meta[3])
    tq, tk = min(TQ, dm.rows), min(TK, dm.rows)
    sort_rows(dm, meta, blocks, packed)

    def tile(t, carry):
        here = pl.ds(mult(t * tq, tq), tq)
        q = stack_heads(dm, packed[here, :w], HEAD_DIM**-0.5)
        row, start = tile_rows(dm, t, tq, cuts)

        def chunk(kb, state):
            top, mass, acc = state
            there = pl.ds(mult(kb * tk, tk), tk)
            col = kb * tk + lax.broadcasted_iota(jnp.int32, (1, tk), 1)
            s = jnp.where((col <= row) & (col >= start), nt(q, packed[there, w : 2 * w]), NEG)
            new_top = jnp.maximum(top, jnp.max(s, axis=1, keepdims=True))
            p = jnp.exp(s - new_top)
            fade = jnp.exp(top - new_top)
            mass = mass * fade + jnp.sum(p, axis=1, keepdims=True)
            acc = acc * fade + nn(p.astype(BF16), packed[there, 2 * w :])
            return new_top, mass, acc

        initial = (
            jnp.full((dm.hl * tq, 1), LOW, F32),
            jnp.zeros((dm.hl * tq, 1), F32),
            jnp.zeros((dm.hl * tq, w), F32),
        )
        top, mass, acc = lax.fori_loop(0, ((t + 1) * tq + tk - 1) // tk, chunk, initial)
        mixed[here, :] = pick_heads(dm, acc * (1.0 / mass))
        norms = top + jnp.log(mass)
        for k in range(dm.hl):
            lse[k, here, :] = norms[k * tq : (k + 1) * tq]
        return carry

    lax.fori_loop(0, dm.rows // tq, tile, 0)
    unsort_rows(dm, meta, mixed, heads, 0)


def attend_section(k, blocks, meta):
    dm = k.dm
    shape = (dm.nc, dm.t, dm.w)
    saved, bufs = k.section(
        functools.partial(attend_body, dm),
        [(meta, "s"), (blocks, "v")],
        [sds((dm.rows, 3 * dm.w), BF16), sds((dm.hl, dm.rows, 1), F32), sds((dm.rows, dm.w), F32)],
        [pltpu.VMEM(shape, BF16)],
        8 * dm.rows * dm.rows * dm.w,
    )
    heads = send_blocks(dm, bufs[0], shape)
    k.start([heads])
    return saved, heads


def attend_back_body(dm, *refs):
    nc, w = dm.nc, dm.w
    meta, packed, lse, mixed, grads, blocks, dmix, dq, dk, dv = refs
    cuts = (meta[2], meta[3])
    tq, tk = min(TQ, dm.rows), min(TK, dm.rows)
    scale = HEAD_DIM**-0.5
    sort_rows(dm, meta, grads, dmix)
    dk[...] = jnp.zeros_like(dk)
    dv[...] = jnp.zeros_like(dv)

    def tile(t, carry):
        here = pl.ds(mult(t * tq, tq), tq)
        q = stack_heads(dm, packed[here, :w], scale)
        do = stack_heads(dm, dmix[here, :])
        o = jnp.concatenate([mixed[here, :]] * dm.hl, axis=0)
        delta = jnp.sum(do.astype(F32) * o, axis=1, keepdims=True)
        norms = jnp.concatenate([lse[k, here, :] for k in range(dm.hl)], axis=0)
        row, start = tile_rows(dm, t, tq, cuts)

        def chunk(kb, acc):
            there = pl.ds(mult(kb * tk, tk), tk)
            col = kb * tk + lax.broadcasted_iota(jnp.int32, (1, tk), 1)
            keys = packed[there, w : 2 * w]
            s = jnp.where((col <= row) & (col >= start), nt(q, keys), NEG)
            p = jnp.exp(s - norms)
            dp = nt(do, packed[there, 2 * w :])
            ds = (p * (dp - delta)).astype(BF16)
            dv[there, :] += tn(p.astype(BF16), do)
            dk[there, :] += tn(ds, q)
            return acc + nn(ds, keys)

        acc = lax.fori_loop(
            0, ((t + 1) * tq + tk - 1) // tk, chunk, jnp.zeros((dm.hl * tq, w), F32)
        )
        dq[here, :] = pick_heads(dm, acc) * scale
        return carry

    lax.fori_loop(0, dm.rows // tq, tile, 0)
    for at, src in enumerate((dq, dk, dv)):
        unsort_rows(dm, meta, src, blocks, at * w)


def attend_back_section(k, saved, grads, meta):
    dm = k.dm
    shape = (dm.nc, dm.t, 3 * dm.w)
    _, bufs = k.section(
        functools.partial(attend_back_body, dm),
        [(meta, "s")] + [(a, "v") for a in saved] + [(grads, "v")],
        [],
        [pltpu.VMEM(shape, BF16), pltpu.VMEM((dm.rows, dm.w), BF16)]
        + [pltpu.VMEM((dm.rows, dm.w), F32)] * 3,
        16 * dm.rows * dm.rows * dm.w,
    )
    blocks = send_blocks(dm, bufs[0], shape)
    k.start([blocks])
    return blocks


def top_body(dm, h, cot, small, result, dh, low, g_gain, g_shift):
    gain = small_vec(dm, small, "gf")
    v = h[...]
    result[...] = norm(v, gain, small_vec(dm, small, "sf")).astype(BF16)
    dv, g_gain[...], g_shift[...] = norm_back(v, gain, cot[...].astype(F32))
    dh[...] = dv
    low[...] = dv.astype(BF16)


def top_section(k, h, cot, small):
    dm = k.dm
    td, vec = (dm.t, dm.d), sds((1, dm.d), F32)
    return k.section(
        functools.partial(top_body, dm),
        [(h, "v"), (cot, "v"), (small, "v")],
        [sds(td, BF16), sds(td, F32), sds(td, BF16), vec, vec],
        [],
        20 * dm.t * dm.d,
    )[0]


def out_back_body(dm, layer, *refs):
    nc = dm.nc
    meta, gm, u, own = refs[:4]
    pieces = refs[4 : 4 + nc]
    du, sum_gm, sum_du = refs[4 + nc : 7 + nc]
    gr, own_buf, piece_buf, sems = refs[7 + nc :]
    c, f = lax.axis_index("ctx"), lax.axis_index("fsdp")
    weight = Pieces(dm, layer, own, pieces, own_buf, piece_buf, sems, None)
    weight.start()
    sum_gm[...] = col_sum(gm[...])
    for col in range(dm.ncs):
        at = mult((lax.rem(c, dm.ncs) ^ col) * dm.pc, dm.pc)
        gr[:, col * dm.pc : (col + 1) * dm.pc] = gm[:, pl.ds(at, dm.pc)]

    def finish(dact, at):
        at = pl.ds(mult(at, dm.pr), dm.pr)
        low = (dact * gelu_slope(u[:, at])).astype(BF16)
        du[:, at] = low
        sum_du[:, at] = col_sum(low)

    weight.wait_own()
    for g in range(nc // dm.ncs):
        finish(nt(gm[...], own_buf[g * dm.pr : (g + 1) * dm.pr, :]), f * dm.ffn + g * dm.pr)
    for g in range(nc // dm.ncs):
        for col in range(dm.ncs):
            weight.copies[g * dm.ncs + col].wait()
        for s in range(1, dm.nf):
            dact = None
            for col in range(dm.ncs):
                part = nt(gr[:, col * dm.pc : (col + 1) * dm.pc], piece_buf[g * dm.ncs + col, s - 1])
                dact = part if dact is None else dact + part
            finish(dact, ring(dm, f, s) * dm.ffn + ((c // dm.ncs) ^ g) * dm.pr)


def out_back_section(k, layer, gm, u, own, pieces, meta):
    dm = k.dm
    return k.section(
        functools.partial(out_back_body, dm, layer),
        [(meta, "s"), (gm, "v"), (u, "v"), (own, "a")] + [(p, "a") for p in pieces],
        [sds((dm.t, dm.ff), BF16), sds((1, dm.d), F32), sds((1, dm.ff), F32)],
        [("xr", pltpu.VMEM((dm.t, dm.d), BF16))] + piece_scratch(dm, (dm.ffn, dm.d)),
        2 * dm.t * dm.d * dm.ff,
    )[0]


def cols_back(dm, f, c, weight, dy, first, last, acc, out):
    weight.wait_own()
    acc[:, : dm.pr] = nt(dy[...], weight.own[...])
    acc[:, dm.pr :] = jnp.zeros((dm.t, dm.d - dm.pr), F32)
    for j in range(dm.nc):
        i = c ^ j

        def step():
            weight.copies[j].wait()
            at = pl.ds(mult((i - first) * dm.pc, dm.pc), dm.pc)
            acc[:, dm.pr :] += nt(dy[:, at], weight.flat(j))

        weight.each(j, step)
    for s in range(dm.nf):
        at = mult(ring(dm, f, s) * dm.pr, dm.pr)
        out[:, pl.ds(at, dm.pr)] = acc[:, s * dm.pr : (s + 1) * dm.pr].astype(out.dtype)


def fc_back_body(dm, layer, *refs):
    nc = dm.nc
    meta, du, dh, mid, small, own = refs[:6]
    pieces = refs[6 : 6 + nc]
    dmid, ga, sum_ga, g_gain, g_shift = refs[6 + nc : 11 + nc]
    acc, dn, own_buf, piece_buf, sems = refs[11 + nc :]
    c, f = lax.axis_index("ctx"), lax.axis_index("fsdp")
    weight = Pieces(dm, layer, own, pieces, own_buf, piece_buf, sems, None)
    weight.start()
    cols_back(dm, f, c, weight, du, 0, nc, acc, dn)
    dv, g_gain[...], g_shift[...] = norm_back(
        mid[...], small_vec(dm, small, "g2" + str(layer)), dn[...]
    )
    total = dh[...] + dv
    dmid[...] = total
    low = total.astype(BF16)
    ga[...] = low
    sum_ga[...] = col_sum(low)


def fc_back_section(k, layer, du, dh, mid, small, own, pieces, meta):
    dm = k.dm
    td, vec = (dm.t, dm.d), sds((1, dm.d), F32)
    return k.section(
        functools.partial(fc_back_body, dm, layer),
        [(meta, "s"), (du, "v"), (dh, "v"), (mid, "v"), (small, "v"), (own, "a")]
        + [(p, "a") for p in pieces],
        [sds(td, F32), sds(td, BF16), vec, vec, vec],
        [pltpu.VMEM(td, F32), pltpu.VMEM(td, F32)] + piece_scratch(dm, (dm.pr, dm.ff)),
        2 * dm.t * dm.d * dm.ff,
    )[0]


def proj_back_body(dm, layer, *refs):
    nc = dm.nc
    meta, ga, own = refs[:3]
    pieces = refs[3 : 3 + nc]
    acc, dob, blocks, own_buf, piece_buf, sems = refs[3 + nc :]
    c, f = lax.axis_index("ctx"), lax.axis_index("fsdp")
    weight = Pieces(dm, layer, own, pieces, own_buf, piece_buf, sems, lambda j: (c ^ j) >= dm.nq)
    weight.start()
    cols_back(dm, f, c, weight, ga, dm.nq, nc, acc, dob)
    for j in range(nc):
        blocks[j] = take_heads(dm, dob, 0, c ^ j)


def proj_back_section(k, layer, ga, own, pieces, meta):
    dm = k.dm
    td, shape = (dm.t, dm.d), (dm.nc, dm.t, dm.w)
    _, bufs = k.section(
        functools.partial(proj_back_body, dm, layer),
        [(meta, "s"), (ga, "v"), (own, "a")] + [(p, "a") for p in pieces],
        [],
        [pltpu.VMEM(td, F32), pltpu.VMEM(td, BF16), pltpu.VMEM(shape, BF16)]
        + piece_scratch(dm, (dm.pr, dm.d)),
        2 * dm.t * dm.d * dm.d,
    )
    blocks = send_blocks(dm, bufs[2], shape)
    k.start([blocks])
    return blocks


def qkv_back_body(dm, layer, *refs):
    nc = dm.nc
    meta, dmid, h, small, own, blocks = refs[:6]
    pieces = refs[6 : 6 + nc]
    dh, low, dqkv, sum_dqkv, g_gain, g_shift = refs[6 + nc : 12 + nc]
    acc, dn, own_buf, piece_buf, sems = refs[12 + nc :]
    blocks = [blocks.at[j] for j in range(nc)]
    c, f = lax.axis_index("ctx"), lax.axis_index("fsdp")
    weight = Pieces(dm, layer, own, pieces, own_buf, piece_buf, sems, lambda j: (c ^ j) < dm.nq)
    weight.start()
    for third in range(3):
        put_heads(dm, dqkv, third * dm.d, blocks, third * dm.w, c)
    sum_dqkv[...] = col_sum(dqkv[...])
    cols_back(dm, f, c, weight, dqkv, 0, dm.nq, acc, dn)
    dv, g_gain[...], g_shift[...] = norm_back(
        h[...].astype(F32), small_vec(dm, small, "g1" + str(layer)), dn[...]
    )
    total = dmid[...] + dv
    dh[...] = total
    low[...] = total.astype(BF16)


def qkv_back_section(k, layer, dmid, h, small, own, blocks, pieces, meta):
    dm = k.dm
    td, vec = (dm.t, dm.d), sds((1, dm.d), F32)
    return k.section(
        functools.partial(qkv_back_body, dm, layer),
        [(meta, "s"), (dmid, "v"), (h, "v"), (small, "v"), (own, "a"), (blocks, "v")]
        + [(p, "a") for p in pieces],
        [sds(td, F32), sds(td, BF16), sds((dm.t, 3 * dm.d), BF16), sds((1, 3 * dm.d), F32), vec, vec],
        [pltpu.VMEM(td, F32), pltpu.VMEM(td, F32)] + piece_scratch(dm, (dm.pr, 3 * dm.d)),
        2 * dm.t * dm.d * 3 * dm.d,
    )[0]


def sum_body(indices, *refs):
    n = len(indices)
    out, bufs, sems = refs[n], refs[n + 1 : 2 * n + 1], refs[2 * n + 1]
    copies = [
        pltpu.make_async_copy(at_of(ref, index), buf, sems.at[at])
        for at, (ref, index, buf) in enumerate(zip(refs, indices, bufs))
    ]
    for copy in copies:
        copy.start()
    for copy in copies:
        copy.wait()
    total = bufs[0][...].astype(F32)
    for buf in bufs[1:]:
        total = total + buf[...].astype(F32)
    out[...] = total.astype(out.dtype)


def sum_section(k, terms, shape, dtype=BF16, parts=None):
    bufs = [
        ("sum" + str((at, shape, dtype)), pltpu.VMEM(shape, dtype)) for at in range(len(terms))
    ]
    return k.section(
        functools.partial(sum_body, [index for _, index in terms]),
        [(src, "a") for src, _ in terms],
        [sds(shape, dtype)],
        bufs + [("sum" + str(len(terms)), pltpu.SemaphoreType.DMA((len(terms),)))],
        0,
    )[0][0]


def collect_body(dm, *refs):
    names, (table, _) = vector_names(), small_offsets(dm)
    for name, ref in zip(names, refs):
        at, size = table[name]
        for g in range(dm.nf):
            refs[-1][g, :, at : at + size] = ref[:, g * size : (g + 1) * size]


def grad_body(dm, kind, *refs):
    c, f = lax.axis_index("ctx"), lax.axis_index("fsdp")
    out, xt = refs[-2:]
    pairs = [refs[n : n + 2] for n in range(0, len(refs) - 2, 2)]
    lefts = pairs[: len(pairs) // 2]
    for n, pair in enumerate(lefts):
        depth = pair[0].shape[1]
        for half, ref in enumerate(pair):
            xt[n * depth : (n + 1) * depth, half * dm.t : (half + 1) * dm.t] = ref[...].T
    rights = pairs[len(pairs) // 2 :]

    def fill(t, row_base, row_step, pair, col):
        cols = pl.ds(mult(col * dm.pc, dm.pc), dm.pc)
        dy = jnp.concatenate([pair[0][:, cols], pair[1][:, cols]], axis=0)
        for s in range(dm.nf):
            at = mult(row_base + ring(dm, f, s) * row_step, dm.pr)
            out[t, s] = nn(xt[pl.ds(at, dm.pr), :], dy).astype(BF16)

    for t in reversed(range(dm.nc // 2)):
        i = c ^ (2 * t)
        if kind == "attn":
            pl.when(i < dm.nq)(lambda: fill(t, 0, dm.pr, rights[0], i))
            pl.when(i >= dm.nq)(lambda: fill(t, dm.d, dm.pr, rights[1], i - dm.nq))
        elif kind == "fc":
            fill(t, 0, dm.pr, rights[0], i)
        else:
            fill(t, (i // dm.ncs) * dm.pr, dm.ffn, rights[0], lax.rem(i, dm.ncs))


def grad_section(k, kind, lefts, rights):
    dm = k.dm
    depth = {"attn": 2 * dm.d, "fc": dm.d, "out": dm.ff}[kind]
    return k.section(
        functools.partial(grad_body, dm, kind),
        [(a, "v") for pair in lefts + rights for a in pair],
        [sds((dm.nc // 2, dm.nf, dm.pr, dm.pc), BF16)],
        [pltpu.VMEM((depth, 2 * dm.t), BF16)],
        2 * dm.t * dm.d * dm.ff,
    )[0][0]


def place_body(dm, *refs):
    nc = dm.nc
    jobs = [(layer, kind) for kind in ("out", "fc", "attn") for layer in reversed(range(LAYERS))]
    pieces = {job: refs[n * nc : (n + 1) * nc] for n, job in enumerate(jobs)}
    vector = refs[len(jobs) * nc]
    qkv, proj, fc, out = refs[len(jobs) * nc + 1 : len(jobs) * nc + 5]
    small = refs[len(jobs) * nc + 5 : -5]
    loads, wide, tall, load_sems, sems = refs[-5:]
    c = lax.axis_index("ctx")

    def fetch(n):
        return [
            pltpu.make_async_copy(pieces[jobs[n]][j], loads.at[n % 2, j], load_sems.at[n % 2, j])
            for j in range(nc)
        ]

    def store(n):
        layer, kind = jobs[n]
        buf, sem = (tall if kind == "out" else wide).at[n % 2], sems.at[n % 2]
        if kind == "attn":
            return [
                pltpu.make_async_copy(buf.at[:, pl.ds(0, 3 * dm.d)], qkv.at[layer], sem.at[0]),
                pltpu.make_async_copy(buf.at[:, pl.ds(3 * dm.d, dm.d)], proj.at[layer], sem.at[1]),
            ]
        return [pltpu.make_async_copy(buf, (out if kind == "out" else fc).at[layer], sem.at[0])]

    for copy in fetch(0):
        copy.start()
    for n, name in enumerate(vector_names()):
        at, size = small_offsets(dm)[0][name]
        row, ref = (n // len(SMALL), small[n % len(SMALL)])
        if row == LAYERS:
            row, ref = 0, small[len(SMALL) + n % len(SMALL)]
        ref[row : row + 1, :] = vector[:, at : at + size]
    for n in range(len(jobs)):
        if n + 1 < len(jobs):
            for copy in fetch(n + 1):
                copy.start()
        if n >= 2:
            for copy in store(n - 2):
                copy.wait()
        for copy in fetch(n):
            copy.wait()
        for j in range(nc):
            i = c ^ j
            v = loads[n % 2, j].astype(F32)
            if jobs[n][1] == "out":
                rows = pl.ds(mult((i // dm.ncs) * dm.pr, dm.pr), dm.pr)
                tall[n % 2, rows, pl.ds(mult(lax.rem(i, dm.ncs) * dm.pc, dm.pc), dm.pc)] = v
            else:
                wide[n % 2, :, pl.ds(mult(i * dm.pc, dm.pc), dm.pc)] = v
        for copy in store(n):
            copy.start()
    for n in (len(jobs) - 2, len(jobs) - 1):
        for copy in store(n):
            copy.wait()


def place_call(dm, done, vector):
    names = [k + str(layer) for k in ("o", "c", "a") for layer in reversed(range(LAYERS))]
    pieces = [p for name in names for p in done[name]]
    shapes = [(dm.pr, 3 * dm.d), (dm.pr, dm.d), (dm.pr, dm.ff), (dm.ffn, dm.d)]
    table = small_offsets(dm)[0]
    vectors = [(LAYERS, table[name + "0"][1]) for name, _ in SMALL] + [(1, dm.pr)] * 2
    return pl.pallas_call(
        functools.partial(place_body, dm),
        out_shape=[sds((LAYERS,) + shape, F32) for shape in shapes] + [sds(v, F32) for v in vectors],
        in_specs=[pl.BlockSpec(memory_space=pl.ANY)] * len(pieces) + [pl.BlockSpec(memory_space=pltpu.VMEM)],
        out_specs=[pl.BlockSpec(memory_space=pl.ANY)] * len(shapes)
        + [pl.BlockSpec(memory_space=pltpu.VMEM)] * len(vectors),
        scratch_shapes=[
            pltpu.VMEM((2, dm.nc, dm.pr, dm.pc), BF16),
            pltpu.VMEM((2, dm.pr, dm.ff), F32),
            pltpu.VMEM((2, dm.ffn, dm.d), F32),
            pltpu.SemaphoreType.DMA((2, dm.nc)),
            pltpu.SemaphoreType.DMA((2, 2)),
        ],
        compiler_params=pltpu.CompilerParams(vmem_limit_bytes=VMEM_BYTES),
    )(*pieces, vector)


def plane_bits(nc):
    bits = []
    bit = 2
    while bit < nc:
        bits.append(bit)
        bit *= 2
    return bits


def moving(moves):
    return lambda k: k.start(moves)


def spread(dm, first):
    bits = plane_bits(dm.nc)
    held = {0: first}
    if len(bits) == 2:
        one, two = bits
        held.update({bit: whole(first, ("ctx", bit)) for bit in (one, two, 1)})
        yield moving([held[one], held[two], held[1]])
        lead = (slice(None),) * (len(first.shape) - 2)
        cut = first.shape[-2] // 2
        low, high = lead + (pl.ds(0, cut),), lead + (pl.ds(cut, cut),)
        far = Move(
            first.shape, first.dtype,
            [([(None, held[two], low)], ("ctx", one), low), ([(None, held[one], high)], ("ctx", two), high)],
        )
        held[one ^ two] = far
        held.update({bit ^ 1: whole(held[bit], ("ctx", 1)) for bit in bits})
        yield moving([far, held[one ^ 1], held[two ^ 1]])
        held[one ^ two ^ 1] = whole(far, ("ctx", 1))
        yield moving([held[one ^ two ^ 1]])
    else:
        for bit in bits + [1]:
            new = {j ^ bit: whole(v, ("ctx", bit)) for j, v in held.items()}
            yield moving(list(new.values()))
            held.update(new)
    return [held[j] for j in range(dm.nc)]


def gather(dm, source):
    others = Move(
        (dm.nf - 1, dm.pr, dm.pc), BF16,
        [(source, ("fsdp", s), (s - 1,)) for s in range(1, dm.nf)],
    )
    yield moving([others])
    return (yield from spread(dm, others))


def plane_sum(dm, terms):
    bits = plane_bits(dm.nc)
    if len(bits) == 2:
        one, two = bits
        cut = dm.pr // 2
        shape = (dm.nf, cut, dm.pc)

        def part(t, first):
            return (t, slice(None), pl.ds(first, cut))

        def send(t, first, bit):
            return Move(shape, BF16, [([(None, terms, part(t, first))], ("ctx", bit), None)])

        far_x, own_x = send(3, 0, one), send(1, 0, one)
        far_y, own_y = send(3, cut, two), send(2, cut, two)
        yield moving([far_x, far_y, own_x, own_y])
        near = []

        def second(k):
            x = sum_section(k, [(terms, part(1, cut)), (far_y, None)], shape)
            near.append(whole(x, ("ctx", one)))
            k.start(near[:1])
            y = sum_section(k, [(terms, part(2, 0)), (far_x, None)], shape)
            near.append(whole(y, ("ctx", two)))
            k.start(near[1:])

        yield second
        return [
            [(terms, part(0, 0)), (own_x, None), (near[1], None)],
            [(terms, part(0, cut)), (near[0], None), (own_y, None)],
        ]
    at, index = terms, ()
    count = dm.nc // 2
    for n, _ in enumerate(bits):
        count //= 2
        shape = (count, dm.nf, dm.pr, dm.pc)
        away = Move(shape, BF16, [([(None, at, (pl.ds(count, count),))], ("ctx", bits[-1 - n]), None)])
        yield moving([away])
        if count > 1:
            made = []

            def add(k):
                made.append(sum_section(k, [(at, (pl.ds(0, count),)), (away, None)], shape))

            yield add
            at = made[0]
    return [[(at, (0,)), (away, (0,))]]


def reduce(dm, terms):
    parts = yield from plane_sum(dm, terms)
    rows = dm.pr // len(parts)
    totals = []
    others = []

    def along(k):
        for n, part in enumerate(parts):
            totals.append(sum_section(k, part, (dm.nf, rows, dm.pc)))
            others.append(
                Move(
                    (dm.nf - 1, rows, dm.pc), BF16,
                    [
                        ([(None, totals[n], (s,))], ("fsdp", dm.nf - s), (s - 1,))
                        for s in range(1, dm.nf)
                    ],
                )
            )
            k.start(others[n:])

    yield along
    mine = []

    def join(k):
        def body(*refs):
            out = refs[-1]
            for n in range(len(parts)):
                out[n * rows : (n + 1) * rows, :] = refs[n][...]

        sums = [
            sum_section(
                k, [(totals[n], (0,))] + [(others[n], (s,)) for s in range(dm.nf - 1)], (rows, dm.pc)
            )
            for n in range(len(parts))
        ]
        mine.append(k.section(body, [(v, "v") for v in sums], [sds((dm.pr, dm.pc), BF16)], [], 0)[0][0])

    stages = spread_later(dm, mine, join)
    return (yield from stages)


def spread_later(dm, mine, join):
    inner = None

    def first(k):
        nonlocal inner
        join(k)
        inner = spread(dm, mine[0])
        next(inner)(k)

    yield first
    return (yield from inner)


def reduce_small(dm, total):
    n = total.shape[-1]
    row = lambda s: (lambda: (ring(dm, lax.axis_index("fsdp"), s),))
    bit = 1
    state = [total]
    while bit < dm.nc:

        def step(k):
            other = whole(state[-1], ("ctx", bit))
            k.start([other])
            state.append(other)

        def add(k):
            other = state.pop()
            state.append(sum_section(k, [(state[-1], None), (other, None)], total.shape, F32))

        yield step
        yield add
        bit *= 2
    total = state[-1]
    others = Move(
        (dm.nf - 1, 1, n), F32,
        [([(None, total, row(s))], ("fsdp", dm.nf - s), (s - 1,)) for s in range(1, dm.nf)],
    )
    yield moving([others])
    made = []

    def last(k):
        terms = [(total, row(0))] + [(others, (s,)) for s in range(dm.nf - 1)]
        made.append(sum_section(k, terms, (1, n), F32))

    yield last
    return made[0]


class Flow:
    def __init__(self, dm):
        self.dm, self.live, self.done = dm, {}, {}
        self.ids = itertools.count()

    def kernel(self, *names):
        k = Kernel(self.dm, self.ids)
        self.go(k, *names)
        return k

    def add(self, name, transfer):
        self.live[name] = transfer

    def go(self, k, *names):
        for name in names:
            if name in self.live:
                try:
                    next(self.live[name])(k)
                except StopIteration as stop:
                    self.done[name] = stop.value
                    del self.live[name]

    def finish(self, k, name):
        while name in self.live:
            self.go(k, name)
        return self.done[name]


def local(acts, cotangent, pair_slots, segments, *tensors):
    (
        attn_gain, attn_shift, qkv_weight, qkv_bias, proj_weight, proj_bias, mlp_gain, mlp_shift,
        fc_weight, fc_bias, out_weight, out_bias, final_gain, final_shift,
    ) = tensors
    nf, nc = lax.axis_size("fsdp"), lax.axis_size("ctx")
    dm = dims_of(acts, fc_weight, nf, nc)
    c, f = lax.axis_index("ctx"), lax.axis_index("fsdp")
    small_size = small_offsets(dm)[1]

    seg = segments[0]
    cut_one = jnp.sum((seg == 0).astype(jnp.int32))
    cut_two = cut_one + jnp.sum((seg == 1).astype(jnp.int32))
    index = jnp.arange(nc, dtype=jnp.int32)
    others = jnp.bitwise_xor(c, index)
    lows = jnp.sum(jnp.where(others[:, None] == index[None, :], pair_slots[None, :], 0), axis=1)
    slots = jnp.sum(jnp.where(lows[None, :] == index[:, None], index[None, :], 0), axis=1)
    meta = jnp.concatenate([jnp.stack([c, f, cut_one, cut_two]).astype(jnp.int32), lows, slots])

    def source(kind, layer):
        def cols(first, last):
            at = jnp.clip(lax.axis_index("ctx"), first, last - 1) - first
            return (layer, pl.ds(0, dm.pr), pl.ds(mult(at * dm.pc, dm.pc), dm.pc))

        def place():
            at = lax.axis_index("ctx")
            row, col = (at // dm.ncs) * dm.pr, lax.rem(at, dm.ncs) * dm.pc
            return (layer, pl.ds(mult(row, dm.pr), dm.pr), pl.ds(mult(col, dm.pc), dm.pc))

        if kind == "attn":
            return [
                (lambda: lax.axis_index("ctx") < dm.nq, qkv_weight, lambda: cols(0, dm.nq)),
                (lambda: lax.axis_index("ctx") >= dm.nq, proj_weight, lambda: cols(dm.nq, nc)),
            ]
        if kind == "fc":
            return [(None, fc_weight, lambda: cols(0, nc))]
        return [(None, out_weight, place)]

    per_layer = (attn_gain, attn_shift, qkv_bias, proj_bias, mlp_gain, mlp_shift, fc_bias, out_bias)
    parts = [p[layer] for layer in range(LAYERS) for p in per_layer] + [final_gain, final_shift]
    packed = jnp.concatenate(parts).reshape(small_size // 128, 128)
    small_move = Move(
        (nf - 1,) + packed.shape, BF16,
        [([(None, packed, None)], ("fsdp", s), (s - 1,)) for s in range(1, nf)],
    )

    def other_core(v):
        return whole(v, ("ctx", 1))

    flow = Flow(dm)
    for layer in range(LAYERS):
        for kind, name in (("attn", "A"), ("fc", "C"), ("out", "O")):
            flow.add(name + str(layer), gather(dm, source(kind, layer)))

    k = flow.kernel()
    k.start([small_move])
    flow.go(k, "A0", "A0", "C0", "A0", "C0", "O0")
    flow.finish(k, "A0")
    k.run()
    backwards = jnp.concatenate([packed[None], value(small_move)])[::-1]
    small = lax.dynamic_slice_in_dim(jnp.concatenate([backwards, backwards]), nf - 1 - f, nf)
    small = small.reshape(nf, small_size).astype(F32)

    h = acts[0]
    kept = []
    k = flow.kernel("C0", "O0", "A1")
    n1, blocks = qkv_section(k, 0, h, small, qkv_weight, flow.done["A0"], meta)
    flow.go(k, "C0")
    k.run()
    vectors = {}
    for layer in range(LAYERS):
        tag, nxt = str(layer), str(layer + 1)
        last = layer + 1 == LAYERS
        twin = [other_core(n1)]
        k = flow.kernel("O" + tag, "A" + nxt, "C" + nxt) if not last else flow.kernel("C" + tag, "O" + tag)
        k.start(twin)
        saved, heads = attend_section(k, blocks, meta)
        flow.go(k, "C" + tag if last else "O" + tag)
        k.run()
        k = flow.kernel("A" + nxt, "O" + nxt, "C" + nxt) if not last else flow.kernel("O" + tag)
        attn = flow.done["A" + tag]
        ob, mid, n2 = proj_section(k, layer, h, small, proj_weight, heads, attn, meta)
        twin += [other_core(ob), other_core(n2)]
        k.start(twin[1:])
        u, act = fc_section(k, layer, n2, small, fc_weight, flow.finish(k, "C" + tag), meta)
        twin.append(other_core(act))
        k.start(twin[3:])
        nxt_h = out_section(k, layer, mid, act, small, out_weight, flow.finish(k, "O" + tag), meta)
        kept.append((h, n1, saved, ob, mid, n2, u, act, twin))
        h = nxt_h
        if not last:
            n1, blocks = qkv_section(k, layer + 1, h, small, qkv_weight, flow.finish(k, "A" + nxt), meta)
            k.run()

    weights = flow.done
    result, dh, gm, vectors["gf"], vectors["sf"] = top_section(k, h, cotangent[0], small)

    for layer in reversed(range(LAYERS)):
        tag, nxt = str(layer), str(layer + 1)
        o_, a_, k_ = "o" + nxt, "a" + nxt, "c" + nxt
        o, a, ck = "o" + tag, "a" + tag, "c" + tag
        h, n1, saved, ob, mid, n2, u, act, (n1_, ob_, n2_, act_) = kept[layer]
        gm_ = other_core(gm)
        k.start([gm_])
        du, vectors["bo" + tag], vectors["bf" + tag] = out_back_section(
            k, layer, gm, u, out_weight, weights["O" + tag], meta
        )
        flow.go(k, k_, k_)
        k.run()
        du_ = other_core(du)
        k = flow.kernel()
        k.start([du_])
        flow.go(k, a_)
        flow.add(o, reduce(dm, grad_section(k, "out", [(act, act_)], [(gm, gm_)])))
        flow.go(k, o)
        dmid, ga, vectors["bp" + tag], vectors["g2" + tag], vectors["s2" + tag] = fc_back_section(
            k, layer, du, dh, mid, small, fc_weight, weights["C" + tag], meta
        )
        k.run()
        k = flow.kernel(a_, o)
        ga_ = other_core(ga)
        k.start([ga_])
        grads = proj_back_section(k, layer, ga, proj_weight, weights["A" + tag], meta)
        flow.add(ck, reduce(dm, grad_section(k, "fc", [(n2, n2_)], [(du, du_)])))
        flow.go(k, ck)
        k.run()
        k = flow.kernel(o, ck, a_)
        blocks = attend_back_section(k, saved, grads, meta)
        flow.go(k, a_)
        k.run()
        k = flow.kernel(o, ck, a_)
        dh, gm, dqkv, vectors["bq" + tag], vectors["g1" + tag], vectors["s1" + tag] = qkv_back_section(
            k, layer, dmid, h, small, qkv_weight, blocks, weights["A" + tag], meta
        )
        dqkv_ = other_core(dqkv)
        k.start([dqkv_])
        flow.go(k, o, o)
        k.run()
        k = flow.kernel(ck)
        if layer == 0:
            shape = (nf, 1, small_size)
            rows = k.section(
                functools.partial(collect_body, dm),
                [(vectors[name], "v") for name in vector_names()],
                [sds(shape, F32)],
                [],
                0,
            )[0][0]
            flow.add("small", reduce_small(dm, rows))
            flow.go(k, "small")
        flow.add(
            a,
            reduce(dm, grad_section(k, "attn", [(n1, n1_), (ob, ob_)], [(dqkv, dqkv_), (ga, ga_)])),
        )
        flow.go(k, a)

    flow.go(k, "c0", "small", "small", "c0", "a0", "small", "small", "a0", "small", "small")
    for name in ("a1", "c1", "o1", "c0", "o0", "a0"):
        flow.finish(k, name)
    mine = flow.finish(k, "small")
    k.run()
    done = {name: [value(v) for v in flow.done[name]] for name in ("o0", "c0", "a0", "o1", "c1", "a1")}
    grads = place_call(dm, done, value(mine))
    qkv_grad, proj_grad, fc_grad, out_grad, g1, s1, bq, bp, g2, s2, bf, bo, gf, sf = grads
    return (
        value(result)[None], value(gm)[None], g1, s1, qkv_grad, bq, proj_grad, bp, g2, s2, fc_grad, bf,
        out_grad, bo, gf.reshape(-1), sf.reshape(-1),
    )


def solution(mesh):
    row = P("fsdp", "ctx", None)
    vec, mat = P(None, "fsdp"), P(None, "fsdp", None)
    tensors = (vec, vec, mat, vec, mat, vec, vec, vec, mat, vec, mat, vec, P("fsdp"), P("fsdp"))
    return jax.shard_map(
        local,
        mesh=mesh,
        in_specs=(row, row, P(), P("fsdp", None)) + tensors,
        out_specs=(row, row) + tensors,
        check_vma=False,
    )
```

time: 990 us -> 858 us (0.87)
  other arithmetic: 89.4 us -> 3.16 us
  Pallas kernels: 870 us -> 830 us
    convert_element_type x12 -> x0, other arithmetic: 40.4 us -> none  [moved(): return whole(v.astype(BF16), ('ctx', bit))]
    pallas_call x41 -> x17, Pallas kernels: 870 us -> 830 us  [the longest x16 815 us: run(): pl.pallas_call(kernel, out_shape=self.outs, in_specs=self.in_specs, out_s...]
    another operation x13 -> x0, other arithmetic: 15.6 us -> none
    pallas_call x18 -> x0, other arithmetic: 12 us -> none  [run(): pl.pallas_call(kernel, out_shape=outs, in_specs=specs, out_specs=out_spec...]
    add x10 -> x0, other arithmetic: 10.5 us -> none  [the longest x6 8.4 us: reduce(): mine = mine + value(others)[s - 1].astype(F32)]
where the time goes in v2:
time: 858 us; the launch traced here: 850 us
  Pallas kernels  830 us (97%)
  local copies, waits for them, and re-layouts  15.1 us (2%)
    pallas_call x16, Pallas kernels, run(): pl.pallas_call(kernel, out_shape=self.outs, in_specs=self.in_specs, out_s...  815 us

profile of v2, /device:TPU:0, one launch (start us, length us, event | category | flops | bytes accessed | tf_op | source)
XLA Modules:
  0.0 850.4 jit_solution(16999215972318938967)
XLA Ops:
  0.7 0.8 select_reduce_fusion.1
  1.6 1.4 fusion.2
  4.3 1.2 concatenate.13.refs_5_.refs_4_.refs_2_.refs_8_.refs_9_.refs_13_.refs_12_.refs_10_
  11.0 0.8 slice_reduce_fusion
  14.9 0.8 dynamic-update-slice.16
  15.7 0.8 dynamic-update-slice.17
  17.1 71.0 %shard_map.297 = (bf16[3,56,128]{2,1,0:T(8,128)(2,1)}, bf16[3,256,512]{2,1,0:T(8,128)(2,1)}, bf16[3,256,512]{2,1,0:T(8,128)(2,1)}, bf16[3,256,512]{2,1,0:T(8,128...) custom-call(bf16[56,128]{1,0:T(8,128)(2,1)} %bitcast.30, ...), custom_call_target="tpu_custom_call" | custom-call | bytes 22863872 | tf_op jit(solution)/shard_map/pallas_call | solution.py:289
  89.7 53.1 %shard_map.298 = (bf16[3,256,512]{2,1,0:T(8,128)(2,1)}, bf16[3,256,512]{2,1,0:T(8,128)(2,1)}, bf16[3,256,512]{2,1,0:T(8,128)(2,1)}, bf16[3,256,512]{2,1,0:T(8,12...) custom-call(bf16[3,256,512]{2,1,0:T(8,128)(2,1)} %get-tuple-element., ...), custom_call_target="tpu_custom_call" | custom-call | flops 1610612736 | bytes 21872720 | tf_op jit(solution)/shard_map/pallas_call | solution.py:289
  142.8 41.0 %shard_map.299 = (bf16[3,256,512]{2,1,0:T(8,128)(2,1)}, bf16[3,256,512]{2,1,0:T(8,128)(2,1)}, bf16[3,256,512]{2,1,0:T(8,128)(2,1)}, bf16[3,256,512]{2,1,0:T(8,12...) custom-call(bf16[3,256,512]{2,1,0:T(8,128)(2,1)} %get-tuple-element., ...), custom_call_target="tpu_custom_call" | custom-call | flops 4294967296 | bytes 18628688 | tf_op jit(solution)/shard_map/pallas_call | solution.py:289
  183.8 51.6 %shard_map.300 = (bf16[3,256,512]{2,1,0:T(8,128)(2,1)}, bf16[3,256,512]{2,1,0:T(8,128)(2,1)}, bf16[3,256,512]{2,1,0:T(8,128)(2,1)}, bf16[3,256,512]{2,1,0:T(8,12...) custom-call(bf16[3,256,512]{2,1,0:T(8,128)(2,1)} %get-tuple-element., ...), custom_call_target="tpu_custom_call" | custom-call | flops 6442450944 | bytes 57524304 | tf_op jit(solution)/shard_map/pallas_call | solution.py:289
  235.4 38.6 %shard_map.301 = (bf16[3,256,512]{2,1,0:T(8,128)(2,1)}, bf16[3,256,512]{2,1,0:T(8,128)(2,1)}, bf16[3,256,512]{2,1,0:T(8,128)(2,1)}, bf16[3,256,512]{2,1,0:T(8,12...) custom-call(bf16[3,256,512]{2,1,0:T(8,128)(2,1)} %get-tuple-element., ...), custom_call_target="tpu_custom_call" | custom-call | flops 4294967296 | bytes 13647952 | tf_op jit(solution)/shard_map/pallas_call | solution.py:289
  274.0 34.0 %shard_map.302 = (bf16[3,256,512]{2,1,0:T(8,128)(2,1)}, bf16[3,256,512]{2,1,0:T(8,128)(2,1)}, bf16[3,256,512]{2,1,0:T(8,128)(2,1)}, bf16[256,1024]{1,0:T(8,128)(...) custom-call(bf16[3,256,512]{2,1,0:T(8,128)(2,1)} %get-tuple-element., ...), custom_call_target="tpu_custom_call" | custom-call | flops 6984564736 | bytes 47853648 | tf_op jit(solution)/shard_map/pallas_call | solution.py:289
  308.0 37.1 %shard_map.303 = (bf16[256,4096]{1,0:T(8,128)(2,1)}, bf16[4,4,256,512]{3,2,1,0:T(8,128)(2,1)}, bf16[4,128,512]{2,1,0:T(8,128)(2,1)}, bf16[4,128,512]{2,1,0:T(8,1...) custom-call(bf16[256,4096]{1,0:T(8,128)(2,1)} %get-tuple-element.306, ...), custom_call_target="tpu_custom_call" | custom-call | flops 4294967296 | bytes 32108624 | tf_op jit(solution)/shard_map/pallas_call | solution.py:289
  345.1 51.5 %shard_map.304 = (bf16[4,128,512]{2,1,0:T(8,128)(2,1)}, bf16[4,128,512]{2,1,0:T(8,128)(2,1)}, bf16[4,128,512]{2,1,0:T(8,128)(2,1)}, bf16[4,128,512]{2,1,0:T(8,12...) custom-call(bf16[4,4,256,512]{3,2,1,0:T(8,128)(2,1)} %get-tuple-elem, ...), custom_call_target="tpu_custom_call" | custom-call | flops 2684354560 | bytes 28311632 | tf_op jit(solution)/shard_map/pallas_call | solution.py:289
  396.6 60.9 %shard_map.305 = (bf16[4,128,512]{2,1,0:T(8,128)(2,1)}, bf16[3,128,512]{2,1,0:T(8,128)(2,1)}, bf16[4,128,512]{2,1,0:T(8,128)(2,1)}, bf16[3,128,512]{2,1,0:T(8,12...) custom-call(bf16[4,4,256,512]{3,2,1,0:T(8,128)(2,1)} %get-tuple-elem, ...), custom_call_target="tpu_custom_call" | custom-call | flops 8589934592 | bytes 20201552 | tf_op jit(solution)/shard_map/pallas_call | solution.py:289
  457.5 36.1 %shard_map.306 = (bf16[128,512]{1,0:T(8,128)(2,1)}, bf16[128,512]{1,0:T(8,128)(2,1)}, bf16[256,512]{1,0:T(8,128)(2,1)}, bf16[256,512]{1,0:T(8,128)(2,1)}, bf16[2...) custom-call(bf16[4,128,512]{2,1,0:T(8,128)(2,1)} %get-tuple-element., ...), custom_call_target="tpu_custom_call" | custom-call | flops 1610612736 | bytes 30281808 | tf_op jit(solution)/shard_map/pallas_call | solution.py:289
  493.6 44.7 %shard_map.307 = (bf16[128,512]{1,0:T(8,128)(2,1)}, bf16[128,512]{1,0:T(8,128)(2,1)}, bf16[256,512]{1,0:T(8,128)(2,1)}, bf16[256,512]{1,0:T(8,128)(2,1)}, bf16[2...) custom-call(bf16[4,128,512]{2,1,0:T(8,128)(2,1)} %get-tuple-element., ...), custom_call_target="tpu_custom_call" | custom-call | flops 4294967296 | bytes 35147856 | tf_op jit(solution)/shard_map/pallas_call | solution.py:289
  538.3 46.4 %shard_map.308 = (bf16[256,4096]{1,0:T(8,128)(2,1)}, bf16[4,128,512]{2,1,0:T(8,128)(2,1)}, bf16[4,128,512]{2,1,0:T(8,128)(2,1)}, bf16[4,128,512]{2,1,0:T(8,128)(...) custom-call(bf16[256,4096]{1,0:T(8,128)(2,1)} %get-tuple-element.353, ...), custom_call_target="tpu_custom_call" | custom-call | flops 4294967296 | bytes 39448656 | tf_op jit(solution)/shard_map/pallas_call | solution.py:289
  584.7 54.8 %shard_map.309 = (bf16[4,128,512]{2,1,0:T(8,128)(2,1)}, bf16[3,128,512]{2,1,0:T(8,128)(2,1)}, bf16[4,128,512]{2,1,0:T(8,128)(2,1)}, bf16[3,128,512]{2,1,0:T(8,12...) custom-call(bf16[4,4,256,512]{3,2,1,0:T(8,128)(2,1)} %get-tuple-elem, ...), custom_call_target="tpu_custom_call" | custom-call | flops 2684354560 | bytes 36438096 | tf_op jit(solution)/shard_map/pallas_call | solution.py:289
  639.5 66.9 %shard_map.310 = (bf16[4,128,512]{2,1,0:T(8,128)(2,1)}, bf16[3,128,512]{2,1,0:T(8,128)(2,1)}, bf16[4,128,512]{2,1,0:T(8,128)(2,1)}, bf16[3,128,512]{2,1,0:T(8,12...) custom-call(bf16[4,4,256,512]{3,2,1,0:T(8,128)(2,1)} %get-tuple-elem, ...), custom_call_target="tpu_custom_call" | custom-call | flops 8589934592 | bytes 24133712 | tf_op jit(solution)/shard_map/pallas_call | solution.py:289
  706.4 34.2 %shard_map.311 = (bf16[128,512]{1,0:T(8,128)(2,1)}, bf16[128,512]{1,0:T(8,128)(2,1)}, bf16[256,512]{1,0:T(8,128)(2,1)}, bf16[256,512]{1,0:T(8,128)(2,1)}, bf16[2...) custom-call(bf16[4,128,512]{2,1,0:T(8,128)(2,1)} %get-tuple-element., ...), custom_call_target="tpu_custom_call" | custom-call | flops 1610612736 | bytes 30281808 | tf_op jit(solution)/shard_map/pallas_call | solution.py:289
  740.6 93.5 %shard_map.312 = (bf16[128,512]{1,0:T(8,128)(2,1)}, bf16[128,512]{1,0:T(8,128)(2,1)}, bf16[256,512]{1,0:T(8,128)(2,1)}, bf16[256,512]{1,0:T(8,128)(2,1)}, bf16[2...) custom-call(bf16[4,128,512]{2,1,0:T(8,128)(2,1)} %get-tuple-element., ...), custom_call_target="tpu_custom_call" | custom-call | flops 2147483648 | bytes 24100864 | tf_op jit(solution)/shard_map/pallas_call | solution.py:289
  834.1 14.5 %shard_map.313 = (f32[2,256,3072]{2,1,0:T(8,128)}, f32[2,256,1024]{2,1,0:T(8,128)}, f32[2,256,4096]{2,1,0:T(8,128)}, f32[2,1024,1024]{2,1,0:T(8,128)}, f32[2,256...) custom-call(bf16[256,512]{1,0:T(8,128)(2,1)} %get-tuple-element.400., ...), custom_call_target="tpu_custom_call" | custom-call | tf_op jit(solution)/shard_map/pallas_call | solution.py:1039
  848.6 0.8 copy.57
  (37 shorter events, 11.6 us)
Async XLA Ops:
  16.5 0.6 copy-start.2
  834.0 14.5 %copy-start = (bf16[256,1024]{1,0:T(8,128)(2,1)S(1)}, bf16[256,1024]{1,0:T(8,128)(2,1)}, u32[]{:S(2)}) copy-start(bf16[256,1024]{1,0:T(8,128)(2,1)} %get-tuple-element.305) | copy-start | bytes 1572868
  834.1 15.3 %copy-start.1 = (bf16[256,1024]{1,0:T(8,128)(2,1)S(1)}, bf16[256,1024]{1,0:T(8,128)(2,1)}, u32[]{:S(2)}) copy-start(bf16[256,1024]{1,0:T(8,128)(2,1)} %get-tuple-element.399) | copy-start | bytes 1572868

commit v3 on v2

--- a/solution.py
+++ b/solution.py
@@ -17,7 +17,7 @@
 LOW = -1e29
 F32 = jnp.float32
 BF16 = jnp.bfloat16
-VMEM_BYTES = 56 * 1024 * 1024
+VMEM_BYTES = 60 * 1024 * 1024
 
 FIELDS = ("t", "d", "ff", "nf", "nc", "pr", "pc", "nq", "ncs", "ffn", "w", "hl", "rows", "half")
 Dims = collections.namedtuple("Dims", FIELDS)
@@ -152,7 +152,7 @@
 
     def operand(self, a, place):
         if isinstance(a, (Slot, Move)) and a.result is None:
-            return a
+            return self.load(a) if isinstance(a, Move) and place == "v" else a
         a = value(a)
         key = (id(a), place)
         if key not in self.slots:
@@ -161,6 +161,21 @@
             self.arrays.append(a)
             self.in_specs.append(pl.BlockSpec(memory_space=spaces[place]))
         return self.slots[key]
+
+    def load(self, move):
+        key = ("load", id(move))
+        if key not in self.keys:
+            self.keys[key] = Slot("scratch", len(self.scratch), move)
+            self.scratch.append(pltpu.VMEM(move.shape, move.dtype))
+            sem = self.buffer(("load", pltpu.SemaphoreType.DMA))
+
+            def body(src, dst, sem):
+                copy = pltpu.make_async_copy(src, dst, sem)
+                copy.start()
+                copy.wait()
+
+            self.steps.append(("body", body, [move, self.keys[key], sem]))
+        return self.keys[key]
 
     def output(self, out, space):
         slot = Slot("out", len(self.outs), out)
@@ -824,7 +839,7 @@
         [(meta, "s"), (du, "v"), (dh, "v"), (mid, "v"), (small, "v"), (own, "a")]
         + [(p, "a") for p in pieces],
         [sds(td, F32), sds(td, BF16), vec, vec, vec],
-        [pltpu.VMEM(td, F32), pltpu.VMEM(td, F32)] + piece_scratch(dm, (dm.pr, dm.ff)),
+        [("acc", pltpu.VMEM(td, F32)), ("dn", pltpu.VMEM(td, F32))] + piece_scratch(dm, (dm.pr, dm.ff)),
         2 * dm.t * dm.d * dm.ff,
     )[0]
 
@@ -849,7 +864,7 @@
         functools.partial(proj_back_body, dm, layer),
         [(meta, "s"), (ga, "v"), (own, "a")] + [(p, "a") for p in pieces],
         [],
-        [pltpu.VMEM(td, F32), pltpu.VMEM(td, BF16), pltpu.VMEM(shape, BF16)]
+        [("acc", pltpu.VMEM(td, F32)), pltpu.VMEM(td, BF16), pltpu.VMEM(shape, BF16)]
         + piece_scratch(dm, (dm.pr, dm.d)),
         2 * dm.t * dm.d * dm.d,
     )
@@ -888,7 +903,7 @@
         [(meta, "s"), (dmid, "v"), (h, "v"), (small, "v"), (own, "a"), (blocks, "v")]
         + [(p, "a") for p in pieces],
         [sds(td, F32), sds(td, BF16), sds((dm.t, 3 * dm.d), BF16), sds((1, 3 * dm.d), F32), vec, vec],
-        [pltpu.VMEM(td, F32), pltpu.VMEM(td, F32)] + piece_scratch(dm, (dm.pr, 3 * dm.d)),
+        [("acc", pltpu.VMEM(td, F32)), ("dn", pltpu.VMEM(td, F32))] + piece_scratch(dm, (dm.pr, 3 * dm.d)),
         2 * dm.t * dm.d * 3 * dm.d,
     )[0]
 
@@ -923,6 +938,13 @@
     )[0][0]
 
 
+def small_body(dm, packed, others, out):
+    f = lax.axis_index("fsdp")
+    out[pl.ds(f, 1), :] = packed[...]
+    for s in range(1, dm.nf):
+        out[pl.ds(ring(dm, f, s), 1), :] = others[s - 1]
+
+
 def collect_body(dm, *refs):
     names, (table, _) = vector_names(), small_offsets(dm)
     for name, ref in zip(names, refs):
@@ -962,12 +984,11 @@
 
 def grad_section(k, kind, lefts, rights):
     dm = k.dm
-    depth = {"attn": 2 * dm.d, "fc": dm.d, "out": dm.ff}[kind]
     return k.section(
         functools.partial(grad_body, dm, kind),
         [(a, "v") for pair in lefts + rights for a in pair],
         [sds((dm.nc // 2, dm.nf, dm.pr, dm.pc), BF16)],
-        [pltpu.VMEM((depth, 2 * dm.t), BF16)],
+        [("xt", pltpu.VMEM((dm.ff, 2 * dm.t), BF16))],
         2 * dm.t * dm.d * dm.ff,
     )[0][0]
 
@@ -1308,9 +1329,9 @@
 
     per_layer = (attn_gain, attn_shift, qkv_bias, proj_bias, mlp_gain, mlp_shift, fc_bias, out_bias)
     parts = [p[layer] for layer in range(LAYERS) for p in per_layer] + [final_gain, final_shift]
-    packed = jnp.concatenate(parts).reshape(small_size // 128, 128)
+    packed = jnp.concatenate(parts).reshape(1, small_size).astype(F32)
     small_move = Move(
-        (nf - 1,) + packed.shape, BF16,
+        (nf - 1,) + packed.shape, F32,
         [([(None, packed, None)], ("fsdp", s), (s - 1,)) for s in range(1, nf)],
     )
 
@@ -1324,43 +1345,50 @@
 
     k = flow.kernel()
     k.start([small_move])
-    flow.go(k, "A0", "A0", "C0", "A0", "C0", "O0")
-    flow.finish(k, "A0")
-    k.run()
-    backwards = jnp.concatenate([packed[None], value(small_move)])[::-1]
-    small = lax.dynamic_slice_in_dim(jnp.concatenate([backwards, backwards]), nf - 1 - f, nf)
-    small = small.reshape(nf, small_size).astype(F32)
-
+    flow.go(k, "A0", "A0", "C0")
+    (small,) = k.section(
+        functools.partial(small_body, dm),
+        [(packed, "v"), (small_move, "v")],
+        [sds((nf, small_size), F32)],
+        [],
+        0,
+    )[0]
+    flow.go(k, "A0", "C0", "O0", "A0")
     h = acts[0]
-    kept = []
-    k = flow.kernel("C0", "O0", "A1")
-    n1, blocks = qkv_section(k, 0, h, small, qkv_weight, flow.done["A0"], meta)
-    flow.go(k, "C0")
-    k.run()
-    vectors = {}
+    n1, blocks = qkv_section(k, 0, h, small, qkv_weight, flow.finish(k, "A0"), meta)
+    flow.go(k, "C0", "O0", "A1")
+    twin = [other_core(n1)]
+    k.start(twin)
+    vectors, kept = {}, []
     for layer in range(LAYERS):
         tag, nxt = str(layer), str(layer + 1)
         last = layer + 1 == LAYERS
-        twin = [other_core(n1)]
-        k = flow.kernel("O" + tag, "A" + nxt, "C" + nxt) if not last else flow.kernel("C" + tag, "O" + tag)
-        k.start(twin)
         saved, heads = attend_section(k, blocks, meta)
-        flow.go(k, "C" + tag if last else "O" + tag)
-        k.run()
-        k = flow.kernel("A" + nxt, "O" + nxt, "C" + nxt) if not last else flow.kernel("O" + tag)
+        if last:
+            flow.go(k, "C" + tag, "O" + tag)
+        else:
+            flow.go(k, "C" + tag, "O" + tag, "A" + nxt, "C" + nxt)
+            k.run()
+            k = flow.kernel("O" + tag, "A" + nxt)
         attn = flow.done["A" + tag]
         ob, mid, n2 = proj_section(k, layer, h, small, proj_weight, heads, attn, meta)
+        if last:
+            flow.go(k, "O" + tag)
         twin += [other_core(ob), other_core(n2)]
         k.start(twin[1:])
         u, act = fc_section(k, layer, n2, small, fc_weight, flow.finish(k, "C" + tag), meta)
         twin.append(other_core(act))
         k.start(twin[3:])
+        if not last:
+            flow.go(k, "C" + nxt, "A" + nxt, "O" + nxt)
         nxt_h = out_section(k, layer, mid, act, small, out_weight, flow.finish(k, "O" + tag), meta)
         kept.append((h, n1, saved, ob, mid, n2, u, act, twin))
         h = nxt_h
         if not last:
             n1, blocks = qkv_section(k, layer + 1, h, small, qkv_weight, flow.finish(k, "A" + nxt), meta)
-            k.run()
+            twin = [other_core(n1)]
+            k.start(twin)
+            flow.go(k, "C" + nxt, "O" + nxt)
 
     weights = flow.done
     result, dh, gm, vectors["gf"], vectors["sf"] = top_section(k, h, cotangent[0], small)
@@ -1375,38 +1403,37 @@
         du, vectors["bo" + tag], vectors["bf" + tag] = out_back_section(
             k, layer, gm, u, out_weight, weights["O" + tag], meta
         )
+        du_ = other_core(du)
+        k.start([du_])
         flow.go(k, k_, k_)
         k.run()
-        du_ = other_core(du)
-        k = flow.kernel()
-        k.start([du_])
-        flow.go(k, a_)
+
+        k = flow.kernel(a_)
         flow.add(o, reduce(dm, grad_section(k, "out", [(act, act_)], [(gm, gm_)])))
         flow.go(k, o)
         dmid, ga, vectors["bp" + tag], vectors["g2" + tag], vectors["s2" + tag] = fc_back_section(
             k, layer, du, dh, mid, small, fc_weight, weights["C" + tag], meta
         )
-        k.run()
-        k = flow.kernel(a_, o)
         ga_ = other_core(ga)
         k.start([ga_])
         grads = proj_back_section(k, layer, ga, proj_weight, weights["A" + tag], meta)
+        flow.go(k, a_)
         flow.add(ck, reduce(dm, grad_section(k, "fc", [(n2, n2_)], [(du, du_)])))
-        flow.go(k, ck)
+        flow.go(k, ck, o)
+        if dm.rows * dm.nc > 2048 * 8:
+            k.run()
+            k = flow.kernel()
+        blocks = attend_back_section(k, saved, grads, meta)
+        flow.go(k, o, ck, a_, a_, a_)
         k.run()
-        k = flow.kernel(o, ck, a_)
-        blocks = attend_back_section(k, saved, grads, meta)
-        flow.go(k, a_)
-        k.run()
-        k = flow.kernel(o, ck, a_)
+
+        k = flow.kernel(ck, o)
         dh, gm, dqkv, vectors["bq" + tag], vectors["g1" + tag], vectors["s1" + tag] = qkv_back_section(
             k, layer, dmid, h, small, qkv_weight, blocks, weights["A" + tag], meta
         )
         dqkv_ = other_core(dqkv)
         k.start([dqkv_])
         flow.go(k, o, o)
-        k.run()
-        k = flow.kernel(ck)
         if layer == 0:
             shape = (nf, 1, small_size)
             rows = k.section(
@@ -1422,9 +1449,9 @@
             a,
             reduce(dm, grad_section(k, "attn", [(n1, n1_), (ob, ob_)], [(dqkv, dqkv_), (ga, ga_)])),
         )
-        flow.go(k, a)
-
-    flow.go(k, "c0", "small", "small", "c0", "a0", "small", "small", "a0", "small", "small")
+        flow.go(k, a, ck)
+
+    flow.go(k, "small", "small", "a0", "c0", "small", "small", "a0", "c0", "small", "small")
     for name in ("a1", "c1", "o1", "c0", "o0", "a0"):
         flow.finish(k, name)
     mine = flow.finish(k, "small")

time: 858 us -> 752 us (0.88)
  Pallas kernels: 830 us -> 722 us
    pallas_call x16 -> x6, Pallas kernels: 815 us -> 707 us  [run(): pl.pallas_call(kernel, out_shape=self.outs, in_specs=self.in_specs, out_s...]
where the time goes in v3:
time: 752 us; the launch traced here: 742 us
  Pallas kernels  722 us (96%)
  local copies, waits for them, and re-layouts  15.2 us (2%)
    pallas_call x6, Pallas kernels, run(): pl.pallas_call(kernel, out_shape=self.outs, in_specs=self.in_specs, out_s...  707 us

profile of v3, /device:TPU:0, one launch (start us, length us, event | category | flops | bytes accessed | tf_op | source)
XLA Modules:
  0.0 742.1 jit_solution(4868303651595903119)
XLA Ops:
  0.7 0.8 select_reduce_fusion.1
  1.6 1.4 fusion.1
  4.3 1.2 concatenate.20.refs_6_.refs_3_.refs_4_.refs_9_.refs_7_
  6.9 0.7 constant_dynamic-update-slice_fusion.15
  7.6 0.7 constant_dynamic-update-slice_fusion.14
  9.6 0.7 constant_dynamic-update-slice_fusion.11
  10.3 0.7 constant_dynamic-update-slice_fusion.10
  11.0 0.7 constant_dynamic-update-slice_fusion.9
  11.7 0.7 constant_dynamic-update-slice_fusion.8
  12.4 0.7 constant_dynamic-update-slice_fusion.7
  13.1 0.7 constant_dynamic-update-slice_fusion.6
  13.8 0.7 constant_dynamic-update-slice_fusion.5
  14.5 0.7 constant_dynamic-update-slice_fusion.4
  15.2 0.7 constant_dynamic-update-slice_fusion.3
  15.9 0.7 constant_dynamic-update-slice_fusion.2
  18.5 149.3 %shard_map.297 = (f32[3,1,7168]{2,1,0:T(1,128)}, bf16[3,256,512]{2,1,0:T(8,128)(2,1)}, bf16[3,256,512]{2,1,0:T(8,128)(2,1)}, bf16[3,256,512]{2,1,0:T(8,128)(2,1)...) custom-call(f32[1,7168]{1,0:T(1,128)} %convert_element_type.11.refs_, ...), custom_call_target="tpu_custom_call" | custom-call | flops 5905580032 | bytes 41168976 | tf_op jit(solution)/shard_map/pallas_call | solution.py:304
  167.9 130.5 %shard_map.298 = (bf16[3,256,512]{2,1,0:T(8,128)(2,1)}, bf16[3,256,512]{2,1,0:T(8,128)(2,1)}, bf16[3,256,512]{2,1,0:T(8,128)(2,1)}, bf16[3,256,512]{2,1,0:T(8,12...) custom-call(bf16[3,256,512]{2,1,0:T(8,128)(2,1)} %get-tuple-element., ...), custom_call_target="tpu_custom_call" | custom-call | flops 17721982976 | bytes 89813072 | tf_op jit(solution)/shard_map/pallas_call | solution.py:304
  298.4 112.2 %shard_map.299 = (bf16[4,4,256,512]{3,2,1,0:T(8,128)(2,1)}, bf16[4,128,512]{2,1,0:T(8,128)(2,1)}, bf16[4,128,512]{2,1,0:T(8,128)(2,1)}, bf16[4,128,512]{2,1,0:T(...) custom-call(bf16[256,4096]{1,0:T(8,128)(2,1)} %get-tuple-element.236, ...), custom_call_target="tpu_custom_call" | custom-call | flops 15569256448 | bytes 55980112 | tf_op jit(solution)/shard_map/pallas_call | solution.py:304
  410.6 67.4 %shard_map.300 = (bf16[4,128,512]{2,1,0:T(8,128)(2,1)}, bf16[3,128,512]{2,1,0:T(8,128)(2,1)}, bf16[4,128,512]{2,1,0:T(8,128)(2,1)}, bf16[3,128,512]{2,1,0:T(8,12...) custom-call(bf16[4,4,256,512]{3,2,1,0:T(8,128)(2,1)} %get-tuple-elem, ...), custom_call_target="tpu_custom_call" | custom-call | flops 5905580032 | bytes 61497424 | tf_op jit(solution)/shard_map/pallas_call | solution.py:304
  478.0 133.3 %shard_map.301 = (bf16[4,128,512]{2,1,0:T(8,128)(2,1)}, bf16[4,128,512]{2,1,0:T(8,128)(2,1)}, bf16[4,128,512]{2,1,0:T(8,128)(2,1)}, bf16[4,128,512]{2,1,0:T(8,12...) custom-call(bf16[4,4,256,512]{3,2,1,0:T(8,128)(2,1)} %get-tuple-elem, ...), custom_call_target="tpu_custom_call" | custom-call | flops 15569256448 | bytes 68563024 | tf_op jit(solution)/shard_map/pallas_call | solution.py:304
  611.2 114.5 %shard_map.302 = (bf16[4,128,512]{2,1,0:T(8,128)(2,1)}, bf16[3,128,512]{2,1,0:T(8,128)(2,1)}, bf16[4,128,512]{2,1,0:T(8,128)(2,1)}, bf16[3,128,512]{2,1,0:T(8,12...) custom-call(bf16[4,4,256,512]{3,2,1,0:T(8,128)(2,1)} %get-tuple-elem, ...), custom_call_target="tpu_custom_call" | custom-call | flops 3758096384 | bytes 48857168 | tf_op jit(solution)/shard_map/pallas_call | solution.py:304
  725.8 14.5 %shard_map.303 = (f32[2,256,3072]{2,1,0:T(8,128)}, f32[2,256,1024]{2,1,0:T(8,128)}, f32[2,256,4096]{2,1,0:T(8,128)}, f32[2,1024,1024]{2,1,0:T(8,128)}, f32[2,256...) custom-call(bf16[256,512]{1,0:T(8,128)(2,1)} %get-tuple-element.331., ...), custom_call_target="tpu_custom_call" | custom-call | tf_op jit(solution)/shard_map/pallas_call | solution.py:1060
  740.3 0.8 copy.53
  741.0 0.8 copy.54
  (13 shorter events, 4.8 us)
Async XLA Ops:
  725.7 14.5 %copy-start = (bf16[256,1024]{1,0:T(8,128)(2,1)S(1)}, bf16[256,1024]{1,0:T(8,128)(2,1)}, u32[]{:S(2)}) copy-start(bf16[256,1024]{1,0:T(8,128)(2,1)} %get-tuple-element.235) | copy-start | bytes 1572868
  725.7 15.3 %copy-start.1 = (bf16[256,1024]{1,0:T(8,128)(2,1)S(1)}, bf16[256,1024]{1,0:T(8,128)(2,1)}, u32[]{:S(2)}) copy-start(bf16[256,1024]{1,0:T(8,128)(2,1)} %get-tuple-element.330) | copy-start | bytes 1572868

commit v4 on v3

--- a/solution.py
+++ b/solution.py
@@ -17,7 +17,7 @@
 LOW = -1e29
 F32 = jnp.float32
 BF16 = jnp.bfloat16
-VMEM_BYTES = 60 * 1024 * 1024
+VMEM_BYTES = 61 * 1024 * 1024
 
 FIELDS = ("t", "d", "ff", "nf", "nc", "pr", "pc", "nq", "ncs", "ffn", "w", "hl", "rows", "half")
 Dims = collections.namedtuple("Dims", FIELDS)
@@ -125,8 +125,8 @@
 
 
 class Move:
-    def __init__(self, shape, dtype, parts):
-        self.shape, self.dtype, self.parts = shape, dtype, parts
+    def __init__(self, shape, dtype, parts, base=None):
+        self.shape, self.dtype, self.parts, self.base = shape, dtype, parts, base
         self.result = None
 
 
@@ -165,17 +165,30 @@
     def load(self, move):
         key = ("load", id(move))
         if key not in self.keys:
-            self.keys[key] = Slot("scratch", len(self.scratch), move)
-            self.scratch.append(pltpu.VMEM(move.shape, move.dtype))
-            sem = self.buffer(("load", pltpu.SemaphoreType.DMA))
-
-            def body(src, dst, sem):
-                copy = pltpu.make_async_copy(src, dst, sem)
+            self.load_all([(move, key)])
+        return self.keys[key]
+
+    def load_all(self, wanted):
+        srcs, dsts = [], []
+        for array, key in wanted:
+            key = key if isinstance(key, tuple) else (key, array.shape)
+            if key not in self.keys:
+                self.keys[key] = Slot("scratch", len(self.scratch), array)
+                self.scratch.append(pltpu.VMEM(array.shape, array.dtype))
+            srcs.append(self.operand(array, "a"))
+            dsts.append(self.keys[key])
+        n = len(wanted)
+
+        def body(*refs):
+            copies = [pltpu.make_async_copy(refs[i], refs[n + i], refs[2 * n].at[i]) for i in range(n)]
+            for copy in copies:
                 copy.start()
+            for copy in copies:
                 copy.wait()
 
-            self.steps.append(("body", body, [move, self.keys[key], sem]))
-        return self.keys[key]
+        sems = self.buffer(("load" + str(n), pltpu.SemaphoreType.DMA((n,))))
+        self.steps.append(("body", body, srcs + dsts + [sems]))
+        return dsts
 
     def output(self, out, space):
         slot = Slot("out", len(self.outs), out)
@@ -208,7 +221,10 @@
                 ([(cond, self.operand(src, "a"), index) for cond, src, index in sources], route, place)
                 for sources, route, place in move.parts
             ]
-            slot = self.output(sds(move.shape, move.dtype), pl.ANY)
+            if move.base is None:
+                slot = self.output(sds(move.shape, move.dtype), pl.ANY)
+            else:
+                slot = next(made for m, _, made in self.moves if m is move.base)
             self.moves.append((move, parts, slot))
             self.steps.append(("start", len(self.moves) - 1, None))
 
@@ -281,6 +297,9 @@
                 if kind == "body":
                     for slot in used:
                         ready(slot)
+                        for n, (m, _, _) in enumerate(moves):
+                            if m.base is slot:
+                                wait(n)
                     what(*[ref_of(slot) for slot in used])
                     continue
                 for sources, _, _ in moves[what][1]:
@@ -610,15 +629,14 @@
     return row, doc_start(cuts[0], cuts[1], row)
 
 
-TQ = 256
-TK = 256
+TILE = 512
 
 
 def attend_body(dm, *refs):
     nc, w = dm.nc, dm.w
     meta, blocks, packed, lse, mixed, heads = refs
     cuts = (meta[2], meta[3])
-    tq, tk = min(TQ, dm.rows), min(TK, dm.rows)
+    tq = tk = min(TILE, dm.rows)
     sort_rows(dm, meta, blocks, packed)
 
     def tile(t, carry):
@@ -626,11 +644,12 @@
         q = stack_heads(dm, packed[here, :w], HEAD_DIM**-0.5)
         row, start = tile_rows(dm, t, tq, cuts)
 
-        def chunk(kb, state):
+        def chunk(kb, state, last=False):
             top, mass, acc = state
             there = pl.ds(mult(kb * tk, tk), tk)
             col = kb * tk + lax.broadcasted_iota(jnp.int32, (1, tk), 1)
-            s = jnp.where((col <= row) & (col >= start), nt(q, packed[there, w : 2 * w]), NEG)
+            seen = (col <= row) & (col >= start) if last else col >= start
+            s = jnp.where(seen, nt(q, packed[there, w : 2 * w]), NEG)
             new_top = jnp.maximum(top, jnp.max(s, axis=1, keepdims=True))
             p = jnp.exp(s - new_top)
             fade = jnp.exp(top - new_top)
@@ -643,11 +662,11 @@
             jnp.zeros((dm.hl * tq, 1), F32),
             jnp.zeros((dm.hl * tq, w), F32),
         )
-        top, mass, acc = lax.fori_loop(0, ((t + 1) * tq + tk - 1) // tk, chunk, initial)
+        top, mass, acc = chunk(t, lax.fori_loop(0, t, chunk, initial), True)
         mixed[here, :] = pick_heads(dm, acc * (1.0 / mass))
         norms = top + jnp.log(mass)
         for k in range(dm.hl):
-            lse[k, here, :] = norms[k * tq : (k + 1) * tq]
+            lse[here, k : k + 1] = norms[k * tq : (k + 1) * tq]
         return carry
 
     lax.fori_loop(0, dm.rows // tq, tile, 0)
@@ -660,7 +679,7 @@
     saved, bufs = k.section(
         functools.partial(attend_body, dm),
         [(meta, "s"), (blocks, "v")],
-        [sds((dm.rows, 3 * dm.w), BF16), sds((dm.hl, dm.rows, 1), F32), sds((dm.rows, dm.w), F32)],
+        [sds((dm.rows, 3 * dm.w), BF16), sds((dm.rows, dm.hl), F32), sds((dm.rows, dm.w), F32)],
         [pltpu.VMEM(shape, BF16)],
         8 * dm.rows * dm.rows * dm.w,
     )
@@ -673,7 +692,7 @@
     nc, w = dm.nc, dm.w
     meta, packed, lse, mixed, grads, blocks, dmix, dq, dk, dv = refs
     cuts = (meta[2], meta[3])
-    tq, tk = min(TQ, dm.rows), min(TK, dm.rows)
+    tq = tk = min(TILE, dm.rows)
     scale = HEAD_DIM**-0.5
     sort_rows(dm, meta, grads, dmix)
     dk[...] = jnp.zeros_like(dk)
@@ -685,14 +704,15 @@
         do = stack_heads(dm, dmix[here, :])
         o = jnp.concatenate([mixed[here, :]] * dm.hl, axis=0)
         delta = jnp.sum(do.astype(F32) * o, axis=1, keepdims=True)
-        norms = jnp.concatenate([lse[k, here, :] for k in range(dm.hl)], axis=0)
+        norms = jnp.concatenate([lse[here, k : k + 1] for k in range(dm.hl)], axis=0)
         row, start = tile_rows(dm, t, tq, cuts)
 
-        def chunk(kb, acc):
+        def chunk(kb, acc, last=False):
             there = pl.ds(mult(kb * tk, tk), tk)
             col = kb * tk + lax.broadcasted_iota(jnp.int32, (1, tk), 1)
             keys = packed[there, w : 2 * w]
-            s = jnp.where((col <= row) & (col >= start), nt(q, keys), NEG)
+            seen = (col <= row) & (col >= start) if last else col >= start
+            s = jnp.where(seen, nt(q, keys), NEG)
             p = jnp.exp(s - norms)
             dp = nt(do, packed[there, 2 * w :])
             ds = (p * (dp - delta)).astype(BF16)
@@ -700,10 +720,8 @@
             dk[there, :] += tn(ds, q)
             return acc + nn(ds, keys)
 
-        acc = lax.fori_loop(
-            0, ((t + 1) * tq + tk - 1) // tk, chunk, jnp.zeros((dm.hl * tq, w), F32)
-        )
-        dq[here, :] = pick_heads(dm, acc) * scale
+        acc = chunk(t, lax.fori_loop(0, t, chunk, jnp.zeros((dm.hl * tq, w), F32)), True)
+        dq[here, :] = (pick_heads(dm, acc) * scale).astype(BF16)
         return carry
 
     lax.fori_loop(0, dm.rows // tq, tile, 0)
@@ -718,8 +736,9 @@
         functools.partial(attend_back_body, dm),
         [(meta, "s")] + [(a, "v") for a in saved] + [(grads, "v")],
         [],
-        [pltpu.VMEM(shape, BF16), pltpu.VMEM((dm.rows, dm.w), BF16)]
-        + [pltpu.VMEM((dm.rows, dm.w), F32)] * 3,
+        [pltpu.VMEM(shape, BF16)]
+        + [pltpu.VMEM((dm.rows, dm.w), BF16)] * 2
+        + [pltpu.VMEM((dm.rows, dm.w), F32)] * 2,
         16 * dm.rows * dm.rows * dm.w,
     )
     blocks = send_blocks(dm, bufs[0], shape)
@@ -938,6 +957,15 @@
     )[0][0]
 
 
+def pack_body(dm, *refs):
+    for n, name in enumerate(vector_names()):
+        at, size = small_offsets(dm)[0][name]
+        layer, which = n // len(SMALL), n % len(SMALL)
+        if layer == LAYERS:
+            layer, which = 0, len(SMALL) + which
+        refs[-1][:, at : at + size] = refs[which][layer : layer + 1, :].astype(F32)
+
+
 def small_body(dm, packed, others, out):
     f = lax.axis_index("fsdp")
     out[pl.ds(f, 1), :] = packed[...]
@@ -961,7 +989,10 @@
     for n, pair in enumerate(lefts):
         depth = pair[0].shape[1]
         for half, ref in enumerate(pair):
-            xt[n * depth : (n + 1) * depth, half * dm.t : (half + 1) * dm.t] = ref[...].T
+            for at in range(0, depth, dm.pc):
+                xt[n * depth + at : n * depth + at + dm.pc, half * dm.t : (half + 1) * dm.t] = ref[
+                    :, at : at + dm.pc
+                ].T
     rights = pairs[len(pairs) // 2 :]
 
     def fill(t, row_base, row_step, pair, col):
@@ -984,6 +1015,14 @@
 
 def grad_section(k, kind, lefts, rights):
     dm = k.dm
+    if kind != "attn":
+        pairs = [lefts[0], rights[0]]
+        if kind == "out":
+            made = k.load_all([(value(v), name) for pair in pairs for v, name in zip(pair, ("own", "twin"))])
+            lefts, rights = [made[:2]], [made[2:]]
+        else:
+            made = k.load_all([(value(pair[1]), "twin") for pair in pairs])
+            lefts, rights = [(pairs[0][0], made[0])], [(pairs[1][0], made[1])]
     return k.section(
         functools.partial(grad_body, dm, kind),
         [(a, "v") for pair in lefts + rights for a in pair],
@@ -1123,15 +1162,57 @@
     return (yield from spread(dm, others))
 
 
-def plane_sum(dm, terms):
+def shift_order(dm):
+    return sorted(range(1, dm.nf), key=lambda s: min(s, dm.nf - s))
+
+
+def gather_split(dm, source):
+    bits = plane_bits(dm.nc)
+    if len(bits) != 2:
+        return (yield from gather(dm, source))
+    order = shift_order(dm)
+    one, two = bits
+
+    def line(parts):
+        made = {}
+        for s in order:
+            base = made[order[0]] if made else None
+            made[s] = Move((dm.nf - 1, dm.pr, dm.pc), BF16, parts(s), base)
+        return made
+
+    def along(prev, route):
+        return line(lambda s: [([(None, prev[s], (s - 1,))], route, (s - 1,))])
+
+    z = line(lambda s: [(source, ("fsdp", s), (s - 1,))])
+    yield moving([z[s] for s in order])
+    x, y, core = along(z, ("ctx", one)), along(z, ("ctx", two)), along(z, ("ctx", 1))
+    for s in order:
+        yield moving([x[s], y[s], core[s]])
+    cut = dm.pr // 2
+
+    def corner(s):
+        low, high = (s - 1, pl.ds(0, cut)), (s - 1, pl.ds(cut, cut))
+        return [([(None, y[s], low)], ("ctx", one), low), ([(None, x[s], high)], ("ctx", two), high)]
+
+    far = line(corner)
+    x_, y_ = along(x, ("ctx", 1)), along(y, ("ctx", 1))
+    for s in order:
+        yield moving([far[s], x_[s], y_[s]])
+    far_ = along(far, ("ctx", 1))
+    yield moving([far_[s] for s in order])
+    held = {0: z, 1: core, one: x, one ^ 1: x_, two: y, two ^ 1: y_, one ^ two: far, one ^ two ^ 1: far_}
+    return [held[j][order[0]] for j in range(dm.nc)]
+
+
+def plane_sum(dm, terms, first_shard, shards):
     bits = plane_bits(dm.nc)
     if len(bits) == 2:
         one, two = bits
         cut = dm.pr // 2
-        shape = (dm.nf, cut, dm.pc)
+        shape = (shards, cut, dm.pc)
 
         def part(t, first):
-            return (t, slice(None), pl.ds(first, cut))
+            return (t, pl.ds(first_shard, shards), pl.ds(first, cut))
 
         def send(t, first, bit):
             return Move(shape, BF16, [([(None, terms, part(t, first))], ("ctx", bit), None)])
@@ -1172,45 +1253,79 @@
     return [[(at, (0,)), (away, (0,))]]
 
 
-def reduce(dm, terms):
-    parts = yield from plane_sum(dm, terms)
-    rows = dm.pr // len(parts)
-    totals = []
-    others = []
-
-    def along(k):
-        for n, part in enumerate(parts):
-            totals.append(sum_section(k, part, (dm.nf, rows, dm.pc)))
-            others.append(
-                Move(
-                    (dm.nf - 1, rows, dm.pc), BF16,
-                    [
-                        ([(None, totals[n], (s,))], ("fsdp", dm.nf - s), (s - 1,))
-                        for s in range(1, dm.nf)
-                    ],
-                )
-            )
-            k.start(others[n:])
-
-    yield along
+def reduce(dm, terms, split=False):
+    split = split and len(plane_bits(dm.nc)) == 2
+    groups = [(s, 1) for s in shift_order(dm) + [0]] if split else [(0, dm.nf)]
+    sums = [plane_sum(dm, terms, *group) for group in groups]
+    parts = [None] * len(groups)
+
+    def stage(n):
+        try:
+            return next(sums[n])
+        except StopIteration as stop:
+            parts[n] = stop.value
+            return None
+
+    own, others = {}, []
+
+    def along(n):
+        first, count = groups[n]
+
+        def put(k):
+            rows = dm.pr // len(parts[n])
+            for at, part in enumerate(parts[n]):
+                total = sum_section(k, part, (count, rows, dm.pc))
+                sent = [s for s in range(first, first + count) if s > 0]
+                if first == 0:
+                    own[at] = total
+                if sent:
+                    move = Move(
+                        (len(sent), rows, dm.pc), BF16,
+                        [
+                            ([(None, total, (s - first,))], ("fsdp", dm.nf - s), (m,))
+                            for m, s in enumerate(sent)
+                        ],
+                    )
+                    others.append((at, move, len(sent)))
+                    k.start([move])
+
+        return put
+
+    for n in range(len(groups)):
+        yield stage(n)
+    if split:
+        for n in range(len(groups) + 1):
+            if n < len(groups):
+                yield stage(n)
+            if n > 0:
+                stage(n - 1)
+                yield along(n - 1)
+    else:
+        more = stage(0)
+        while more is not None:
+            yield more
+            more = stage(0)
+        yield along(0)
     mine = []
 
     def join(k):
+        rows = dm.pr // len(own)
+
         def body(*refs):
-            out = refs[-1]
-            for n in range(len(parts)):
-                out[n * rows : (n + 1) * rows, :] = refs[n][...]
+            for n in range(len(own)):
+                refs[-1][n * rows : (n + 1) * rows, :] = refs[n][...]
 
         sums = [
             sum_section(
-                k, [(totals[n], (0,))] + [(others[n], (s,)) for s in range(dm.nf - 1)], (rows, dm.pc)
+                k,
+                [(own[at], (0,))] + [(m, (i,)) for to, m, size in others if to == at for i in range(size)],
+                (rows, dm.pc),
             )
-            for n in range(len(parts))
+            for at in range(len(own))
         ]
         mine.append(k.section(body, [(v, "v") for v in sums], [sds((dm.pr, dm.pc), BF16)], [], 0)[0][0])
 
-    stages = spread_later(dm, mine, join)
-    return (yield from stages)
+    return (yield from spread_later(dm, mine, join))
 
 
 def spread_later(dm, mine, join):
@@ -1327,25 +1442,31 @@
             return [(None, fc_weight, lambda: cols(0, nc))]
         return [(None, out_weight, place)]
 
-    per_layer = (attn_gain, attn_shift, qkv_bias, proj_bias, mlp_gain, mlp_shift, fc_bias, out_bias)
-    parts = [p[layer] for layer in range(LAYERS) for p in per_layer] + [final_gain, final_shift]
-    packed = jnp.concatenate(parts).reshape(1, small_size).astype(F32)
-    small_move = Move(
-        (nf - 1,) + packed.shape, F32,
-        [([(None, packed, None)], ("fsdp", s), (s - 1,)) for s in range(1, nf)],
-    )
-
     def other_core(v):
         return whole(v, ("ctx", 1))
 
     flow = Flow(dm)
     for layer in range(LAYERS):
         for kind, name in (("attn", "A"), ("fc", "C"), ("out", "O")):
-            flow.add(name + str(layer), gather(dm, source(kind, layer)))
+            how = gather_split if layer == 0 and name == "A" else gather
+            flow.add(name + str(layer), how(dm, source(kind, layer)))
 
     k = flow.kernel()
+    flow.go(k, "A0")
+    per_layer = (attn_gain, attn_shift, qkv_bias, proj_bias, mlp_gain, mlp_shift, fc_bias, out_bias)
+    _, (packed,) = k.section(
+        functools.partial(pack_body, dm),
+        [(v, "v") for v in per_layer] + [(v.reshape(1, -1), "v") for v in (final_gain, final_shift)],
+        [],
+        [pltpu.VMEM((1, small_size), F32)],
+        0,
+    )
+    small_move = Move(
+        (nf - 1, 1, small_size), F32,
+        [([(None, packed, None)], ("fsdp", s), (s - 1,)) for s in range(1, nf)],
+    )
     k.start([small_move])
-    flow.go(k, "A0", "A0", "C0")
+    flow.go(k, "A0", "A0", "A0", "C0", "A0", "A0", "A0")
     (small,) = k.section(
         functools.partial(small_body, dm),
         [(packed, "v"), (small_move, "v")],
@@ -1353,12 +1474,15 @@
         [],
         0,
     )[0]
-    flow.go(k, "A0", "C0", "O0", "A0")
     h = acts[0]
-    n1, blocks = qkv_section(k, 0, h, small, qkv_weight, flow.finish(k, "A0"), meta)
-    flow.go(k, "C0", "O0", "A1")
+    first = flow.finish(k, "A0")
+    flow.go(k, "O0")
+    n1, blocks = qkv_section(k, 0, h, small, qkv_weight, first, meta)
+    flow.go(k, "A1")
     twin = [other_core(n1)]
     k.start(twin)
+    k.load(blocks)
+    flow.go(k, "C0", "O0")
     vectors, kept = {}, []
     for layer in range(LAYERS):
         tag, nxt = str(layer), str(layer + 1)
@@ -1367,9 +1491,9 @@
         if last:
             flow.go(k, "C" + tag, "O" + tag)
         else:
-            flow.go(k, "C" + tag, "O" + tag, "A" + nxt, "C" + nxt)
+            flow.go(k, "C" + tag, "O" + tag, "C" + tag)
             k.run()
-            k = flow.kernel("O" + tag, "A" + nxt)
+            k = flow.kernel("A" + nxt, "O" + tag, "C" + nxt)
         attn = flow.done["A" + tag]
         ob, mid, n2 = proj_section(k, layer, h, small, proj_weight, heads, attn, meta)
         if last:
@@ -1380,7 +1504,7 @@
         twin.append(other_core(act))
         k.start(twin[3:])
         if not last:
-            flow.go(k, "C" + nxt, "A" + nxt, "O" + nxt)
+            flow.go(k, "A" + nxt, "O" + nxt, "C" + nxt)
         nxt_h = out_section(k, layer, mid, act, small, out_weight, flow.finish(k, "O" + tag), meta)
         kept.append((h, n1, saved, ob, mid, n2, u, act, twin))
         h = nxt_h
@@ -1405,10 +1529,10 @@
         )
         du_ = other_core(du)
         k.start([du_])
-        flow.go(k, k_, k_)
+        flow.go(k, o_)
         k.run()
 
-        k = flow.kernel(a_)
+        k = flow.kernel(a_, k_, o_)
         flow.add(o, reduce(dm, grad_section(k, "out", [(act, act_)], [(gm, gm_)])))
         flow.go(k, o)
         dmid, ga, vectors["bp" + tag], vectors["g2" + tag], vectors["s2" + tag] = fc_back_section(
@@ -1417,14 +1541,14 @@
         ga_ = other_core(ga)
         k.start([ga_])
         grads = proj_back_section(k, layer, ga, proj_weight, weights["A" + tag], meta)
-        flow.go(k, a_)
+        flow.go(k, a_, k_, o_)
         flow.add(ck, reduce(dm, grad_section(k, "fc", [(n2, n2_)], [(du, du_)])))
         flow.go(k, ck, o)
         if dm.rows * dm.nc > 2048 * 8:
             k.run()
             k = flow.kernel()
         blocks = attend_back_section(k, saved, grads, meta)
-        flow.go(k, o, ck, a_, a_, a_)
+        flow.go(k, a_, a_, a_, k_)
         k.run()
 
         k = flow.kernel(ck, o)
@@ -1433,7 +1557,7 @@
         )
         dqkv_ = other_core(dqkv)
         k.start([dqkv_])
-        flow.go(k, o, o)
+        flow.go(k, ck)
         if layer == 0:
             shape = (nf, 1, small_size)
             rows = k.section(
@@ -1447,11 +1571,14 @@
             flow.go(k, "small")
         flow.add(
             a,
-            reduce(dm, grad_section(k, "attn", [(n1, n1_), (ob, ob_)], [(dqkv, dqkv_), (ga, ga_)])),
+            reduce(
+                dm, grad_section(k, "attn", [(n1, n1_), (ob, ob_)], [(dqkv, dqkv_), (ga, ga_)]), layer == 0
+            ),
         )
-        flow.go(k, a, ck)
-
-    flow.go(k, "small", "small", "a0", "c0", "small", "small", "a0", "c0", "small", "small")
+        flow.go(k, a, *([a] * 3 if layer == 0 else []))
+
+    flow.go(k, "o0", "a0", "small", "small", "a0", "o0", "a0", "c0", "small", "small", "a0", "o0", "a0", "c0")
+    flow.go(k, "small", "a0", "a0", "c0", "a0", "small", "small")
     for name in ("a1", "c1", "o1", "c0", "o0", "a0"):
         flow.finish(k, name)
     mine = flow.finish(k, "small")

time: 752 us -> 728 us (0.968)
  Pallas kernels: 722 us -> 710 us
  local copies, waits for them, and re-layouts: 15.2 us -> 5.28 us
    pallas_call x6, Pallas kernels: 707 us -> 695 us  [run(): pl.pallas_call(kernel, out_shape=self.outs, in_specs=self.in_specs, out_s...]
    unnamed x23 -> x6, local copies, waits for them, and re-layouts: 13.3 us -> 1.6 us
where the time goes in v4:
time: 728 us; the launch traced here: 720 us
  Pallas kernels  710 us (98%)
    pallas_call x6, Pallas kernels, run(): pl.pallas_call(kernel, out_shape=self.outs, in_specs=self.in_specs, out_s...  695 us

profile of v4, /device:TPU:0, one launch (start us, length us, event | category | flops | bytes accessed | tf_op | source)
XLA Modules:
  0.0 719.8 jit_solution(7892571879018543004)
XLA Ops:
  0.7 0.8 select_reduce_fusion.1
  1.5 0.1 select_reduce_fusion
  1.6 1.2 reshape.56.refs_10_
  2.8 1.2 reshape.57.refs_11_
  4.1 1.4 fusion.1
  6.7 1.2 concatenate.3.refs_14_.refs_3_.refs_4_.refs_8_.refs_13_
  8.0 135.7 %shard_map.297 = (bf16[3,256,512]{2,1,0:T(8,128)(2,1)}, f32[3,1,7168]{2,1,0:T(1,128)}, bf16[3,256,512]{2,1,0:T(8,128)(2,1)}, bf16[3,256,512]{2,1,0:T(8,128)(2,1)...) custom-call(bf16[2,256,3072]{2,1,0:T(8,128)(2,1)} %refs_12_.5, ...), custom_call_target="tpu_custom_call" | custom-call | flops 5905580032 | bytes 37980240 | tf_op jit(solution)/shard_map/pallas_call | solution.py:323
  143.7 143.1 %shard_map.298 = (bf16[3,256,512]{2,1,0:T(8,128)(2,1)}, bf16[3,256,512]{2,1,0:T(8,128)(2,1)}, bf16[3,256,512]{2,1,0:T(8,128)(2,1)}, bf16[3,256,512]{2,1,0:T(8,12...) custom-call(bf16[3,256,512]{2,1,0:T(8,128)(2,1)} %get-tuple-element., ...), custom_call_target="tpu_custom_call" | custom-call | flops 17721982976 | bytes 89813072 | tf_op jit(solution)/shard_map/pallas_call | solution.py:323
  286.8 97.7 %shard_map.299 = (bf16[4,4,256,512]{3,2,1,0:T(8,128)(2,1)}, bf16[4,128,512]{2,1,0:T(8,128)(2,1)}, bf16[4,128,512]{2,1,0:T(8,128)(2,1)}, bf16[4,128,512]{2,1,0:T(...) custom-call(bf16[256,4096]{1,0:T(8,128)(2,1)} %get-tuple-element.238, ...), custom_call_target="tpu_custom_call" | custom-call | flops 15569256448 | bytes 52047952 | tf_op jit(solution)/shard_map/pallas_call | solution.py:323
  384.5 72.4 %shard_map.300 = (bf16[4,128,512]{2,1,0:T(8,128)(2,1)}, bf16[4,128,512]{2,1,0:T(8,128)(2,1)}, bf16[4,128,512]{2,1,0:T(8,128)(2,1)}, bf16[4,128,512]{2,1,0:T(8,12...) custom-call(bf16[4,4,256,512]{3,2,1,0:T(8,128)(2,1)} %get-tuple-elem, ...), custom_call_target="tpu_custom_call" | custom-call | flops 5905580032 | bytes 66478160 | tf_op jit(solution)/shard_map/pallas_call | solution.py:323
  456.9 129.1 %shard_map.301 = (bf16[4,128,512]{2,1,0:T(8,128)(2,1)}, bf16[4,128,512]{2,1,0:T(8,128)(2,1)}, bf16[4,128,512]{2,1,0:T(8,128)(2,1)}, bf16[4,128,512]{2,1,0:T(8,12...) custom-call(bf16[4,4,256,512]{3,2,1,0:T(8,128)(2,1)} %get-tuple-elem, ...), custom_call_target="tpu_custom_call" | custom-call | flops 15569256448 | bytes 70398032 | tf_op jit(solution)/shard_map/pallas_call | solution.py:323
  586.0 117.4 %shard_map.302 = (bf16[4,128,512]{2,1,0:T(8,128)(2,1)}, bf16[4,128,512]{2,1,0:T(8,128)(2,1)}, bf16[4,128,512]{2,1,0:T(8,128)(2,1)}, bf16[4,128,512]{2,1,0:T(8,12...) custom-call(bf16[4,4,256,512]{3,2,1,0:T(8,128)(2,1)} %get-tuple-elem, ...), custom_call_target="tpu_custom_call" | custom-call | flops 3758096384 | bytes 57245776 | tf_op jit(solution)/shard_map/pallas_call | solution.py:323
  703.4 0.0 copy-start
  703.4 0.0 copy-start.1
  703.4 14.5 %shard_map.303 = (f32[2,256,3072]{2,1,0:T(8,128)}, f32[2,256,1024]{2,1,0:T(8,128)}, f32[2,256,4096]{2,1,0:T(8,128)}, f32[2,1024,1024]{2,1,0:T(8,128)}, f32[2,256...) custom-call(bf16[256,512]{1,0:T(8,128)(2,1)} %get-tuple-element.345., ...), custom_call_target="tpu_custom_call" | custom-call | tf_op jit(solution)/shard_map/pallas_call | solution.py:1099
  717.9 0.0 copy-done
  717.9 0.8 copy.36
  718.7 0.0 copy-done.1
  718.7 0.8 copy.37
  (1 shorter events, 0.0 us)
Async XLA Ops:
  703.4 14.5 %copy-start = (bf16[256,1024]{1,0:T(8,128)(2,1)S(1)}, bf16[256,1024]{1,0:T(8,128)(2,1)}, u32[]{:S(2)}) copy-start(bf16[256,1024]{1,0:T(8,128)(2,1)} %get-tuple-element.237) | copy-start | bytes 1572868
  703.4 15.3 %copy-start.1 = (bf16[256,1024]{1,0:T(8,128)(2,1)S(1)}, bf16[256,1024]{1,0:T(8,128)(2,1)}, u32[]{:S(2)}) copy-start(bf16[256,1024]{1,0:T(8,128)(2,1)} %get-tuple-element.344) | copy-start | bytes 1572868

commit v5 on v4

--- a/solution.py
+++ b/solution.py
@@ -981,12 +981,12 @@
             refs[-1][g, :, at : at + size] = ref[:, g * size : (g + 1) * size]
 
 
-def grad_body(dm, kind, *refs):
+def grad_body(dm, kind, shards, more, *refs):
     c, f = lax.axis_index("ctx"), lax.axis_index("fsdp")
     out, xt = refs[-2:]
     pairs = [refs[n : n + 2] for n in range(0, len(refs) - 2, 2)]
     lefts = pairs[: len(pairs) // 2]
-    for n, pair in enumerate(lefts):
+    for n, pair in enumerate([] if more else lefts):
         depth = pair[0].shape[1]
         for half, ref in enumerate(pair):
             for at in range(0, depth, dm.pc):
@@ -998,7 +998,7 @@
     def fill(t, row_base, row_step, pair, col):
         cols = pl.ds(mult(col * dm.pc, dm.pc), dm.pc)
         dy = jnp.concatenate([pair[0][:, cols], pair[1][:, cols]], axis=0)
-        for s in range(dm.nf):
+        for s in shards:
             at = mult(row_base + ring(dm, f, s) * row_step, dm.pr)
             out[t, s] = nn(xt[pl.ds(at, dm.pr), :], dy).astype(BF16)
 
@@ -1013,7 +1013,7 @@
             fill(t, (i // dm.ncs) * dm.pr, dm.ffn, rights[0], lax.rem(i, dm.ncs))
 
 
-def grad_section(k, kind, lefts, rights):
+def grad_section(k, kind, lefts, rights, shards=None, out=None):
     dm = k.dm
     if kind != "attn":
         pairs = [lefts[0], rights[0]]
@@ -1023,13 +1023,14 @@
         else:
             made = k.load_all([(value(pair[1]), "twin") for pair in pairs])
             lefts, rights = [(pairs[0][0], made[0])], [(pairs[1][0], made[1])]
-    return k.section(
-        functools.partial(grad_body, dm, kind),
-        [(a, "v") for pair in lefts + rights for a in pair],
-        [sds((dm.nc // 2, dm.nf, dm.pr, dm.pc), BF16)],
+    made = k.section(
+        functools.partial(grad_body, dm, kind, shards or range(dm.nf), out is not None),
+        [(a, "v") for pair in lefts + rights for a in pair] + ([(out, "v")] if out is not None else []),
+        [] if out is not None else [sds((dm.nc // 2, dm.nf, dm.pr, dm.pc), BF16)],
         [("xt", pltpu.VMEM((dm.ff, 2 * dm.t), BF16))],
         2 * dm.t * dm.d * dm.ff,
-    )[0][0]
+    )[0]
+    return out if out is not None else made[0]
 
 
 def place_body(dm, *refs):
@@ -1504,11 +1505,12 @@
         twin.append(other_core(act))
         k.start(twin[3:])
         if not last:
-            flow.go(k, "A" + nxt, "O" + nxt, "C" + nxt)
+            flow.go(k, "A" + nxt, "O" + nxt)
         nxt_h = out_section(k, layer, mid, act, small, out_weight, flow.finish(k, "O" + tag), meta)
         kept.append((h, n1, saved, ob, mid, n2, u, act, twin))
         h = nxt_h
         if not last:
+            flow.go(k, "C" + nxt)
             n1, blocks = qkv_section(k, layer + 1, h, small, qkv_weight, flow.finish(k, "A" + nxt), meta)
             twin = [other_core(n1)]
             k.start(twin)
@@ -1532,9 +1534,9 @@
         flow.go(k, o_)
         k.run()
 
-        k = flow.kernel(a_, k_, o_)
+        k = flow.kernel(a_)
         flow.add(o, reduce(dm, grad_section(k, "out", [(act, act_)], [(gm, gm_)])))
-        flow.go(k, o)
+        flow.go(k, o, k_, o_)
         dmid, ga, vectors["bp" + tag], vectors["g2" + tag], vectors["s2" + tag] = fc_back_section(
             k, layer, du, dh, mid, small, fc_weight, weights["C" + tag], meta
         )
@@ -1548,16 +1550,16 @@
             k.run()
             k = flow.kernel()
         blocks = attend_back_section(k, saved, grads, meta)
-        flow.go(k, a_, a_, a_, k_)
+        flow.go(k, a_, k_)
         k.run()
 
-        k = flow.kernel(ck, o)
+        k = flow.kernel(a_)
         dh, gm, dqkv, vectors["bq" + tag], vectors["g1" + tag], vectors["s1" + tag] = qkv_back_section(
             k, layer, dmid, h, small, qkv_weight, blocks, weights["A" + tag], meta
         )
         dqkv_ = other_core(dqkv)
         k.start([dqkv_])
-        flow.go(k, ck)
+        flow.go(k, a_, k_, ck, o)
         if layer == 0:
             shape = (nf, 1, small_size)
             rows = k.section(
@@ -1569,13 +1571,19 @@
             )[0][0]
             flow.add("small", reduce_small(dm, rows))
             flow.go(k, "small")
-        flow.add(
-            a,
-            reduce(
-                dm, grad_section(k, "attn", [(n1, n1_), (ob, ob_)], [(dqkv, dqkv_), (ga, ga_)]), layer == 0
-            ),
-        )
-        flow.go(k, a, *([a] * 3 if layer == 0 else []))
+        pairs = [(n1, n1_), (ob, ob_)], [(dqkv, dqkv_), (ga, ga_)]
+        if layer == 0 and len(plane_bits(nc)) == 2:
+            order = shift_order(dm) + [0]
+            terms = grad_section(k, "attn", *pairs, order[:1])
+            flow.add(a, reduce(dm, terms, True))
+            flow.go(k, a)
+            for s in order[1:]:
+                grad_section(k, "attn", *pairs, [s], terms)
+                flow.go(k, a)
+            flow.go(k, ck)
+        else:
+            flow.add(a, reduce(dm, grad_section(k, "attn", *pairs)))
+            flow.go(k, a)
 
     flow.go(k, "o0", "a0", "small", "small", "a0", "o0", "a0", "c0", "small", "small", "a0", "o0", "a0", "c0")
     flow.go(k, "small", "a0", "a0", "c0", "a0", "small", "small")

time: 728 us -> 715 us (0.982)
  Pallas kernels: 710 us -> 697 us
    pallas_call x6, Pallas kernels: 695 us -> 683 us  [run(): pl.pallas_call(kernel, out_shape=self.outs, in_specs=self.in_specs, out_s...]
where the time goes in v5:
time: 715 us; the launch traced here: 707 us
  Pallas kernels  697 us (97%)
    pallas_call x6, Pallas kernels, run(): pl.pallas_call(kernel, out_shape=self.outs, in_specs=self.in_specs, out_s...  683 us
    pallas_call x1, Pallas kernels, place_call(): pl.pallas_call(functools.partial(place_body, dm), out_shape=[sds((LAYERS,...  14.5 us

profile of v5, /device:TPU:0, one launch (start us, length us, event | category | flops | bytes accessed | tf_op | source)
XLA Modules:
  0.0 707.3 jit_solution(16297050484736539520)
XLA Ops:
  0.7 0.8 select_reduce_fusion.1
  1.5 0.1 select_reduce_fusion
  1.6 1.2 reshape.56.refs_10_
  2.8 1.2 reshape.57.refs_11_
  4.1 1.4 fusion.1
  6.7 1.2 concatenate.3.refs_14_.refs_3_.refs_4_.refs_0_.refs_2_
  8.0 135.7 %shard_map.297 = (bf16[3,256,512]{2,1,0:T(8,128)(2,1)}, f32[3,1,7168]{2,1,0:T(1,128)}, bf16[3,256,512]{2,1,0:T(8,128)(2,1)}, bf16[3,256,512]{2,1,0:T(8,128)(2,1)...) custom-call(bf16[2,256,3072]{2,1,0:T(8,128)(2,1)} %refs_6_.5, ...), custom_call_target="tpu_custom_call" | custom-call | flops 5905580032 | bytes 37980240 | tf_op jit(solution)/shard_map/pallas_call | solution.py:323
  143.7 143.1 %shard_map.298 = (bf16[3,256,512]{2,1,0:T(8,128)(2,1)}, bf16[3,256,512]{2,1,0:T(8,128)(2,1)}, bf16[3,256,512]{2,1,0:T(8,128)(2,1)}, bf16[3,256,512]{2,1,0:T(8,12...) custom-call(bf16[3,256,512]{2,1,0:T(8,128)(2,1)} %get-tuple-element., ...), custom_call_target="tpu_custom_call" | custom-call | flops 17721982976 | bytes 89813072 | tf_op jit(solution)/shard_map/pallas_call | solution.py:323
  286.8 97.8 %shard_map.299 = (bf16[4,4,256,512]{3,2,1,0:T(8,128)(2,1)}, bf16[4,128,512]{2,1,0:T(8,128)(2,1)}, bf16[4,128,512]{2,1,0:T(8,128)(2,1)}, bf16[4,128,512]{2,1,0:T(...) custom-call(bf16[256,4096]{1,0:T(8,128)(2,1)} %get-tuple-element.236, ...), custom_call_target="tpu_custom_call" | custom-call | flops 15569256448 | bytes 52047952 | tf_op jit(solution)/shard_map/pallas_call | solution.py:323
  384.6 68.1 %shard_map.300 = (f32[256,1024]{1,0:T(8,128)}, bf16[256,1024]{1,0:T(8,128)(2,1)}, bf16[256,3072]{1,0:T(8,128)(2,1)}, f32[1,3072]{1,0:T(1,128)}, f32[1,1024]{1,0:...) custom-call(s32[20]{0:T(128)} %concatenate.3.refs_14_.refs_3_.refs_4, ...), custom_call_target="tpu_custom_call" | custom-call | flops 5905580032 | bytes 63594576 | tf_op jit(solution)/shard_map/pallas_call | solution.py:323
  452.7 123.1 %shard_map.301 = (bf16[4,128,512]{2,1,0:T(8,128)(2,1)}, bf16[4,128,512]{2,1,0:T(8,128)(2,1)}, bf16[4,128,512]{2,1,0:T(8,128)(2,1)}, bf16[4,128,512]{2,1,0:T(8,12...) custom-call(bf16[4,4,256,512]{3,2,1,0:T(8,128)(2,1)} %get-tuple-elem, ...), custom_call_target="tpu_custom_call" | custom-call | flops 15569256448 | bytes 75378768 | tf_op jit(solution)/shard_map/pallas_call | solution.py:323
  575.8 115.2 %shard_map.302 = (bf16[256,512]{1,0:T(8,128)(2,1)}, bf16[256,512]{1,0:T(8,128)(2,1)}, bf16[256,512]{1,0:T(8,128)(2,1)}, f32[256,1024]{1,0:T(8,128)}, bf16[256,10...) custom-call(bf16[256,512]{1,0:T(8,128)(2,1)} %get-tuple-element.307., ...), custom_call_target="tpu_custom_call" | custom-call | flops 10200547328 | bytes 59342928 | tf_op jit(solution)/shard_map/pallas_call | solution.py:323
  691.0 0.0 copy-start
  691.0 0.0 copy-start.1
  691.0 14.5 %shard_map.303 = (f32[2,256,3072]{2,1,0:T(8,128)}, f32[2,256,1024]{2,1,0:T(8,128)}, f32[2,256,4096]{2,1,0:T(8,128)}, f32[2,1024,1024]{2,1,0:T(8,128)}, f32[2,256...) custom-call(bf16[256,512]{1,0:T(8,128)(2,1)} %get-tuple-element.344., ...), custom_call_target="tpu_custom_call" | custom-call | tf_op jit(solution)/shard_map/pallas_call | solution.py:1100
  705.5 0.0 copy-done
  705.5 0.8 copy.36
  706.3 0.0 copy-done.1
  706.3 0.8 copy.37
  (1 shorter events, 0.0 us)
Async XLA Ops:
  691.0 14.5 %copy-start = (bf16[256,1024]{1,0:T(8,128)(2,1)S(1)}, bf16[256,1024]{1,0:T(8,128)(2,1)}, u32[]{:S(2)}) copy-start(bf16[256,1024]{1,0:T(8,128)(2,1)} %get-tuple-element.235) | copy-start | bytes 1572868
  691.0 15.3 %copy-start.1 = (bf16[256,1024]{1,0:T(8,128)(2,1)S(1)}, bf16[256,1024]{1,0:T(8,128)(2,1)}, u32[]{:S(2)}) copy-start(bf16[256,1024]{1,0:T(8,128)(2,1)} %get-tuple-element.343) | copy-start | bytes 1572868
